TPU v7x, 256 devices: a whole 4x4x8 slice. The times are simulated.
256 devices in a mesh: dp: 2 (over x_hi), ctx: 32 (over y, z), mp: 4 (over x_lo, core).
Axes of the slice: x: 4 (x_hi: 2, x_lo: 2; x = x_hi * 2 + x_lo), y: 4, z: 8, core: 2. Of those that a mesh axis runs over, the one named last changes fastest.
Arguments:
- queries: bfloat16 [16384, 2560], P(('dp', 'ctx'), 'mp'), parts along dimension 0, may hold values from -6 to 6
- keys: bfloat16 [16384, 512], P(('dp', 'ctx'), 'mp'), parts along dimension 0, may hold values from -6 to 6
- values: bfloat16 [16384, 512], P(('dp', 'ctx'), 'mp'), parts along dimension 0, may hold values from -6 to 6
- out_weight: bfloat16 [2560, 5120], P('mp'), may hold values from -0.125 to 0.125
- block_order: int32 [128], P('dp'), parts along dimension 0, may hold values from 0 to 63, each once
- doc_lengths: int32 [16], P('dp'), parts along dimension 0, may hold values from 1 to 2048, 8192 in all
- reveal_step: int32 [128, 64], P('dp'), parts along dimension 0, may hold values from 0 to 16, as said below
- train_step: int32 [2], P('dp'), parts along dimension 0, may hold values from 1 to 15
Outputs:
- mixed: bfloat16 [16384, 5120], P(('dp', 'ctx'), 'mp'), parts along dimension 0
There are 2 independent parts, one for each index of `dp`. A program takes and returns all parts, laid end to end along the dimension named above; an argument that names none is the same for every part. Nothing has to cross between parts.
Inputs may be any that keep to these rules, and one draw needn't show every extreme that they name: `reveal_step`: 0 where the key block does not come after the query block, between 1 and 16 where it does.
All inputs are finite; a program needn't handle non-finite values.
Results may differ from a plain program's by a relative error of at most 0.017.
Values may be sent and summed in bfloat16 or wider, within the bound.
No kernel may reach another device: no remote copies, remote signals or barrier semaphores. Data moves between devices by JAX's collectives and lax.ppermute only.
A program may use at most 64 MiB of HBM per device.

v0:
```python
import math

import jax
import jax.numpy as jnp
from jax import lax
from jax.sharding import PartitionSpec as P

HEAD_WIDTH = 128
BLK = 128


def passed_along(block, axis, distance):
    devices = range(lax.axis_size(axis))
    route = [((i - distance) % len(devices), i) for i in devices]
    return lax.ppermute(block, axis, route)


def documents(slot_pos, doc_lengths):
    doc_ends = jnp.cumsum(doc_lengths)
    return jnp.sum((slot_pos[:, None] >= doc_ends[None, :]).astype(jnp.int32), axis=1)


def per_device(
    queries, keys, values, out_weight, block_order, doc_lengths, reveal_step, train_step
):
    q_rows = queries.shape[0]
    kv_heads = keys.shape[1] // HEAD_WIDTH
    group_size = queries.shape[1] // keys.shape[1]
    cycle_size = lax.axis_size("ctx")
    own_rank = lax.axis_index("ctx")
    all_slots = jnp.arange(cycle_size * q_rows, dtype=jnp.int32)
    slot_pos = block_order[all_slots // BLK] * BLK + all_slots % BLK
    slot_doc = documents(slot_pos, doc_lengths)
    slot_block = slot_pos // BLK
    own_start = own_rank * q_rows
    query_doc = lax.dynamic_slice_in_dim(slot_doc, own_start, q_rows, 0)
    query_block = lax.dynamic_slice_in_dim(slot_block, own_start, q_rows, 0)
    reveal_rows = reveal_step[query_block] <= train_step[0]
    query_heads = queries.reshape(q_rows, kv_heads, group_size, HEAD_WIDTH)
    scaling = 1.0 / math.sqrt(HEAD_WIDTH)

    def update_tile(running, key_piece, key_start):
        key_rows = key_piece.shape[1]
        key_heads = key_piece[0].reshape(key_rows, kv_heads, HEAD_WIDTH)
        value_heads = key_piece[1].reshape(key_rows, kv_heads, HEAD_WIDTH)
        key_doc = lax.dynamic_slice_in_dim(slot_doc, key_start, key_rows, 0)
        key_block = lax.dynamic_slice_in_dim(slot_block, key_start, key_rows, 0)
        allowed = (query_doc[:, None] == key_doc[None, :]) & jnp.take(
            reveal_rows, key_block, axis=1
        )
        row_max, row_total, partial_out = running
        scores = (
            jnp.einsum("qhgd,khd->hgqk", query_heads, key_heads, preferred_element_type=jnp.float32)
            * scaling
        )
        new_max = jnp.maximum(row_max, jnp.max(jnp.where(allowed, scores, -1e30), axis=3))
        probs = jnp.where(allowed, jnp.exp(scores - new_max[..., None]), 0.0)
        factor = jnp.exp(row_max - new_max)
        new_total = row_total * factor + jnp.sum(probs, axis=3)
        carried = jnp.einsum(
            "hgqk,khd->qhgd",
            probs.astype(jnp.bfloat16),
            value_heads,
            preferred_element_type=jnp.float32,
        )
        new_out = partial_out * jnp.transpose(factor, (2, 0, 1))[..., None] + carried
        return (new_max, new_total, new_out)

    def fold_piece(running, key_piece, key_start):
        key_rows = key_piece.shape[1]
        return update_tile(running, key_piece, key_start)

    start_state = (
        jnp.full((kv_heads, group_size, q_rows), -1e30, jnp.float32),
        jnp.zeros((kv_heads, group_size, q_rows), jnp.float32),
        jnp.zeros((q_rows, kv_heads, group_size, HEAD_WIDTH), jnp.float32),
    )
    packed = jnp.stack([keys, values])
    running = fold_piece(start_state, packed, own_start)

    def one_hop(step_num, loop_carry):
        current, moving = loop_carry
        moving = passed_along(moving, "ctx", 1)
        source = (own_rank - step_num) % cycle_size
        return (fold_piece(current, moving, source * q_rows), moving)

    running, moving = lax.fori_loop(1, cycle_size, one_hop, (running, packed))
    row_max, row_total, partial_out = running
    attended = partial_out / jnp.transpose(row_total, (2, 0, 1))[..., None]
    attended = attended.reshape(q_rows, kv_heads * group_size * HEAD_WIDTH).astype(jnp.bfloat16)
    partial_value = jnp.dot(attended, out_weight, preferred_element_type=jnp.float32)
    return lax.psum_scatter(
        partial_value.astype(jnp.bfloat16), "mp", scatter_dimension=1, tiled=True
    )


def solution(mesh):
    in_specs = (
        P(("dp", "ctx"), "mp"),
        P(("dp", "ctx"), "mp"),
        P(("dp", "ctx"), "mp"),
        P("mp", None),
        P("dp"),
        P("dp"),
        P("dp", None),
        P("dp"),
    )
    out_specs = P(("dp", "ctx"), "mp")
    return jax.shard_map(
        per_device, mesh=mesh, in_specs=in_specs, out_specs=out_specs, check_vma=False
    )
```

profile of v0, /device:TPU:1, one launch (start us, length us, event | category | flops | bytes accessed | tf_op | source)
XLA Modules:
  0.0 415.2 jit_solution(8797349940492321684)
XLA Ops:
  21.8 35.9 %add_select_fusion = (s32[8192]{0:T(1024)S(1)}, s32[8192]{0:T(1024)S(1)}) fusion(pred[8192]{0:T(1024)(128)(4,1)S(1)} %compare_reduce_fusion, pred[8192]{0:T(1024)(128)(4,1)S(1)} %compare_reduce_fusion.1, pred[8192]{0:T(1024)(128)(4,1)S(1)} %compare_reduce_fusion.2, pred[8192]{0:T(1024)(128)(4,1)S(1)} %compare_reduce_fusion.3, ...), kind=kLoop, calls=%fused_computation.115 | loop fusion | flops 655360 | bytes 565476 | tf_op jit(solution)/shard_map/jit(floor_divide)/jit(_where)/select_n | solution.py:34
  62.9 275.9 %while.21 = (s32[]{:T(128)}, f32[1,5,256]{2,1,0:T(8,128)S(1)}, f32[1,5,256]{2,1,0:T(8,128)S(1)}, f32[256,1,5,128]{3,0,2,1:T(8,128)S(1)}, bf16[2,256,128]{2,1,0:T...) while((s32[]{:T(128)}, f32[1,5,256]{2,1,0:T(8,128)S(1)}, ...), condition=%wide.region_7.9_spmd, body=%wide.region_4.8_spmd.sunk | while | flops 171251984 | bytes 7048052 | solution.py:87
  66.8 8.2 %collective-permute-done = bf16[2,256,128]{2,1,0:T(8,128)(2,1)S(1)} collective-permute-done((bf16[2,256,128]{2,1,0:T(8,128)(2,1)S(1)}, bf16[2,256,128]{2,1,0:T(8,128)(2,1)S(1)}, u32[]{:S(2)}, u32[]{:S(2)}) %collective-permute-start) | collective-permute-done | bytes 131104 | tf_op jit(solution)/shard_map/while/body/eval_jaxpr/ppermute | solution.py:15
  77.8 5.7 %collective-permute-done = bf16[2,256,128]{2,1,0:T(8,128)(2,1)S(1)} collective-permute-done((bf16[2,256,128]{2,1,0:T(8,128)(2,1)S(1)}, bf16[2,256,128]{2,1,0:T(8,128)(2,1)S(1)}, u32[]{:S(2)}, u32[]{:S(2)}) %collective-permute-start) | collective-permute-done | bytes 131104 | tf_op jit(solution)/shard_map/while/body/eval_jaxpr/ppermute | solution.py:15
  86.3 5.7 %collective-permute-done = bf16[2,256,128]{2,1,0:T(8,128)(2,1)S(1)} collective-permute-done((bf16[2,256,128]{2,1,0:T(8,128)(2,1)S(1)}, bf16[2,256,128]{2,1,0:T(8,128)(2,1)S(1)}, u32[]{:S(2)}, u32[]{:S(2)}) %collective-permute-start) | collective-permute-done | bytes 131104 | tf_op jit(solution)/shard_map/while/body/eval_jaxpr/ppermute | solution.py:15
  94.8 5.7 %collective-permute-done = bf16[2,256,128]{2,1,0:T(8,128)(2,1)S(1)} collective-permute-done((bf16[2,256,128]{2,1,0:T(8,128)(2,1)S(1)}, bf16[2,256,128]{2,1,0:T(8,128)(2,1)S(1)}, u32[]{:S(2)}, u32[]{:S(2)}) %collective-permute-start) | collective-permute-done | bytes 131104 | tf_op jit(solution)/shard_map/while/body/eval_jaxpr/ppermute | solution.py:15
  103.3 5.7 %collective-permute-done = bf16[2,256,128]{2,1,0:T(8,128)(2,1)S(1)} collective-permute-done((bf16[2,256,128]{2,1,0:T(8,128)(2,1)S(1)}, bf16[2,256,128]{2,1,0:T(8,128)(2,1)S(1)}, u32[]{:S(2)}, u32[]{:S(2)}) %collective-permute-start) | collective-permute-done | bytes 131104 | tf_op jit(solution)/shard_map/while/body/eval_jaxpr/ppermute | solution.py:15
  111.8 5.7 %collective-permute-done = bf16[2,256,128]{2,1,0:T(8,128)(2,1)S(1)} collective-permute-done((bf16[2,256,128]{2,1,0:T(8,128)(2,1)S(1)}, bf16[2,256,128]{2,1,0:T(8,128)(2,1)S(1)}, u32[]{:S(2)}, u32[]{:S(2)}) %collective-permute-start) | collective-permute-done | bytes 131104 | tf_op jit(solution)/shard_map/while/body/eval_jaxpr/ppermute | solution.py:15
  120.3 5.7 %collective-permute-done = bf16[2,256,128]{2,1,0:T(8,128)(2,1)S(1)} collective-permute-done((bf16[2,256,128]{2,1,0:T(8,128)(2,1)S(1)}, bf16[2,256,128]{2,1,0:T(8,128)(2,1)S(1)}, u32[]{:S(2)}, u32[]{:S(2)}) %collective-permute-start) | collective-permute-done | bytes 131104 | tf_op jit(solution)/shard_map/while/body/eval_jaxpr/ppermute | solution.py:15
  128.8 6.1 %collective-permute-done = bf16[2,256,128]{2,1,0:T(8,128)(2,1)S(1)} collective-permute-done((bf16[2,256,128]{2,1,0:T(8,128)(2,1)S(1)}, bf16[2,256,128]{2,1,0:T(8,128)(2,1)S(1)}, u32[]{:S(2)}, u32[]{:S(2)}) %collective-permute-start) | collective-permute-done | bytes 131104 | tf_op jit(solution)/shard_map/while/body/eval_jaxpr/ppermute | solution.py:15
  137.6 7.3 %collective-permute-done = bf16[2,256,128]{2,1,0:T(8,128)(2,1)S(1)} collective-permute-done((bf16[2,256,128]{2,1,0:T(8,128)(2,1)S(1)}, bf16[2,256,128]{2,1,0:T(8,128)(2,1)S(1)}, u32[]{:S(2)}, u32[]{:S(2)}) %collective-permute-start) | collective-permute-done | bytes 131104 | tf_op jit(solution)/shard_map/while/body/eval_jaxpr/ppermute | solution.py:15
  147.7 6.5 %collective-permute-done = bf16[2,256,128]{2,1,0:T(8,128)(2,1)S(1)} collective-permute-done((bf16[2,256,128]{2,1,0:T(8,128)(2,1)S(1)}, bf16[2,256,128]{2,1,0:T(8,128)(2,1)S(1)}, u32[]{:S(2)}, u32[]{:S(2)}) %collective-permute-start) | collective-permute-done | bytes 131104 | tf_op jit(solution)/shard_map/while/body/eval_jaxpr/ppermute | solution.py:15
  157.0 5.7 %collective-permute-done = bf16[2,256,128]{2,1,0:T(8,128)(2,1)S(1)} collective-permute-done((bf16[2,256,128]{2,1,0:T(8,128)(2,1)S(1)}, bf16[2,256,128]{2,1,0:T(8,128)(2,1)S(1)}, u32[]{:S(2)}, u32[]{:S(2)}) %collective-permute-start) | collective-permute-done | bytes 131104 | tf_op jit(solution)/shard_map/while/body/eval_jaxpr/ppermute | solution.py:15
  165.5 5.7 %collective-permute-done = bf16[2,256,128]{2,1,0:T(8,128)(2,1)S(1)} collective-permute-done((bf16[2,256,128]{2,1,0:T(8,128)(2,1)S(1)}, bf16[2,256,128]{2,1,0:T(8,128)(2,1)S(1)}, u32[]{:S(2)}, u32[]{:S(2)}) %collective-permute-start) | collective-permute-done | bytes 131104 | tf_op jit(solution)/shard_map/while/body/eval_jaxpr/ppermute | solution.py:15
  174.0 5.7 %collective-permute-done = bf16[2,256,128]{2,1,0:T(8,128)(2,1)S(1)} collective-permute-done((bf16[2,256,128]{2,1,0:T(8,128)(2,1)S(1)}, bf16[2,256,128]{2,1,0:T(8,128)(2,1)S(1)}, u32[]{:S(2)}, u32[]{:S(2)}) %collective-permute-start) | collective-permute-done | bytes 131104 | tf_op jit(solution)/shard_map/while/body/eval_jaxpr/ppermute | solution.py:15
  182.5 5.7 %collective-permute-done = bf16[2,256,128]{2,1,0:T(8,128)(2,1)S(1)} collective-permute-done((bf16[2,256,128]{2,1,0:T(8,128)(2,1)S(1)}, bf16[2,256,128]{2,1,0:T(8,128)(2,1)S(1)}, u32[]{:S(2)}, u32[]{:S(2)}) %collective-permute-start) | collective-permute-done | bytes 131104 | tf_op jit(solution)/shard_map/while/body/eval_jaxpr/ppermute | solution.py:15
  191.0 5.7 %collective-permute-done = bf16[2,256,128]{2,1,0:T(8,128)(2,1)S(1)} collective-permute-done((bf16[2,256,128]{2,1,0:T(8,128)(2,1)S(1)}, bf16[2,256,128]{2,1,0:T(8,128)(2,1)S(1)}, u32[]{:S(2)}, u32[]{:S(2)}) %collective-permute-start) | collective-permute-done | bytes 131104 | tf_op jit(solution)/shard_map/while/body/eval_jaxpr/ppermute | solution.py:15
  199.5 5.7 %collective-permute-done = bf16[2,256,128]{2,1,0:T(8,128)(2,1)S(1)} collective-permute-done((bf16[2,256,128]{2,1,0:T(8,128)(2,1)S(1)}, bf16[2,256,128]{2,1,0:T(8,128)(2,1)S(1)}, u32[]{:S(2)}, u32[]{:S(2)}) %collective-permute-start) | collective-permute-done | bytes 131104 | tf_op jit(solution)/shard_map/while/body/eval_jaxpr/ppermute | solution.py:15
  208.0 6.2 %collective-permute-done = bf16[2,256,128]{2,1,0:T(8,128)(2,1)S(1)} collective-permute-done((bf16[2,256,128]{2,1,0:T(8,128)(2,1)S(1)}, bf16[2,256,128]{2,1,0:T(8,128)(2,1)S(1)}, u32[]{:S(2)}, u32[]{:S(2)}) %collective-permute-start) | collective-permute-done | bytes 131104 | tf_op jit(solution)/shard_map/while/body/eval_jaxpr/ppermute | solution.py:15
  216.9 7.2 %collective-permute-done = bf16[2,256,128]{2,1,0:T(8,128)(2,1)S(1)} collective-permute-done((bf16[2,256,128]{2,1,0:T(8,128)(2,1)S(1)}, bf16[2,256,128]{2,1,0:T(8,128)(2,1)S(1)}, u32[]{:S(2)}, u32[]{:S(2)}) %collective-permute-start) | collective-permute-done | bytes 131104 | tf_op jit(solution)/shard_map/while/body/eval_jaxpr/ppermute | solution.py:15
  226.9 6.3 %collective-permute-done = bf16[2,256,128]{2,1,0:T(8,128)(2,1)S(1)} collective-permute-done((bf16[2,256,128]{2,1,0:T(8,128)(2,1)S(1)}, bf16[2,256,128]{2,1,0:T(8,128)(2,1)S(1)}, u32[]{:S(2)}, u32[]{:S(2)}) %collective-permute-start) | collective-permute-done | bytes 131104 | tf_op jit(solution)/shard_map/while/body/eval_jaxpr/ppermute | solution.py:15
  235.9 5.7 %collective-permute-done = bf16[2,256,128]{2,1,0:T(8,128)(2,1)S(1)} collective-permute-done((bf16[2,256,128]{2,1,0:T(8,128)(2,1)S(1)}, bf16[2,256,128]{2,1,0:T(8,128)(2,1)S(1)}, u32[]{:S(2)}, u32[]{:S(2)}) %collective-permute-start) | collective-permute-done | bytes 131104 | tf_op jit(solution)/shard_map/while/body/eval_jaxpr/ppermute | solution.py:15
  244.4 5.7 %collective-permute-done = bf16[2,256,128]{2,1,0:T(8,128)(2,1)S(1)} collective-permute-done((bf16[2,256,128]{2,1,0:T(8,128)(2,1)S(1)}, bf16[2,256,128]{2,1,0:T(8,128)(2,1)S(1)}, u32[]{:S(2)}, u32[]{:S(2)}) %collective-permute-start) | collective-permute-done | bytes 131104 | tf_op jit(solution)/shard_map/while/body/eval_jaxpr/ppermute | solution.py:15
  252.9 5.7 %collective-permute-done = bf16[2,256,128]{2,1,0:T(8,128)(2,1)S(1)} collective-permute-done((bf16[2,256,128]{2,1,0:T(8,128)(2,1)S(1)}, bf16[2,256,128]{2,1,0:T(8,128)(2,1)S(1)}, u32[]{:S(2)}, u32[]{:S(2)}) %collective-permute-start) | collective-permute-done | bytes 131104 | tf_op jit(solution)/shard_map/while/body/eval_jaxpr/ppermute | solution.py:15
  261.4 5.7 %collective-permute-done = bf16[2,256,128]{2,1,0:T(8,128)(2,1)S(1)} collective-permute-done((bf16[2,256,128]{2,1,0:T(8,128)(2,1)S(1)}, bf16[2,256,128]{2,1,0:T(8,128)(2,1)S(1)}, u32[]{:S(2)}, u32[]{:S(2)}) %collective-permute-start) | collective-permute-done | bytes 131104 | tf_op jit(solution)/shard_map/while/body/eval_jaxpr/ppermute | solution.py:15
  269.9 5.7 %collective-permute-done = bf16[2,256,128]{2,1,0:T(8,128)(2,1)S(1)} collective-permute-done((bf16[2,256,128]{2,1,0:T(8,128)(2,1)S(1)}, bf16[2,256,128]{2,1,0:T(8,128)(2,1)S(1)}, u32[]{:S(2)}, u32[]{:S(2)}) %collective-permute-start) | collective-permute-done | bytes 131104 | tf_op jit(solution)/shard_map/while/body/eval_jaxpr/ppermute | solution.py:15
  278.4 5.7 %collective-permute-done = bf16[2,256,128]{2,1,0:T(8,128)(2,1)S(1)} collective-permute-done((bf16[2,256,128]{2,1,0:T(8,128)(2,1)S(1)}, bf16[2,256,128]{2,1,0:T(8,128)(2,1)S(1)}, u32[]{:S(2)}, u32[]{:S(2)}) %collective-permute-start) | collective-permute-done | bytes 131104 | tf_op jit(solution)/shard_map/while/body/eval_jaxpr/ppermute | solution.py:15
  286.9 6.4 %collective-permute-done = bf16[2,256,128]{2,1,0:T(8,128)(2,1)S(1)} collective-permute-done((bf16[2,256,128]{2,1,0:T(8,128)(2,1)S(1)}, bf16[2,256,128]{2,1,0:T(8,128)(2,1)S(1)}, u32[]{:S(2)}, u32[]{:S(2)}) %collective-permute-start) | collective-permute-done | bytes 131104 | tf_op jit(solution)/shard_map/while/body/eval_jaxpr/ppermute | solution.py:15
  296.1 7.1 %collective-permute-done = bf16[2,256,128]{2,1,0:T(8,128)(2,1)S(1)} collective-permute-done((bf16[2,256,128]{2,1,0:T(8,128)(2,1)S(1)}, bf16[2,256,128]{2,1,0:T(8,128)(2,1)S(1)}, u32[]{:S(2)}, u32[]{:S(2)}) %collective-permute-start) | collective-permute-done | bytes 131104 | tf_op jit(solution)/shard_map/while/body/eval_jaxpr/ppermute | solution.py:15
  305.9 6.2 %collective-permute-done = bf16[2,256,128]{2,1,0:T(8,128)(2,1)S(1)} collective-permute-done((bf16[2,256,128]{2,1,0:T(8,128)(2,1)S(1)}, bf16[2,256,128]{2,1,0:T(8,128)(2,1)S(1)}, u32[]{:S(2)}, u32[]{:S(2)}) %collective-permute-start) | collective-permute-done | bytes 131104 | tf_op jit(solution)/shard_map/while/body/eval_jaxpr/ppermute | solution.py:15
  339.1 6.6 %convolution_convert_fusion = bf16[256,5120]{1,0:T(8,128)(2,1)} fusion(bf16[256,640]{0,1:T(8,128)(2,1)S(1)} %bitcast.179, bf16[640,5120]{1,0:T(8,128)(2,1)} %param.15), kind=kOutput, calls=%fused_computation.27 | convolution fusion | flops 1679032320 | bytes 9502720 | tf_op jit(solution)/shard_map/dot_general | solution.py:91
  345.8 62.6 %reduce-scatter.2.cloned.1.call-done = bf16[256,1280]{1,0:T(8,128)(2,1)} async-done(((bf16[256,5120]{1,0:T(8,128)(2,1)}), bf16[256,1280]{1,0:T(8,128)(2,1)}) %reduce-scatter.2.cloned.1.call-update) | async-done | bytes 655376 | tf_op jit(solution)/shard_map/reduce_scatter | solution.py:92
  (500 shorter events, 122.0 us)
Async XLA Ops:
  6.5 401.8 %reduce-scatter.2.cloned.1.call-start = ((), (), s32[]{:S(2)}) async-start(), calls=%async_computation.1 | async-start | bytes 3276800 | tf_op jit(solution)/shard_map/reduce_scatter | solution.py:92
  62.9 12.1 %collective-permute-start = (bf16[2,256,128]{2,1,0:T(8,128)(2,1)S(1)}, bf16[2,256,128]{2,1,0:T(8,128)(2,1)S(1)}, u32[]{:S(2)}, u32[]{:S(2)}) collective-permute-start(bf16[2,256,128]{2,1,0:T(8,128)(2,1)S(1)} %get-tuple-element.509), channel_id=1, source_target_pairs={{124,0},{0,4},{4,8},{8,12},{12,16},{16,20},{20,24},{24,28},{28,32}... | collective-permute-start | bytes 393224 | tf_op jit(solution)/shard_map/while/body/eval_jaxpr/ppermute | solution.py:15
  76.3 7.2 %collective-permute-start = (bf16[2,256,128]{2,1,0:T(8,128)(2,1)S(1)}, bf16[2,256,128]{2,1,0:T(8,128)(2,1)S(1)}, u32[]{:S(2)}, u32[]{:S(2)}) collective-permute-start(bf16[2,256,128]{2,1,0:T(8,128)(2,1)S(1)} %get-tuple-element.509), channel_id=1, source_target_pairs={{124,0},{0,4},{4,8},{8,12},{12,16},{16,20},{20,24},{24,28},{28,32}... | collective-permute-start | bytes 393224 | tf_op jit(solution)/shard_map/while/body/eval_jaxpr/ppermute | solution.py:15
  84.8 7.2 %collective-permute-start = (bf16[2,256,128]{2,1,0:T(8,128)(2,1)S(1)}, bf16[2,256,128]{2,1,0:T(8,128)(2,1)S(1)}, u32[]{:S(2)}, u32[]{:S(2)}) collective-permute-start(bf16[2,256,128]{2,1,0:T(8,128)(2,1)S(1)} %get-tuple-element.509), channel_id=1, source_target_pairs={{124,0},{0,4},{4,8},{8,12},{12,16},{16,20},{20,24},{24,28},{28,32}... | collective-permute-start | bytes 393224 | tf_op jit(solution)/shard_map/while/body/eval_jaxpr/ppermute | solution.py:15
  93.3 7.2 %collective-permute-start = (bf16[2,256,128]{2,1,0:T(8,128)(2,1)S(1)}, bf16[2,256,128]{2,1,0:T(8,128)(2,1)S(1)}, u32[]{:S(2)}, u32[]{:S(2)}) collective-permute-start(bf16[2,256,128]{2,1,0:T(8,128)(2,1)S(1)} %get-tuple-element.509), channel_id=1, source_target_pairs={{124,0},{0,4},{4,8},{8,12},{12,16},{16,20},{20,24},{24,28},{28,32}... | collective-permute-start | bytes 393224 | tf_op jit(solution)/shard_map/while/body/eval_jaxpr/ppermute | solution.py:15
  101.8 7.2 %collective-permute-start = (bf16[2,256,128]{2,1,0:T(8,128)(2,1)S(1)}, bf16[2,256,128]{2,1,0:T(8,128)(2,1)S(1)}, u32[]{:S(2)}, u32[]{:S(2)}) collective-permute-start(bf16[2,256,128]{2,1,0:T(8,128)(2,1)S(1)} %get-tuple-element.509), channel_id=1, source_target_pairs={{124,0},{0,4},{4,8},{8,12},{12,16},{16,20},{20,24},{24,28},{28,32}... | collective-permute-start | bytes 393224 | tf_op jit(solution)/shard_map/while/body/eval_jaxpr/ppermute | solution.py:15
  110.3 7.2 %collective-permute-start = (bf16[2,256,128]{2,1,0:T(8,128)(2,1)S(1)}, bf16[2,256,128]{2,1,0:T(8,128)(2,1)S(1)}, u32[]{:S(2)}, u32[]{:S(2)}) collective-permute-start(bf16[2,256,128]{2,1,0:T(8,128)(2,1)S(1)} %get-tuple-element.509), channel_id=1, source_target_pairs={{124,0},{0,4},{4,8},{8,12},{12,16},{16,20},{20,24},{24,28},{28,32}... | collective-permute-start | bytes 393224 | tf_op jit(solution)/shard_map/while/body/eval_jaxpr/ppermute | solution.py:15
  118.8 7.2 %collective-permute-start = (bf16[2,256,128]{2,1,0:T(8,128)(2,1)S(1)}, bf16[2,256,128]{2,1,0:T(8,128)(2,1)S(1)}, u32[]{:S(2)}, u32[]{:S(2)}) collective-permute-start(bf16[2,256,128]{2,1,0:T(8,128)(2,1)S(1)} %get-tuple-element.509), channel_id=1, source_target_pairs={{124,0},{0,4},{4,8},{8,12},{12,16},{16,20},{20,24},{24,28},{28,32}... | collective-permute-start | bytes 393224 | tf_op jit(solution)/shard_map/while/body/eval_jaxpr/ppermute | solution.py:15
  127.3 7.6 %collective-permute-start = (bf16[2,256,128]{2,1,0:T(8,128)(2,1)S(1)}, bf16[2,256,128]{2,1,0:T(8,128)(2,1)S(1)}, u32[]{:S(2)}, u32[]{:S(2)}) collective-permute-start(bf16[2,256,128]{2,1,0:T(8,128)(2,1)S(1)} %get-tuple-element.509), channel_id=1, source_target_pairs={{124,0},{0,4},{4,8},{8,12},{12,16},{16,20},{20,24},{24,28},{28,32}... | collective-permute-start | bytes 393224 | tf_op jit(solution)/shard_map/while/body/eval_jaxpr/ppermute | solution.py:15
  136.2 8.8 %collective-permute-start = (bf16[2,256,128]{2,1,0:T(8,128)(2,1)S(1)}, bf16[2,256,128]{2,1,0:T(8,128)(2,1)S(1)}, u32[]{:S(2)}, u32[]{:S(2)}) collective-permute-start(bf16[2,256,128]{2,1,0:T(8,128)(2,1)S(1)} %get-tuple-element.509), channel_id=1, source_target_pairs={{124,0},{0,4},{4,8},{8,12},{12,16},{16,20},{20,24},{24,28},{28,32}... | collective-permute-start | bytes 393224 | tf_op jit(solution)/shard_map/while/body/eval_jaxpr/ppermute | solution.py:15
  146.3 8.0 %collective-permute-start = (bf16[2,256,128]{2,1,0:T(8,128)(2,1)S(1)}, bf16[2,256,128]{2,1,0:T(8,128)(2,1)S(1)}, u32[]{:S(2)}, u32[]{:S(2)}) collective-permute-start(bf16[2,256,128]{2,1,0:T(8,128)(2,1)S(1)} %get-tuple-element.509), channel_id=1, source_target_pairs={{124,0},{0,4},{4,8},{8,12},{12,16},{16,20},{20,24},{24,28},{28,32}... | collective-permute-start | bytes 393224 | tf_op jit(solution)/shard_map/while/body/eval_jaxpr/ppermute | solution.py:15
  155.5 7.2 %collective-permute-start = (bf16[2,256,128]{2,1,0:T(8,128)(2,1)S(1)}, bf16[2,256,128]{2,1,0:T(8,128)(2,1)S(1)}, u32[]{:S(2)}, u32[]{:S(2)}) collective-permute-start(bf16[2,256,128]{2,1,0:T(8,128)(2,1)S(1)} %get-tuple-element.509), channel_id=1, source_target_pairs={{124,0},{0,4},{4,8},{8,12},{12,16},{16,20},{20,24},{24,28},{28,32}... | collective-permute-start | bytes 393224 | tf_op jit(solution)/shard_map/while/body/eval_jaxpr/ppermute | solution.py:15
  164.0 7.2 %collective-permute-start = (bf16[2,256,128]{2,1,0:T(8,128)(2,1)S(1)}, bf16[2,256,128]{2,1,0:T(8,128)(2,1)S(1)}, u32[]{:S(2)}, u32[]{:S(2)}) collective-permute-start(bf16[2,256,128]{2,1,0:T(8,128)(2,1)S(1)} %get-tuple-element.509), channel_id=1, source_target_pairs={{124,0},{0,4},{4,8},{8,12},{12,16},{16,20},{20,24},{24,28},{28,32}... | collective-permute-start | bytes 393224 | tf_op jit(solution)/shard_map/while/body/eval_jaxpr/ppermute | solution.py:15
  172.5 7.2 %collective-permute-start = (bf16[2,256,128]{2,1,0:T(8,128)(2,1)S(1)}, bf16[2,256,128]{2,1,0:T(8,128)(2,1)S(1)}, u32[]{:S(2)}, u32[]{:S(2)}) collective-permute-start(bf16[2,256,128]{2,1,0:T(8,128)(2,1)S(1)} %get-tuple-element.509), channel_id=1, source_target_pairs={{124,0},{0,4},{4,8},{8,12},{12,16},{16,20},{20,24},{24,28},{28,32}... | collective-permute-start | bytes 393224 | tf_op jit(solution)/shard_map/while/body/eval_jaxpr/ppermute | solution.py:15
  181.0 7.2 %collective-permute-start = (bf16[2,256,128]{2,1,0:T(8,128)(2,1)S(1)}, bf16[2,256,128]{2,1,0:T(8,128)(2,1)S(1)}, u32[]{:S(2)}, u32[]{:S(2)}) collective-permute-start(bf16[2,256,128]{2,1,0:T(8,128)(2,1)S(1)} %get-tuple-element.509), channel_id=1, source_target_pairs={{124,0},{0,4},{4,8},{8,12},{12,16},{16,20},{20,24},{24,28},{28,32}... | collective-permute-start | bytes 393224 | tf_op jit(solution)/shard_map/while/body/eval_jaxpr/ppermute | solution.py:15
  189.5 7.2 %collective-permute-start = (bf16[2,256,128]{2,1,0:T(8,128)(2,1)S(1)}, bf16[2,256,128]{2,1,0:T(8,128)(2,1)S(1)}, u32[]{:S(2)}, u32[]{:S(2)}) collective-permute-start(bf16[2,256,128]{2,1,0:T(8,128)(2,1)S(1)} %get-tuple-element.509), channel_id=1, source_target_pairs={{124,0},{0,4},{4,8},{8,12},{12,16},{16,20},{20,24},{24,28},{28,32}... | collective-permute-start | bytes 393224 | tf_op jit(solution)/shard_map/while/body/eval_jaxpr/ppermute | solution.py:15
  198.0 7.2 %collective-permute-start = (bf16[2,256,128]{2,1,0:T(8,128)(2,1)S(1)}, bf16[2,256,128]{2,1,0:T(8,128)(2,1)S(1)}, u32[]{:S(2)}, u32[]{:S(2)}) collective-permute-start(bf16[2,256,128]{2,1,0:T(8,128)(2,1)S(1)} %get-tuple-element.509), channel_id=1, source_target_pairs={{124,0},{0,4},{4,8},{8,12},{12,16},{16,20},{20,24},{24,28},{28,32}... | collective-permute-start | bytes 393224 | tf_op jit(solution)/shard_map/while/body/eval_jaxpr/ppermute | solution.py:15
  206.5 7.7 %collective-permute-start = (bf16[2,256,128]{2,1,0:T(8,128)(2,1)S(1)}, bf16[2,256,128]{2,1,0:T(8,128)(2,1)S(1)}, u32[]{:S(2)}, u32[]{:S(2)}) collective-permute-start(bf16[2,256,128]{2,1,0:T(8,128)(2,1)S(1)} %get-tuple-element.509), channel_id=1, source_target_pairs={{124,0},{0,4},{4,8},{8,12},{12,16},{16,20},{20,24},{24,28},{28,32}... | collective-permute-start | bytes 393224 | tf_op jit(solution)/shard_map/while/body/eval_jaxpr/ppermute | solution.py:15
  215.5 8.7 %collective-permute-start = (bf16[2,256,128]{2,1,0:T(8,128)(2,1)S(1)}, bf16[2,256,128]{2,1,0:T(8,128)(2,1)S(1)}, u32[]{:S(2)}, u32[]{:S(2)}) collective-permute-start(bf16[2,256,128]{2,1,0:T(8,128)(2,1)S(1)} %get-tuple-element.509), channel_id=1, source_target_pairs={{124,0},{0,4},{4,8},{8,12},{12,16},{16,20},{20,24},{24,28},{28,32}... | collective-permute-start | bytes 393224 | tf_op jit(solution)/shard_map/while/body/eval_jaxpr/ppermute | solution.py:15
  225.4 7.8 %collective-permute-start = (bf16[2,256,128]{2,1,0:T(8,128)(2,1)S(1)}, bf16[2,256,128]{2,1,0:T(8,128)(2,1)S(1)}, u32[]{:S(2)}, u32[]{:S(2)}) collective-permute-start(bf16[2,256,128]{2,1,0:T(8,128)(2,1)S(1)} %get-tuple-element.509), channel_id=1, source_target_pairs={{124,0},{0,4},{4,8},{8,12},{12,16},{16,20},{20,24},{24,28},{28,32}... | collective-permute-start | bytes 393224 | tf_op jit(solution)/shard_map/while/body/eval_jaxpr/ppermute | solution.py:15
  234.5 7.2 %collective-permute-start = (bf16[2,256,128]{2,1,0:T(8,128)(2,1)S(1)}, bf16[2,256,128]{2,1,0:T(8,128)(2,1)S(1)}, u32[]{:S(2)}, u32[]{:S(2)}) collective-permute-start(bf16[2,256,128]{2,1,0:T(8,128)(2,1)S(1)} %get-tuple-element.509), channel_id=1, source_target_pairs={{124,0},{0,4},{4,8},{8,12},{12,16},{16,20},{20,24},{24,28},{28,32}... | collective-permute-start | bytes 393224 | tf_op jit(solution)/shard_map/while/body/eval_jaxpr/ppermute | solution.py:15
  242.9 7.2 %collective-permute-start = (bf16[2,256,128]{2,1,0:T(8,128)(2,1)S(1)}, bf16[2,256,128]{2,1,0:T(8,128)(2,1)S(1)}, u32[]{:S(2)}, u32[]{:S(2)}) collective-permute-start(bf16[2,256,128]{2,1,0:T(8,128)(2,1)S(1)} %get-tuple-element.509), channel_id=1, source_target_pairs={{124,0},{0,4},{4,8},{8,12},{12,16},{16,20},{20,24},{24,28},{28,32}... | collective-permute-start | bytes 393224 | tf_op jit(solution)/shard_map/while/body/eval_jaxpr/ppermute | solution.py:15
  251.4 7.2 %collective-permute-start = (bf16[2,256,128]{2,1,0:T(8,128)(2,1)S(1)}, bf16[2,256,128]{2,1,0:T(8,128)(2,1)S(1)}, u32[]{:S(2)}, u32[]{:S(2)}) collective-permute-start(bf16[2,256,128]{2,1,0:T(8,128)(2,1)S(1)} %get-tuple-element.509), channel_id=1, source_target_pairs={{124,0},{0,4},{4,8},{8,12},{12,16},{16,20},{20,24},{24,28},{28,32}... | collective-permute-start | bytes 393224 | tf_op jit(solution)/shard_map/while/body/eval_jaxpr/ppermute | solution.py:15
  259.9 7.2 %collective-permute-start = (bf16[2,256,128]{2,1,0:T(8,128)(2,1)S(1)}, bf16[2,256,128]{2,1,0:T(8,128)(2,1)S(1)}, u32[]{:S(2)}, u32[]{:S(2)}) collective-permute-start(bf16[2,256,128]{2,1,0:T(8,128)(2,1)S(1)} %get-tuple-element.509), channel_id=1, source_target_pairs={{124,0},{0,4},{4,8},{8,12},{12,16},{16,20},{20,24},{24,28},{28,32}... | collective-permute-start | bytes 393224 | tf_op jit(solution)/shard_map/while/body/eval_jaxpr/ppermute | solution.py:15
  268.4 7.2 %collective-permute-start = (bf16[2,256,128]{2,1,0:T(8,128)(2,1)S(1)}, bf16[2,256,128]{2,1,0:T(8,128)(2,1)S(1)}, u32[]{:S(2)}, u32[]{:S(2)}) collective-permute-start(bf16[2,256,128]{2,1,0:T(8,128)(2,1)S(1)} %get-tuple-element.509), channel_id=1, source_target_pairs={{124,0},{0,4},{4,8},{8,12},{12,16},{16,20},{20,24},{24,28},{28,32}... | collective-permute-start | bytes 393224 | tf_op jit(solution)/shard_map/while/body/eval_jaxpr/ppermute | solution.py:15
  276.9 7.2 %collective-permute-start = (bf16[2,256,128]{2,1,0:T(8,128)(2,1)S(1)}, bf16[2,256,128]{2,1,0:T(8,128)(2,1)S(1)}, u32[]{:S(2)}, u32[]{:S(2)}) collective-permute-start(bf16[2,256,128]{2,1,0:T(8,128)(2,1)S(1)} %get-tuple-element.509), channel_id=1, source_target_pairs={{124,0},{0,4},{4,8},{8,12},{12,16},{16,20},{20,24},{24,28},{28,32}... | collective-permute-start | bytes 393224 | tf_op jit(solution)/shard_map/while/body/eval_jaxpr/ppermute | solution.py:15
  285.4 7.9 %collective-permute-start = (bf16[2,256,128]{2,1,0:T(8,128)(2,1)S(1)}, bf16[2,256,128]{2,1,0:T(8,128)(2,1)S(1)}, u32[]{:S(2)}, u32[]{:S(2)}) collective-permute-start(bf16[2,256,128]{2,1,0:T(8,128)(2,1)S(1)} %get-tuple-element.509), channel_id=1, source_target_pairs={{124,0},{0,4},{4,8},{8,12},{12,16},{16,20},{20,24},{24,28},{28,32}... | collective-permute-start | bytes 393224 | tf_op jit(solution)/shard_map/while/body/eval_jaxpr/ppermute | solution.py:15
  294.6 8.5 %collective-permute-start = (bf16[2,256,128]{2,1,0:T(8,128)(2,1)S(1)}, bf16[2,256,128]{2,1,0:T(8,128)(2,1)S(1)}, u32[]{:S(2)}, u32[]{:S(2)}) collective-permute-start(bf16[2,256,128]{2,1,0:T(8,128)(2,1)S(1)} %get-tuple-element.509), channel_id=1, source_target_pairs={{124,0},{0,4},{4,8},{8,12},{12,16},{16,20},{20,24},{24,28},{28,32}... | collective-permute-start | bytes 393224 | tf_op jit(solution)/shard_map/while/body/eval_jaxpr/ppermute | solution.py:15
  304.4 7.7 %collective-permute-start = (bf16[2,256,128]{2,1,0:T(8,128)(2,1)S(1)}, bf16[2,256,128]{2,1,0:T(8,128)(2,1)S(1)}, u32[]{:S(2)}, u32[]{:S(2)}) collective-permute-start(bf16[2,256,128]{2,1,0:T(8,128)(2,1)S(1)} %get-tuple-element.509), channel_id=1, source_target_pairs={{124,0},{0,4},{4,8},{8,12},{12,16},{16,20},{20,24},{24,28},{28,32}... | collective-permute-start | bytes 393224 | tf_op jit(solution)/shard_map/while/body/eval_jaxpr/ppermute | solution.py:15
  313.4 7.2 %collective-permute-start = (bf16[2,256,128]{2,1,0:T(8,128)(2,1)S(1)}, bf16[2,256,128]{2,1,0:T(8,128)(2,1)S(1)}, u32[]{:S(2)}, u32[]{:S(2)}) collective-permute-start(bf16[2,256,128]{2,1,0:T(8,128)(2,1)S(1)} %get-tuple-element.509), channel_id=1, source_target_pairs={{124,0},{0,4},{4,8},{8,12},{12,16},{16,20},{20,24},{24,28},{28,32}... | collective-permute-start | bytes 393224 | tf_op jit(solution)/shard_map/while/body/eval_jaxpr/ppermute | solution.py:15
  321.9 7.2 %collective-permute-start = (bf16[2,256,128]{2,1,0:T(8,128)(2,1)S(1)}, bf16[2,256,128]{2,1,0:T(8,128)(2,1)S(1)}, u32[]{:S(2)}, u32[]{:S(2)}) collective-permute-start(bf16[2,256,128]{2,1,0:T(8,128)(2,1)S(1)} %get-tuple-element.509), channel_id=1, source_target_pairs={{124,0},{0,4},{4,8},{8,12},{12,16},{16,20},{20,24},{24,28},{28,32}... | collective-permute-start | bytes 393224 | tf_op jit(solution)/shard_map/while/body/eval_jaxpr/ppermute | solution.py:15
  330.4 7.2 %collective-permute-start = (bf16[2,256,128]{2,1,0:T(8,128)(2,1)S(1)}, bf16[2,256,128]{2,1,0:T(8,128)(2,1)S(1)}, u32[]{:S(2)}, u32[]{:S(2)}) collective-permute-start(bf16[2,256,128]{2,1,0:T(8,128)(2,1)S(1)} %get-tuple-element.509), channel_id=1, source_target_pairs={{124,0},{0,4},{4,8},{8,12},{12,16},{16,20},{20,24},{24,28},{28,32}... | collective-permute-start | bytes 393224 | tf_op jit(solution)/shard_map/while/body/eval_jaxpr/ppermute | solution.py:15
  (5 other events, 133.1 us)
Sparse Core Ops, SparseCore 0:
  345.9 62.4 reduce-scatter.1
where the time goes:
time: 416 us; the launch traced here: 415 us
  waiting for transfers between devices  250 us (60%)
  other arithmetic  59.3 us (14%)
  local copies, waits for them, and re-layouts  46.3 us (11%)
  matrix products  36.6 us (9%)
  between operations  14.2 us (3%)
  starting transfers between devices  5.06 us (1%)
    ppermute x31, waiting for transfers between devices, passed_along(): return lax.ppermute(block, axis, route)  188 us
    reduce_scatter x1, waiting for transfers between devices, per_device(): lax.psum_scatter(partial_value.astype(jnp.bfloat16), 'mp', scatter_dimens...  62.6 us
    select_n x1, other arithmetic, per_device(): slot_block = slot_pos // BLK  35.9 us
    gather x32, local copies, waits for them, and re-layouts, update_tile(): jnp.take(reveal_rows, key_block, axis=1)  33.7 us
    dot_general x32, matrix products, update_tile(): jnp.einsum('hgqk,khd->qhgd', probs.astype(jnp.bfloat16), value_heads, pre...  18.5 us
    dot_general x32, matrix products, update_tile(): jnp.einsum('qhgd,khd->hgqk', query_heads, key_heads, preferred_element_ty...  11.5 us
  transfers between devices with their start and end apart: 32, of which 32 were waited for; matrix products, arithmetic and copies ran while one was open for 10% of the time, Pallas kernels for 0%

commit v1 on v0

v1 whole, which is shorter than its diff:
```python
import math

import jax
import jax.numpy as jnp
from jax import lax
from jax.experimental import pallas as pl
from jax.experimental.pallas import tpu as pltpu
from jax.sharding import Mesh
from jax.sharding import PartitionSpec as P

HEAD_WIDTH = 128
BLK = 128
NY, NZ, NX, NC = 4, 8, 2, 2
RANKS = NY * NZ
SLOTS = 2 * RANKS
MASKED = -1e30
LOWEST = -1e20


def moved(x, dy, dz):
    route = [(((i // NZ + dy) % NY) * NZ + (i % NZ + dz) % NZ, i) for i in range(RANKS)]
    return lax.ppermute(x, ("y", "z"), route)


def gathered(kv):
    rows = kv.shape[0] // 2
    centre = {0: kv}
    for j in (2, -2, 1, -1, 4, 3, -3):
        centre[j % 8] = moved(kv, 2 * j, j)
    key_of, value_of = {}, {}
    for j, block in centre.items():
        at = ((2 * j) % NY, j % NZ)
        key_of[at], value_of[at] = block[:rows], block[rows:]
    for group in ((0, 2, 6, 1, 7), (4, 3, 5)):
        blocks = [centre[j] for j in group]
        both = jnp.concatenate(blocks)
        only_keys = jnp.concatenate([b[:rows] for b in blocks])
        only_values = jnp.concatenate([b[rows:] for b in blocks])
        for dy in (1, -1):
            got = moved(both, dy, 0)
            for i, j in enumerate(group):
                at = ((2 * j + dy) % NY, j % NZ)
                key_of[at] = got[2 * i * rows : (2 * i + 1) * rows]
                value_of[at] = got[(2 * i + 1) * rows : (2 * i + 2) * rows]
        got = moved(only_keys, 0, 1)
        for i, j in enumerate(group):
            key_of[((2 * j) % NY, (j + 1) % NZ)] = got[i * rows : (i + 1) * rows]
        got = moved(only_values, 0, -1)
        for i, j in enumerate(group):
            value_of[((2 * j) % NY, (j - 1) % NZ)] = got[i * rows : (i + 1) * rows]
    order = [(dy, dz) for dy in range(NY) for dz in range(NZ)]
    return jnp.concatenate([key_of[at] for at in order]), jnp.concatenate([value_of[at] for at in order])


def plan_kernel(place, order, lengths, reveal, step, lists, counts):
    y, z = place[0], place[1]
    for t in range(2):
        block = order[2 * (y * NZ + z) + t]
        first, last = block * BLK, block * BLK + BLK - 1
        end = jnp.int32(0)
        low, high, first_end = jnp.int32(0), jnp.int32(0), jnp.int32(0)
        for d in range(lengths.shape[0]):
            begin = end
            end = end + lengths[d]
            holds_first = (begin <= first) & (first < end)
            low = jnp.where(holds_first, begin, low)
            first_end = jnp.where(holds_first, end, first_end)
            high = jnp.where((begin <= last) & (last < end), end, high)
        one_doc = first_end == high

        def seen(s, key_block):
            begin = key_block * BLK
            near = (begin < high) & (begin + BLK > low)
            whole = one_doc & (begin >= low) & (begin + BLK <= high)
            return near & (reveal[block, key_block] <= step[0]), whole

        def key_block_of(s):
            dy, dz = s // (2 * NZ), (s // 2) % NZ
            rank = ((y + dy) % NY) * NZ + (z + dz) % NZ
            return order[2 * rank + s % 2]

        def put(at, s, key_block):
            lists[t, 0, at] = s
            lists[t, 1, at] = key_block

        def whole_ones(s, n):
            key_block = key_block_of(s)
            near, whole = seen(s, key_block)
            take = near & whole

            @pl.when(take)
            def _():
                put(n, s, key_block)

            return n + take.astype(jnp.int32)

        def masked_ones(s, n):
            key_block = key_block_of(s)
            near, whole = seen(s, key_block)
            take = near & jnp.logical_not(whole)

            @pl.when(take)
            def _():
                put(n, s, key_block)

            return n + take.astype(jnp.int32)

        n_whole = lax.fori_loop(0, SLOTS, whole_ones, jnp.int32(0))
        n = lax.fori_loop(0, SLOTS, masked_ones, n_whole)

        @pl.when(n % 2 == 1)
        def _():
            put(n, 0, SLOTS)

        counts[t, 0] = n_whole // 2
        counts[t, 1] = (n + 1) // 2


def attention_kernel(lists, counts, place, order, lengths, q_ref, k_ref, v_ref, out_ref, scores, top, total, acc):
    heads = q_ref.shape[1] // HEAD_WIDTH
    scale = math.log2(math.e) / math.sqrt(HEAD_WIDTH)

    def doc_of(pos):
        doc = jnp.zeros(pos.shape, jnp.int32)
        end = jnp.int32(0)
        for d in range(lengths.shape[0]):
            end = end + lengths[d]
            doc = doc + (pos >= end).astype(jnp.int32)
        return doc

    for t in range(2):
        block = order[2 * (place[0] * NZ + place[1]) + t]
        rows = pl.ds(t * BLK, BLK)
        q = jnp.concatenate([q_ref[rows, h * HEAD_WIDTH : (h + 1) * HEAD_WIDTH] for h in range(heads)])
        q_doc = doc_of(block * BLK + lax.broadcasted_iota(jnp.int32, (BLK, BLK), 0))
        top[...] = jnp.full(top.shape, LOWEST, jnp.float32)
        n_whole, n = counts[t, 0], counts[t, 1]

        def two(ref, i):
            return jnp.concatenate(
                [ref[pl.ds(pl.multiple_of(lists[t, 0, 2 * i + e] * BLK, BLK), BLK), :] for e in range(2)]
            )

        def dots(i):
            return lax.dot_general(q, two(k_ref, i), (((1,), (1,)), ((), ())), preferred_element_type=jnp.float32)

        def whole_pair(i, carry):
            s = dots(i)
            scores[i] = s
            top[...] = jnp.maximum(top[...], jnp.maximum(s[:, :BLK], s[:, BLK:]))
            return carry

        def masked_pair(i, carry):
            s = dots(i)
            lane = lax.broadcasted_iota(jnp.int32, (1, BLK), 1)
            for e in range(2):
                k_doc = doc_of(lists[t, 1, 2 * i + e] * BLK + lane)
                allowed = q_doc == k_doc
                for h in range(heads):
                    part = jnp.where(
                        allowed, s[h * BLK : (h + 1) * BLK, e * BLK : (e + 1) * BLK], MASKED
                    )
                    scores[i, pl.ds(h * BLK, BLK), pl.ds(e * BLK, BLK)] = part
                    top[pl.ds(h * BLK, BLK), :] = jnp.maximum(top[pl.ds(h * BLK, BLK), :], part)
            return carry

        lax.fori_loop(0, n_whole, whole_pair, 0)
        lax.fori_loop(n_whole, n, masked_pair, 0)
        top[...] = jnp.broadcast_to(jnp.max(top[...], axis=1, keepdims=True) * scale, top.shape)
        total[...] = jnp.zeros(total.shape, jnp.float32)
        acc[...] = jnp.zeros(acc.shape, jnp.float32)

        def weigh(i, carry):
            s = scores[i]
            m = top[...]
            p0 = jnp.exp2(s[:, :BLK] * scale - m)
            p1 = jnp.exp2(s[:, BLK:] * scale - m)
            total[...] += p0 + p1
            p = jnp.concatenate([p0.astype(jnp.bfloat16), p1.astype(jnp.bfloat16)], axis=1)
            acc[...] += jnp.dot(p, two(v_ref, i), preferred_element_type=jnp.float32)
            return carry

        lax.fori_loop(0, n, weigh, 0)
        attended = (acc[...] / jnp.sum(total[...], axis=1, keepdims=True)).astype(jnp.bfloat16)
        for h in range(heads):
            out_ref[rows, h * HEAD_WIDTH : (h + 1) * HEAD_WIDTH] = attended[h * BLK : (h + 1) * BLK]


def attention(queries, keys, values, block_order, doc_lengths, reveal_step, train_step):
    place = jnp.stack([lax.axis_index("y"), lax.axis_index("z")]).astype(jnp.int32)
    smem = pl.BlockSpec(memory_space=pltpu.SMEM)
    vmem = pl.BlockSpec(memory_space=pltpu.VMEM)
    lists, counts = pl.pallas_call(
        plan_kernel,
        out_shape=(
            jax.ShapeDtypeStruct((2, 2, SLOTS + 2), jnp.int32),
            jax.ShapeDtypeStruct((2, 2), jnp.int32),
        ),
        in_specs=[smem] * 5,
        out_specs=(smem, smem),
        name="plan",
    )(place, block_order, doc_lengths, reveal_step, train_step)
    rows = queries.shape[1] // HEAD_WIDTH * BLK
    return pl.pallas_call(
        attention_kernel,
        out_shape=jax.ShapeDtypeStruct(queries.shape, jnp.bfloat16),
        in_specs=[smem] * 5 + [vmem] * 3,
        out_specs=vmem,
        scratch_shapes=[
            pltpu.VMEM((17, rows, 2 * BLK), jnp.float32),
            pltpu.VMEM((rows, BLK), jnp.float32),
            pltpu.VMEM((rows, BLK), jnp.float32),
            pltpu.VMEM((rows, BLK), jnp.float32),
        ],
        compiler_params=pltpu.CompilerParams(vmem_limit_bytes=40 * 2**20),
        cost_estimate=pl.CostEstimate(flops=10**9, bytes_accessed=10**7, transcendentals=3 * 10**6),
        name="attention",
    )(lists, counts, place, block_order, doc_lengths, queries, keys, values)


def swapped(x, axis):
    return lax.ppermute(x, axis, [(0, 1), (1, 0)])


def per_device(queries, keys, values, out_weight, block_order, doc_lengths, reveal_step, train_step):
    x, core = lax.axis_index("x"), lax.axis_index("core")
    width = out_weight.shape[1] // (NX * NC)
    columns = out_weight.reshape(out_weight.shape[0], NX, NC, width)
    own_weight = lax.dynamic_index_in_dim(columns, core, 2, keepdims=False)
    other_weight = swapped(lax.dynamic_index_in_dim(columns, 1 - core, 2, keepdims=False), "core")
    all_keys, all_values = gathered(jnp.concatenate([keys, values]))
    attended = attention(queries, all_keys, all_values, block_order, doc_lengths, reveal_step, train_step)
    other_attended = swapped(attended, "core")

    def share(chip):
        return jnp.dot(
            attended, lax.dynamic_index_in_dim(own_weight, chip, 1, keepdims=False), preferred_element_type=jnp.float32
        ) + jnp.dot(
            other_attended,
            lax.dynamic_index_in_dim(other_weight, chip, 1, keepdims=False),
            preferred_element_type=jnp.float32,
        )

    sent = swapped(share(1 - x).astype(jnp.bfloat16), "x")
    return (share(x) + sent.astype(jnp.float32)).astype(jnp.bfloat16)


def solution(mesh):
    fine = Mesh(mesh.devices.reshape(mesh.devices.shape[0], NY, NZ, NX, NC), ("dp", "y", "z", "x", "core"))
    rows, heads = ("dp", "y", "z"), ("x", "core")
    in_specs = (
        P(rows, heads),
        P(rows, heads),
        P(rows, heads),
        P(heads, None),
        P("dp"),
        P("dp"),
        P("dp", None),
        P("dp"),
    )
    return jax.shard_map(per_device, mesh=fine, in_specs=in_specs, out_specs=P(rows, heads), check_vma=False)
```

time: 416 us -> 138 us (0.33)
  waiting for transfers between devices: 250 us -> 37.5 us
  other arithmetic: 59.3 us -> 0.67 us
  starting transfers between devices: 5.06 us -> 40.9 us
  matrix products: 36.6 us -> 10.2 us
  local copies, waits for them, and re-layouts: 46.3 us -> 26.2 us
  Pallas kernels: 0 us -> 18.8 us
  between operations: 14.2 us -> 1.1 us
    ppermute x31 -> x18, waiting for transfers between devices: 188 us -> 37.5 us  [the longest x15 23.4 us: moved(): return lax.ppermute(x, ('y', 'z'), route)]
    reduce_scatter x1 -> x0, waiting for transfers between devices: 62.6 us -> none  [per_device(): lax.psum_scatter(partial_value.astype(jnp.bfloat16), 'mp', scatter_dimens...]
    gather x37 -> x0, local copies, waits for them, and re-layouts: 42.3 us -> none  [the longest x32 33.7 us: update_tile(): jnp.take(reveal_rows, key_block, axis=1)]
    select_n x1 -> x0, other arithmetic: 35.9 us -> none  [per_device(): slot_block = slot_pos // BLK]
    ppermute x31 -> x18, starting transfers between devices: 5.05 us -> 40.9 us  [the longest x15 33.9 us: moved(): return lax.ppermute(x, ('y', 'z'), route)]
    dot_general x65 -> x4, matrix products: 36.6 us -> 10.2 us  [the longest x2 5.97 us: share(): jnp.dot(attended, lax.dynamic_index_in_dim(own_weight, chip, 1, keepdims=...]
    pallas_call x0 -> x2, Pallas kernels: none -> 18.8 us  [the longest x1 11.3 us: attention(): pl.pallas_call(plan_kernel, out_shape=(jax.ShapeDtypeStruct((2, 2, SLOTS...]
    unnamed x11 -> x62, local copies, waits for them, and re-layouts: 0.54 us -> 15.7 us
  transfers between devices with their start and end apart: 32 -> 18, of which waited for: 32 -> 7; matrix products, arithmetic and copies ran while one was open for 10% -> 19% of each run, Pallas kernels for 0% -> 14%
where the time goes in v1:
time: 138 us; the launch traced here: 135 us
  starting transfers between devices  40.9 us (30%)
  waiting for transfers between devices  37.5 us (27%)
  local copies, waits for them, and re-layouts  26.2 us (19%)
  Pallas kernels  18.8 us (14%)
  matrix products  10.2 us (7%)
    ppermute x15, starting transfers between devices, moved(): return lax.ppermute(x, ('y', 'z'), route)  33.9 us
    ppermute x15, waiting for transfers between devices, moved(): return lax.ppermute(x, ('y', 'z'), route)  23.4 us
    unnamed x62, local copies, waits for them, and re-layouts  15.7 us
    ppermute x3, waiting for transfers between devices, swapped(): return lax.ppermute(x, axis, [(0, 1), (1, 0)])  14.1 us
    pallas_call x1, Pallas kernels, attention(): pl.pallas_call(plan_kernel, out_shape=(jax.ShapeDtypeStruct((2, 2, SLOTS...  11.3 us
    dynamic_slice x2, local copies, waits for them, and re-layouts, per_device(): lax.dynamic_index_in_dim(columns, 1 - core, 2, keepdims=False)  9.71 us
    pallas_call x1, Pallas kernels, attention(): pl.pallas_call(attention_kernel, out_shape=jax.ShapeDtypeStruct(queries.s...  7.57 us
    ppermute x3, starting transfers between devices, swapped(): return lax.ppermute(x, axis, [(0, 1), (1, 0)])  7.06 us
  transfers between devices with their start and end apart: 18, of which 7 were waited for; matrix products, arithmetic and copies ran while one was open for 19% of the time, Pallas kernels for 14%

profile of v1, /device:TPU:1, one launch (start us, length us, event | category | flops | bytes accessed | tf_op | source)
XLA Modules:
  0.0 135.4 jit_solution(6258414870236465472)
XLA Ops:
  0.0 1.5 %constant_dynamic-update-slice_fusion.12 = (bf16[2560,128]{1,0:T(8,128)(2,1)}, bf16[1280,128]{1,0:T(8,128)(2,1)S(1)}, bf16[512,128]{1,0:T(8,128)(2,1)S(1)}, bf16[8192,128]{1,0:T(8,128)(2,1)}) fusion(bf16[256,128]{1,0:T(8,128)(2,1)} %param.9), kind=kLoop, calls=%fused_computation.29 | loop fusion | bytes 327680
  1.5 1.5 %constant_dynamic-update-slice_fusion.52 = (bf16[1280,128]{1,0:T(8,128)(2,1)S(1)}, bf16[2560,128]{1,0:T(8,128)(2,1)}, bf16[512,128]{1,0:T(8,128)(2,1)S(1)}, bf16[8192,128]{1,0:T(8,128)(2,1)S(1)}) fusion(bf16[256,128]{1,0:T(8,128)(2,1)} %param.10, bf16[2560,128]{1,0:T(8,128)(2,1)} %get-tuple-element.72, bf16[512,128]{1,0:T(8,128)(2,1)S(1)} %get-tuple-element.74), kind=kLoop, calls=%fused_computation.69 | loop fusion | bytes 327680
  3.0 6.8 %collective-permute-start = (bf16[512,128]{1,0:T(8,128)(2,1)S(1)}, bf16[512,128]{1,0:T(8,128)(2,1)S(1)}, u32[]{:S(2)}, u32[]{:S(2)}) collective-permute-start(bf16[512,128]{1,0:T(8,128)(2,1)S(1)} %get-tuple-element.70), channel_id=1, source_target_pairs={{8,0},{12,4},{16,8},{20,12},{24,16},{28,20},{0,24},{4,28},{40,32},... | collective-permute-start | bytes 393224 | tf_op jit(solution)/shard_map/ppermute | solution.py:22
  9.9 5.8 %collective-permute-start.2 = (bf16[512,128]{1,0:T(8,128)(2,1)S(1)}, bf16[512,128]{1,0:T(8,128)(2,1)S(1)}, u32[]{:S(2)}, u32[]{:S(2)}) collective-permute-start(bf16[512,128]{1,0:T(8,128)(2,1)S(1)} %get-tuple-element.70), channel_id=1, source_target_pairs={{68,0},{72,4},{76,8},{80,12},{84,16},{88,20},{92,24},{64,28},{100,... | collective-permute-start | bytes 393224 | tf_op jit(solution)/shard_map/ppermute | solution.py:22
  15.6 3.5 %collective-permute-start.6 = (bf16[512,128]{1,0:T(8,128)(2,1)S(1)}, bf16[512,128]{1,0:T(8,128)(2,1)S(1)}, u32[]{:S(2)}, u32[]{:S(2)}) collective-permute-start(bf16[512,128]{1,0:T(8,128)(2,1)S(1)} %get-tuple-element.70), channel_id=1, source_target_pairs={{76,0},{80,4},{84,8},{88,12},{92,16},{64,20},{68,24},{72,28},{108,... | collective-permute-start | bytes 393224 | tf_op jit(solution)/shard_map/ppermute | solution.py:22
  19.2 9.4 %copy.9 = bf16[640,5120]{0,1:T(8,128)(2,1)} copy(bf16[640,5120]{1,0:T(8,128)(2,1)} %param.11) | data formatting | bytes 13107200 | tf_op args[3]
  28.6 4.0 %constant_dynamic-slice_fusion = bf16[640,2,1,1280]{0,3,2,1:T(8,128)(2,1)} fusion(bf16[640,2,2,1280]{0,3,2,1:T(8,128)(2,1)} %bitcast.22, s32[]{:T(128)S(6)} %select_n.26), kind=kLoop, calls=%fused_computation.105 | loop fusion | bytes 6553604 | tf_op jit(solution)/shard_map/jit(dynamic_index_in_dim)/dynamic_slice | solution.py:230
  33.9 5.7 %copy.11 = bf16[640,2,1,1280]{3,0,2,1:T(8,128)(2,1)} copy(bf16[640,2,1,1280]{0,3,2,1:T(8,128)(2,1)} %constant_dynamic-slice_fusion) | data formatting | bytes 6553600 | tf_op jit(solution)/shard_map/jit(dynamic_index_in_dim)/dynamic_slice | solution.py:230
  39.6 11.3 %plan.1 = (s32[2,2,66]{2,1,0:T(2,128)}, s32[2,2]{1,0:T(2,128)}) custom-call(s32[2]{0:T(128)} %pad_add_fusion.place, s32[64]{0:T(128)} %order.3, s32[8]{0:T(128)} %lengths.3, s32[64,64]{1,0:T(8,128)} %reveal.1, s32[1]{0:T(128)S(6)} %copy.91.step), custom_call_target="tpu_custom_call" | custom-call | tf_op jit(solution)/shard_map/plan/pallas_call | solution.py:193
  50.9 2.2 %collective-permute-start.7 = (bf16[512,128]{1,0:T(8,128)(2,1)S(1)}, bf16[512,128]{1,0:T(8,128)(2,1)S(1)}, u32[]{:S(2)}, u32[]{:S(2)}) collective-permute-start(bf16[512,128]{1,0:T(8,128)(2,1)S(1)} %get-tuple-element.70), channel_id=1, source_target_pairs={{84,0},{88,4},{92,8},{64,12},{68,16},{72,20},{76,24},{80,28},{116,... | collective-permute-start | bytes 393224 | tf_op jit(solution)/shard_map/ppermute | solution.py:22
  53.8 2.4 %collective-permute-start.5 = (bf16[512,128]{1,0:T(8,128)(2,1)S(1)}, bf16[512,128]{1,0:T(8,128)(2,1)S(1)}, u32[]{:S(2)}, u32[]{:S(2)}) collective-permute-start(bf16[512,128]{1,0:T(8,128)(2,1)S(1)} %get-tuple-element.70), channel_id=1, source_target_pairs={{16,0},{20,4},{24,8},{28,12},{0,16},{4,20},{8,24},{12,28},{48,32},... | collective-permute-start | bytes 393224 | tf_op jit(solution)/shard_map/ppermute | solution.py:22
  56.8 2.4 %collective-permute-start.16 = (bf16[640,2,1280]{2,0,1:T(8,128)(2,1)}, bf16[640,2,1280]{2,0,1:T(8,128)(2,1)}, u32[]{:S(2)}, u32[]{:S(2)}) collective-permute-start(bf16[640,2,1280]{2,0,1:T(8,128)(2,1)} %bitcast.25), channel_id=1, source_target_pairs={{0,1},{1,0},{2,3},{3,2},{4,5},{5,4},{6,7},{7,6},{8,9},{9,8},{10,11... | collective-permute-start | bytes 9830408 | tf_op jit(solution)/shard_map/ppermute | solution.py:222
  59.9 0.7 constant_dynamic-update-slice_fusion.7
  60.5 2.0 %collective-permute-start.9 = (bf16[2560,128]{1,0:T(8,128)(2,1)}, bf16[2560,128]{1,0:T(8,128)(2,1)S(1)}, u32[]{:S(2)}, u32[]{:S(2)}) collective-permute-start(bf16[2560,128]{1,0:T(8,128)(2,1)} %constant_dynamic-update-slice_fusion.7), channel_id=1, source_target_pairs={{32,0},{36,4},{40,8},{44,12},{48,16},{52,20},{56,24},{60,28},{64,3... | collective-permute-start | bytes 1966088 | tf_op jit(solution)/shard_map/ppermute | solution.py:22
  62.6 5.6 %collective-permute-done.5 = bf16[512,128]{1,0:T(8,128)(2,1)S(1)} collective-permute-done((bf16[512,128]{1,0:T(8,128)(2,1)S(1)}, bf16[512,128]{1,0:T(8,128)(2,1)S(1)}, u32[]{:S(2)}, u32[]{:S(2)}) %collective-permute-start.5) | collective-permute-done | bytes 131104 | tf_op jit(solution)/shard_map/ppermute | solution.py:22
  68.3 2.2 %collective-permute-start.13 = (bf16[1280,128]{1,0:T(8,128)(2,1)S(1)}, bf16[1280,128]{1,0:T(8,128)(2,1)S(1)}, u32[]{:S(2)}, u32[]{:S(2)}) collective-permute-start(bf16[1280,128]{1,0:T(8,128)(2,1)S(1)} %get-tuple-element.60), channel_id=1, source_target_pairs={{28,0},{0,4},{4,8},{8,12},{12,16},{16,20},{20,24},{24,28},{60,32},... | collective-permute-start | bytes 983048 | tf_op jit(solution)/shard_map/ppermute | solution.py:22
  70.5 5.2 %collective-permute-done.4 = bf16[1280,128]{1,0:T(8,128)(2,1)S(1)} collective-permute-done((bf16[1280,128]{1,0:T(8,128)(2,1)S(1)}, bf16[1280,128]{1,0:T(8,128)(2,1)S(1)}, u32[]{:S(2)}, u32[]{:S(2)}) %collective-permute-start.4) | collective-permute-done | bytes 327712 | tf_op jit(solution)/shard_map/ppermute | solution.py:22
  75.7 4.9 %collective-permute-start.14 = (bf16[768,128]{1,0:T(8,128)(2,1)S(1)}, bf16[768,128]{1,0:T(8,128)(2,1)S(1)}, u32[]{:S(2)}, u32[]{:S(2)}) collective-permute-start(bf16[768,128]{1,0:T(8,128)(2,1)S(1)} %pad_maximum_fusion.1), channel_id=1, source_target_pairs={{28,0},{0,4},{4,8},{8,12},{12,16},{16,20},{20,24},{24,28},{60,32},... | collective-permute-start | bytes 589832 | tf_op jit(solution)/shard_map/ppermute | solution.py:22
  80.8 3.0 %collective-permute-done.14 = bf16[768,128]{1,0:T(8,128)(2,1)S(1)} collective-permute-done((bf16[768,128]{1,0:T(8,128)(2,1)S(1)}, bf16[768,128]{1,0:T(8,128)(2,1)S(1)}, u32[]{:S(2)}, u32[]{:S(2)}) %collective-permute-start.14) | collective-permute-done | bytes 196640 | tf_op jit(solution)/shard_map/ppermute | solution.py:22
  83.9 1.9 %collective-permute-start.8 = (bf16[768,128]{1,0:T(8,128)(2,1)S(1)}, bf16[768,128]{1,0:T(8,128)(2,1)S(1)}, u32[]{:S(2)}, u32[]{:S(2)}) collective-permute-start(bf16[768,128]{1,0:T(8,128)(2,1)S(1)} %pad_maximum_fusion), channel_id=1, source_target_pairs={{4,0},{8,4},{12,8},{16,12},{20,16},{24,20},{28,24},{0,28},{36,32},... | collective-permute-start | bytes 589832 | tf_op jit(solution)/shard_map/ppermute | solution.py:22
  85.8 3.8 %collective-permute-done.8 = bf16[768,128]{1,0:T(8,128)(2,1)S(1)} collective-permute-done((bf16[768,128]{1,0:T(8,128)(2,1)S(1)}, bf16[768,128]{1,0:T(8,128)(2,1)S(1)}, u32[]{:S(2)}, u32[]{:S(2)}) %collective-permute-start.8) | collective-permute-done | bytes 196640 | tf_op jit(solution)/shard_map/ppermute | solution.py:22
  89.6 2.1 %collective-permute-start.12 = (bf16[1536,128]{1,0:T(8,128)(2,1)S(1)}, bf16[1536,128]{1,0:T(8,128)(2,1)S(1)}, u32[]{:S(2)}, u32[]{:S(2)}) collective-permute-start(bf16[1536,128]{1,0:T(8,128)(2,1)S(1)} %constant_dynamic-update-slice_fusion.13), channel_id=1, source_target_pairs={{32,0},{36,4},{40,8},{44,12},{48,16},{52,20},{56,24},{60,28},{64,3... | collective-permute-start | bytes 1179656 | tf_op jit(solution)/shard_map/ppermute | solution.py:22
  91.9 5.8 %collective-permute-done.12 = bf16[1536,128]{1,0:T(8,128)(2,1)S(1)} collective-permute-done((bf16[1536,128]{1,0:T(8,128)(2,1)S(1)}, bf16[1536,128]{1,0:T(8,128)(2,1)S(1)}, u32[]{:S(2)}, u32[]{:S(2)}) %collective-permute-start.12) | collective-permute-done | bytes 393248 | tf_op jit(solution)/shard_map/ppermute | solution.py:22
  98.8 7.6 %attention.1 = bf16[256,640]{1,0:T(8,128)(2,1)S(1)} custom-call(s32[2,2,66]{2,1,0:T(2,128)S(1)} %copy-done.5, s32[2,2]{1,0:T(2,128)S(1)} %copy-done.6, s32[2]{0:T(128)S(1)} %copy-done.3, s32[64]{0:T(128)S(1)} %copy-done.1, s32[8]{0:T(128)S(1)} %copy-done.2, bf16[256,640]{1,0:T(8,128)(2,1)S(1)} %copy-done.4, bf16[8192,128]{1,0:T(8,128)(2,1)S(1)} %get-tuple-element.10.k_ref, ...), custom_call_target="tpu_custom_call" | custom-call | flops 1000000000 | bytes 10000000 | tf_op jit(solution)/shard_map/attention/pallas_call | solution.py:204
  106.4 3.5 %collective-permute-start.15 = (bf16[256,640]{1,0:T(8,128)(2,1)S(1)}, bf16[256,640]{1,0:T(8,128)(2,1)S(1)}, u32[]{:S(2)}, u32[]{:S(2)}) collective-permute-start(bf16[256,640]{1,0:T(8,128)(2,1)S(1)} %attention.1), channel_id=1, source_target_pairs={{0,1},{1,0},{2,3},{3,2},{4,5},{5,4},{6,7},{7,6},{8,9},{9,8},{10,11... | collective-permute-start | bytes 983048 | tf_op jit(solution)/shard_map/ppermute | solution.py:222
  109.9 1.3 collective-permute-done.15
  111.2 2.1 %fusion.5 = f32[256,1280]{1,0:T(8,128)S(1)} fusion(bf16[256,640]{1,0:T(8,128)(2,1)S(1)} %collective-permute-done.15, bf16[640,2,1280]{2,0,1:T(8,128)(2,1)} %collective-permute-done.16, s32[]{:T(128)S(6)} %select_n.27), kind=kOutput, calls=%fused_computation.7 | convolution fusion | flops 419430400 | bytes 3276804 | tf_op jit(solution)/shard_map/dot_general | solution.py:238
  113.3 3.0 %fusion.1 = bf16[256,1280]{1,0:T(8,128)(2,1)} fusion(f32[256,1280]{1,0:T(8,128)S(1)} %fusion.5, bf16[256,640]{1,0:T(8,128)(2,1)S(1)} %attention.1, bf16[640,2,2,1280]{0,3,2,1:T(8,128)(2,1)} %bitcast.23, s32[]{:T(128)S(6)} %select_n.28, s32[]{:T(128)S(6)} %select_n.25), kind=kOutput, calls=%fused_computation.3 | convolution fusion | flops 420085760 | bytes 3932168 | tf_op jit(solution)/shard_map/dot_general | solution.py:236
  116.3 1.2 collective-permute-start.17
  117.5 2.1 %fusion.7 = f32[256,1280]{1,0:T(8,128)S(1)} fusion(bf16[256,640]{1,0:T(8,128)(2,1)S(1)} %collective-permute-done.15, bf16[640,2,1280]{2,0,1:T(8,128)(2,1)} %collective-permute-done.16, s32[]{:T(128)S(6)} %select_n.22), kind=kOutput, calls=%fused_computation.9 | convolution fusion | flops 419430400 | bytes 3276804 | tf_op jit(solution)/shard_map/dot_general | solution.py:238
  119.6 12.8 %collective-permute-done.17 = bf16[256,1280]{1,0:T(8,128)(2,1)S(1)} collective-permute-done((bf16[256,1280]{1,0:T(8,128)(2,1)}, bf16[256,1280]{1,0:T(8,128)(2,1)S(1)}, u32[]{:S(2)}, u32[]{:S(2)}) %collective-permute-start.17) | collective-permute-done | bytes 655392 | tf_op jit(solution)/shard_map/ppermute | solution.py:222
  132.4 3.0 %fusion.2 = bf16[256,1280]{1,0:T(8,128)(2,1)} fusion(f32[256,1280]{1,0:T(8,128)S(1)} %fusion.7, bf16[256,640]{1,0:T(8,128)(2,1)S(1)} %attention.1, bf16[640,2,2,1280]{0,3,2,1:T(8,128)(2,1)} %bitcast.24, s32[]{:T(128)S(6)} %select_n.23, s32[]{:T(128)S(6)} %select_n.25, bf16[256,1280]{1,0:T(8,128)(2,1)S(1)} %collective-permute-done.17), kind=kOutput, calls=%fused_computation.4 | convolution fusion | flops 420741120 | bytes 4587528 | tf_op jit(solution)/shard_map/dot_general | solution.py:236
  (84 shorter events, 4.1 us)
Async XLA Ops:
  3.0 47.9 %collective-permute-start = (bf16[512,128]{1,0:T(8,128)(2,1)S(1)}, bf16[512,128]{1,0:T(8,128)(2,1)S(1)}, u32[]{:S(2)}, u32[]{:S(2)}) collective-permute-start(bf16[512,128]{1,0:T(8,128)(2,1)S(1)} %get-tuple-element.70), channel_id=1, source_target_pairs={{8,0},{12,4},{16,8},{20,12},{24,16},{28,20},{0,24},{4,28},{40,32},... | collective-permute-start | bytes 393224 | tf_op jit(solution)/shard_map/ppermute | solution.py:22
  9.9 43.9 %collective-permute-start.1 = (bf16[512,128]{1,0:T(8,128)(2,1)S(1)}, bf16[512,128]{1,0:T(8,128)(2,1)S(1)}, u32[]{:S(2)}, u32[]{:S(2)}) collective-permute-start(bf16[512,128]{1,0:T(8,128)(2,1)S(1)} %get-tuple-element.70), channel_id=1, source_target_pairs={{24,0},{28,4},{0,8},{4,12},{8,16},{12,20},{16,24},{20,28},{56,32},... | collective-permute-start | bytes 393224 | tf_op jit(solution)/shard_map/ppermute | solution.py:22
  9.9 47.0 %collective-permute-start.2 = (bf16[512,128]{1,0:T(8,128)(2,1)S(1)}, bf16[512,128]{1,0:T(8,128)(2,1)S(1)}, u32[]{:S(2)}, u32[]{:S(2)}) collective-permute-start(bf16[512,128]{1,0:T(8,128)(2,1)S(1)} %get-tuple-element.70), channel_id=1, source_target_pairs={{68,0},{72,4},{76,8},{80,12},{84,16},{88,20},{92,24},{64,28},{100,... | collective-permute-start | bytes 393224 | tf_op jit(solution)/shard_map/ppermute | solution.py:22
  15.6 44.2 %collective-permute-start.3 = (bf16[512,128]{1,0:T(8,128)(2,1)S(1)}, bf16[512,128]{1,0:T(8,128)(2,1)S(1)}, u32[]{:S(2)}, u32[]{:S(2)}) collective-permute-start(bf16[512,128]{1,0:T(8,128)(2,1)S(1)} %get-tuple-element.70), channel_id=1, source_target_pairs={{92,0},{64,4},{68,8},{72,12},{76,16},{80,20},{84,24},{88,28},{124,... | collective-permute-start | bytes 393224 | tf_op jit(solution)/shard_map/ppermute | solution.py:22
  15.6 46.9 %collective-permute-start.6 = (bf16[512,128]{1,0:T(8,128)(2,1)S(1)}, bf16[512,128]{1,0:T(8,128)(2,1)S(1)}, u32[]{:S(2)}, u32[]{:S(2)}) collective-permute-start(bf16[512,128]{1,0:T(8,128)(2,1)S(1)} %get-tuple-element.70), channel_id=1, source_target_pairs={{76,0},{80,4},{84,8},{88,12},{92,16},{64,20},{68,24},{72,28},{108,... | collective-permute-start | bytes 393224 | tf_op jit(solution)/shard_map/ppermute | solution.py:22
  50.9 29.7 %copy-start = (bf16[8192,128]{1,0:T(8,128)(2,1)S(1)}, bf16[8192,128]{1,0:T(8,128)(2,1)}, u32[]{:S(2)}) copy-start(bf16[8192,128]{1,0:T(8,128)(2,1)} %get-tuple-element.75) | copy-start | bytes 6291460
  50.9 17.4 %collective-permute-start.7 = (bf16[512,128]{1,0:T(8,128)(2,1)S(1)}, bf16[512,128]{1,0:T(8,128)(2,1)S(1)}, u32[]{:S(2)}, u32[]{:S(2)}) collective-permute-start(bf16[512,128]{1,0:T(8,128)(2,1)S(1)} %get-tuple-element.70), channel_id=1, source_target_pairs={{84,0},{88,4},{92,8},{64,12},{68,16},{72,20},{76,24},{80,28},{116,... | collective-permute-start | bytes 393224 | tf_op jit(solution)/shard_map/ppermute | solution.py:22
  53.8 14.5 %collective-permute-start.5 = (bf16[512,128]{1,0:T(8,128)(2,1)S(1)}, bf16[512,128]{1,0:T(8,128)(2,1)S(1)}, u32[]{:S(2)}, u32[]{:S(2)}) collective-permute-start(bf16[512,128]{1,0:T(8,128)(2,1)S(1)} %get-tuple-element.70), channel_id=1, source_target_pairs={{16,0},{20,4},{24,8},{28,12},{0,16},{4,20},{8,24},{12,28},{48,32},... | collective-permute-start | bytes 393224 | tf_op jit(solution)/shard_map/ppermute | solution.py:22
  56.8 54.4 %collective-permute-start.16 = (bf16[640,2,1280]{2,0,1:T(8,128)(2,1)}, bf16[640,2,1280]{2,0,1:T(8,128)(2,1)}, u32[]{:S(2)}, u32[]{:S(2)}) collective-permute-start(bf16[640,2,1280]{2,0,1:T(8,128)(2,1)} %bitcast.25), channel_id=1, source_target_pairs={{0,1},{1,0},{2,3},{3,2},{4,5},{5,4},{6,7},{7,6},{8,9},{9,8},{10,11... | collective-permute-start | bytes 9830408 | tf_op jit(solution)/shard_map/ppermute | solution.py:222
  60.5 31.2 %collective-permute-start.9 = (bf16[2560,128]{1,0:T(8,128)(2,1)}, bf16[2560,128]{1,0:T(8,128)(2,1)S(1)}, u32[]{:S(2)}, u32[]{:S(2)}) collective-permute-start(bf16[2560,128]{1,0:T(8,128)(2,1)} %constant_dynamic-update-slice_fusion.7), channel_id=1, source_target_pairs={{32,0},{36,4},{40,8},{44,12},{48,16},{52,20},{56,24},{60,28},{64,3... | collective-permute-start | bytes 1966088 | tf_op jit(solution)/shard_map/ppermute | solution.py:22
  62.5 29.3 %collective-permute-start.10 = (bf16[2560,128]{1,0:T(8,128)(2,1)}, bf16[2560,128]{1,0:T(8,128)(2,1)S(1)}, u32[]{:S(2)}, u32[]{:S(2)}) collective-permute-start(bf16[2560,128]{1,0:T(8,128)(2,1)} %constant_dynamic-update-slice_fusion.7), channel_id=1, source_target_pairs={{96,0},{100,4},{104,8},{108,12},{112,16},{116,20},{120,24},{124,28... | collective-permute-start | bytes 1966088 | tf_op jit(solution)/shard_map/ppermute | solution.py:22
  68.2 7.5 %collective-permute-start.4 = (bf16[1280,128]{1,0:T(8,128)(2,1)S(1)}, bf16[1280,128]{1,0:T(8,128)(2,1)S(1)}, u32[]{:S(2)}, u32[]{:S(2)}) collective-permute-start(bf16[1280,128]{1,0:T(8,128)(2,1)S(1)} %get-tuple-element.61), channel_id=1, source_target_pairs={{4,0},{8,4},{12,8},{16,12},{20,16},{24,20},{28,24},{0,28},{36,32},... | collective-permute-start | bytes 983048 | tf_op jit(solution)/shard_map/ppermute | solution.py:22
  68.3 12.3 %collective-permute-start.13 = (bf16[1280,128]{1,0:T(8,128)(2,1)S(1)}, bf16[1280,128]{1,0:T(8,128)(2,1)S(1)}, u32[]{:S(2)}, u32[]{:S(2)}) collective-permute-start(bf16[1280,128]{1,0:T(8,128)(2,1)S(1)} %get-tuple-element.60), channel_id=1, source_target_pairs={{28,0},{0,4},{4,8},{8,12},{12,16},{16,20},{20,24},{24,28},{60,32},... | collective-permute-start | bytes 983048 | tf_op jit(solution)/shard_map/ppermute | solution.py:22
  75.7 8.1 %collective-permute-start.14 = (bf16[768,128]{1,0:T(8,128)(2,1)S(1)}, bf16[768,128]{1,0:T(8,128)(2,1)S(1)}, u32[]{:S(2)}, u32[]{:S(2)}) collective-permute-start(bf16[768,128]{1,0:T(8,128)(2,1)S(1)} %pad_maximum_fusion.1), channel_id=1, source_target_pairs={{28,0},{0,4},{4,8},{8,12},{12,16},{16,20},{20,24},{24,28},{60,32},... | collective-permute-start | bytes 589832 | tf_op jit(solution)/shard_map/ppermute | solution.py:22
  80.6 11.2 %collective-permute-start.11 = (bf16[1536,128]{1,0:T(8,128)(2,1)S(1)}, bf16[1536,128]{1,0:T(8,128)(2,1)S(1)}, u32[]{:S(2)}, u32[]{:S(2)}) collective-permute-start(bf16[1536,128]{1,0:T(8,128)(2,1)S(1)} %constant_dynamic-update-slice_fusion.13), channel_id=1, source_target_pairs={{96,0},{100,4},{104,8},{108,12},{112,16},{116,20},{120,24},{124,28... | collective-permute-start | bytes 1179656 | tf_op jit(solution)/shard_map/ppermute | solution.py:22
  83.9 5.7 %collective-permute-start.8 = (bf16[768,128]{1,0:T(8,128)(2,1)S(1)}, bf16[768,128]{1,0:T(8,128)(2,1)S(1)}, u32[]{:S(2)}, u32[]{:S(2)}) collective-permute-start(bf16[768,128]{1,0:T(8,128)(2,1)S(1)} %pad_maximum_fusion), channel_id=1, source_target_pairs={{4,0},{8,4},{12,8},{16,12},{20,16},{24,20},{28,24},{0,28},{36,32},... | collective-permute-start | bytes 589832 | tf_op jit(solution)/shard_map/ppermute | solution.py:22
  89.6 8.1 %collective-permute-start.12 = (bf16[1536,128]{1,0:T(8,128)(2,1)S(1)}, bf16[1536,128]{1,0:T(8,128)(2,1)S(1)}, u32[]{:S(2)}, u32[]{:S(2)}) collective-permute-start(bf16[1536,128]{1,0:T(8,128)(2,1)S(1)} %constant_dynamic-update-slice_fusion.13), channel_id=1, source_target_pairs={{32,0},{36,4},{40,8},{44,12},{48,16},{52,20},{56,24},{60,28},{64,3... | collective-permute-start | bytes 1179656 | tf_op jit(solution)/shard_map/ppermute | solution.py:22
  97.8 0.7 copy-start.1
  97.8 0.7 copy-start.2
  97.9 0.7 copy-start.3
  97.9 1.0 copy-start.4
  97.9 1.0 copy-start.5
  97.9 1.0 copy-start.6
  106.4 4.8 %collective-permute-start.15 = (bf16[256,640]{1,0:T(8,128)(2,1)S(1)}, bf16[256,640]{1,0:T(8,128)(2,1)S(1)}, u32[]{:S(2)}, u32[]{:S(2)}) collective-permute-start(bf16[256,640]{1,0:T(8,128)(2,1)S(1)} %attention.1), channel_id=1, source_target_pairs={{0,1},{1,0},{2,3},{3,2},{4,5},{5,4},{6,7},{7,6},{8,9},{9,8},{10,11... | collective-permute-start | bytes 983048 | tf_op jit(solution)/shard_map/ppermute | solution.py:222
  116.3 16.2 %collective-permute-start.17 = (bf16[256,1280]{1,0:T(8,128)(2,1)}, bf16[256,1280]{1,0:T(8,128)(2,1)S(1)}, u32[]{:S(2)}, u32[]{:S(2)}) collective-permute-start(bf16[256,1280]{1,0:T(8,128)(2,1)} %fusion.1), channel_id=1, source_target_pairs={{0,2},{2,0},{1,3},{3,1},{4,6},{6,4},{5,7},{7,5},{8,10},{10,8},{9,1... | collective-permute-start | bytes 1966088 | tf_op jit(solution)/shard_map/ppermute | solution.py:222

commit v2 on v1

v2 whole, which is shorter than its diff:
```python
import functools
import math

import jax
import jax.numpy as jnp
import numpy as np
from jax import lax
from jax.experimental import pallas as pl
from jax.experimental.pallas import tpu as pltpu
from jax.sharding import Mesh
from jax.sharding import PartitionSpec as P

HEAD_WIDTH = 128
BLK = 128
NY, NZ, NX, NC = 4, 8, 2, 2
RANKS = NY * NZ
SLOTS = 2 * RANKS
CENTRES = ((0, 0), (0, 4), (2, 2), (2, -2))
STEPS = ((1, 0), (-1, 0), (0, 1), (0, -1))
PICKS = (((3, 0), (4, 0), (1, 0)), ((4, 1), (3, 0), (2, 1)), ((1, 1), (2, 1), (3, 0)), ((2, 0), (1, 1), (4, 0)))


def offsets():
    near = [[(cy + sy, cz + sz) for cy, cz in CENTRES] for sy, sz in ((0, 0), *STEPS)]
    last = [(near[n][m][0] + sy, near[n][m][1] + sz) for (sy, sz), picks in zip(STEPS, PICKS) for n, m in picks]
    every = [(dy % NY, dz % NZ) for dy, dz in [o for group in near for o in group] + last]
    assert sorted(every) == [(dy, dz) for dy in range(NY) for dz in range(NZ)]
    return every


NEAR = 20


MASKED = -1e30
LOWEST = -1e20


def moved(x, dy, dz):
    route = [(((i // NZ + dy) % NY) * NZ + (i % NZ + dz) % NZ, i) for i in range(RANKS)]
    return lax.ppermute(x, ("y", "z"), route)


def first_round(kv):
    return jnp.concatenate([kv] + [moved(kv, *c) for c in CENTRES[1:]])


def second_round(centres):
    return [centres] + [moved(centres, *s) for s in STEPS]


def third_round(near, rows):
    return [
        moved(jnp.concatenate([near[n][m * rows : (m + 1) * rows] for n, m in picks]), *step)
        for step, picks in zip(STEPS, PICKS)
    ]


COUNTS, OWN, ENDS, LISTS = 0, 8, 16, 64
LONGEST = SLOTS + 2


def listed(l, through_mask, which, at):
    return LISTS + ((2 * l + through_mask) * 2 + which) * LONGEST + at


def plan_kernel(place, ranks, order, lengths, reveal, step, plan):
    y, z = place[0], place[1]
    now = step[0]
    own, low, high, one_doc = [], [], [], []
    for t in range(2):
        block = order[2 * (y * NZ + z) + t]
        first, last = block * BLK, block * BLK + BLK - 1
        begin = jnp.int32(0)
        low_t, first_end, last_end = jnp.int32(0), jnp.int32(0), jnp.int32(0)
        for d in range(lengths.shape[0]):
            end = begin + lengths[d]
            plan[ENDS + d] = end
            holds = (begin <= first) & (first < end)
            low_t = jnp.where(holds, begin, low_t)
            first_end = jnp.where(holds, end, first_end)
            last_end = jnp.where((begin <= last) & (last < end), end, last_end)
            begin = end
        plan[OWN + t] = block
        own.append(block)
        low.append(low_t)
        high.append(last_end)
        one_doc.append(first_end == last_end)

    def slot(first_rank, j, n):
        i = lax.shift_right_logical(j, 1)
        e = jnp.bitwise_and(j, 1)
        key_block = order[2 * ranks[first_rank + i] + e]
        row = i * (4 * BLK) + e * BLK
        begin = key_block * BLK
        n = list(n)
        for t in range(2):
            near = (begin < high[t]) & (begin + BLK > low[t]) & (reveal[own[t], key_block] <= now)
            inside = one_doc[t] & (begin >= low[t]) & (begin + BLK <= high[t])
            l = t if first_rank == 0 else 2 + t
            for m, take in enumerate((near & inside, near & jnp.logical_not(inside))):
                at = n[2 * t + m]
                plan[listed(l, m, 0, at)] = row
                plan[listed(l, m, 1, at)] = key_block
                n[2 * t + m] = at + take.astype(jnp.int32)
        return tuple(n)

    for stage, (first_rank, n_ranks) in enumerate(((0, NEAR), (NEAR, RANKS - NEAR))):
        n = lax.fori_loop(0, 2 * n_ranks, functools.partial(slot, first_rank), (jnp.int32(0),) * 4, unroll=2)
        for t in range(2):
            l = 2 * stage + t
            n_whole, n_masked = n[2 * t], n[2 * t + 1]
            odd = jnp.bitwise_and(n_whole, 1)
            kept = n_whole - odd
            for which in range(2):
                plan[listed(l, 1, which, n_masked)] = plan[listed(l, 0, which, kept)]
            n_masked = n_masked + odd
            plan[listed(l, 1, 0, n_masked)] = 0
            plan[listed(l, 1, 1, n_masked)] = SLOTS
            plan[COUNTS + 2 * l] = lax.shift_right_logical(n_whole, 1)
            plan[COUNTS + 2 * l + 1] = lax.shift_right_logical(n_masked + 1, 1)


def attention_kernel(plan, q_ref, kv, *refs, stage, docs):
    heads = q_ref.shape[1] // HEAD_WIDTH
    scale = math.log2(math.e) / math.sqrt(HEAD_WIDTH)
    if stage == 0:
        top_out, total_out, acc_out, scores, top = refs
    else:
        top_in, total_in, acc_in, out_ref, scores, top, total_out, acc_out = refs

    def doc_of(pos):
        return sum((pos >= plan[ENDS + d]).astype(jnp.int32) for d in range(docs))

    for t in range(2):
        l = 2 * stage + t
        block = plan[OWN + t]
        rows = pl.ds(t * BLK, BLK)
        q = jnp.concatenate([q_ref[rows, h * HEAD_WIDTH : (h + 1) * HEAD_WIDTH] for h in range(heads)])
        q_doc = doc_of(block * BLK + lax.broadcasted_iota(jnp.int32, (BLK, BLK), 0))
        top[...] = jnp.full(top.shape, LOWEST, jnp.float32) if stage == 0 else top_in[t]
        total, acc = (total_out.at[t], acc_out.at[t]) if stage == 0 else (total_out, acc_out)
        n_whole, n_masked = plan[COUNTS + 2 * l], plan[COUNTS + 2 * l + 1]

        def two(through_mask, i, start):
            return jnp.concatenate(
                [
                    kv[pl.ds(pl.multiple_of(plan[listed(l, through_mask, 0, 2 * i + e)] + start, BLK), BLK), :]
                    for e in range(2)
                ]
            )

        def dots(through_mask, i):
            return lax.dot_general(
                q, two(through_mask, i, 0), (((1,), (1,)), ((), ())), preferred_element_type=jnp.float32
            )

        def whole_pair(i, carry):
            s = dots(0, i)
            scores[i] = s
            top[...] = jnp.maximum(top[...], jnp.maximum(s[:, :BLK], s[:, BLK:]))
            return carry

        def masked_pair(i, carry):
            s = dots(1, i)
            lane = lax.broadcasted_iota(jnp.int32, (1, BLK), 1)
            for e in range(2):
                k_doc = doc_of(plan[listed(l, 1, 1, 2 * i + e)] * BLK + lane)
                allowed = q_doc == k_doc
                for h in range(heads):
                    part = jnp.where(
                        allowed, s[h * BLK : (h + 1) * BLK, e * BLK : (e + 1) * BLK], MASKED
                    )
                    scores[n_whole + i, pl.ds(h * BLK, BLK), pl.ds(e * BLK, BLK)] = part
                    top[pl.ds(h * BLK, BLK), :] = jnp.maximum(top[pl.ds(h * BLK, BLK), :], part)
            return carry

        lax.fori_loop(0, n_whole, whole_pair, 0)
        lax.fori_loop(0, n_masked, masked_pair, 0)
        best = jnp.broadcast_to(jnp.max(top[...], axis=1, keepdims=True), top.shape)
        if stage == 0:
            top_out[t] = best
            total[...] = jnp.zeros(total.shape, jnp.float32)
            acc[...] = jnp.zeros(acc.shape, jnp.float32)
        else:
            factor = jnp.exp2((top_in[t] - best) * scale)
            total[...] = total_in[t] * factor
            acc[...] = acc_in[t] * factor
        top[...] = best * scale

        def weigh(through_mask, at, i, carry):
            s = scores[at + i]
            m = top[...]
            p0 = jnp.exp2(s[:, :BLK] * scale - m)
            p1 = jnp.exp2(s[:, BLK:] * scale - m)
            total[...] += p0 + p1
            p = jnp.concatenate([p0.astype(jnp.bfloat16), p1.astype(jnp.bfloat16)], axis=1)
            acc[...] += jnp.dot(p, two(through_mask, i, 2 * BLK), preferred_element_type=jnp.float32)
            return carry

        lax.fori_loop(0, n_whole, functools.partial(weigh, 0, 0), 0)
        lax.fori_loop(0, n_masked, functools.partial(weigh, 1, n_whole), 0)
        if stage == 1:
            attended = (acc[...] / jnp.sum(total[...], axis=1, keepdims=True)).astype(jnp.bfloat16)
            for h in range(heads):
                out_ref[rows, h * HEAD_WIDTH : (h + 1) * HEAD_WIDTH] = attended[h * BLK : (h + 1) * BLK]


SMEM = pl.BlockSpec(memory_space=pltpu.SMEM)
VMEM = pl.BlockSpec(memory_space=pltpu.VMEM)


def planned(place, ranks, block_order, doc_lengths, reveal_step, train_step):
    return pl.pallas_call(
        plan_kernel,
        out_shape=jax.ShapeDtypeStruct((listed(4, 0, 0, 0),), jnp.int32),
        in_specs=[SMEM] * 6,
        out_specs=SMEM,
        name="plan",
    )(place, ranks, block_order, doc_lengths, reveal_step, train_step)


def attention(stage, plan, docs, queries, kv, before=()):
    rows = queries.shape[1] // HEAD_WIDTH * BLK
    running = jax.ShapeDtypeStruct((2, rows, HEAD_WIDTH), jnp.float32)
    held = pltpu.VMEM((rows, HEAD_WIDTH), jnp.float32)
    return pl.pallas_call(
        functools.partial(attention_kernel, stage=stage, docs=docs),
        out_shape=(running,) * 3 if stage == 0 else jax.ShapeDtypeStruct(queries.shape, jnp.bfloat16),
        in_specs=[SMEM] + [VMEM] * (2 + len(before)),
        out_specs=(VMEM,) * 3 if stage == 0 else VMEM,
        scratch_shapes=[pltpu.VMEM((17, rows, 2 * BLK), jnp.float32)] + [held] * (1 if stage == 0 else 3),
        compiler_params=pltpu.CompilerParams(vmem_limit_bytes=15 * 2**20),
        cost_estimate=pl.CostEstimate(flops=10**9, bytes_accessed=10**7, transcendentals=3 * 10**6),
        name="attention_%d" % stage,
    )(plan, queries, kv, *before)


def swapped(x, axis):
    return lax.ppermute(x, axis, [(0, 1), (1, 0)])


def from_both_sides(x):
    ring = 2 * NX
    route = [(((i + (1, -1)[c]) % ring) * NC + c, i * NC + c) for i in range(ring) for c in range(NC)]
    return lax.ppermute(x, ("dp", "x", "core"), route)


def project_kernel(at, heads, weight, *refs):
    *before, out_ref = refs
    width = out_ref.shape[1]
    columns = pl.ds(pl.multiple_of(at[0] * width, width), width)
    total = jnp.dot(heads[...], weight[:, columns], preferred_element_type=jnp.float32)
    if before:
        total = before[0][...] + total
    out_ref[...] = total.astype(out_ref.dtype)


def projected(heads, weight, column, width, dtype, before=()):
    rows, depth = heads.shape
    return pl.pallas_call(
        project_kernel,
        out_shape=jax.ShapeDtypeStruct((rows, width), dtype),
        in_specs=[SMEM] + [VMEM] * (2 + len(before)),
        out_specs=VMEM,
        compiler_params=pltpu.CompilerParams(vmem_limit_bytes=12 * 2**20),
        cost_estimate=pl.CostEstimate(
            flops=2 * rows * width * depth, bytes_accessed=2 * width * depth, transcendentals=0
        ),
        name="project",
    )(column.reshape(1).astype(jnp.int32), heads, weight, *before)


def per_device(queries, keys, values, out_weight, block_order, doc_lengths, reveal_step, train_step):
    x, core = lax.axis_index("x"), lax.axis_index("core")
    y, z = lax.axis_index("y"), lax.axis_index("z")
    width = out_weight.shape[1] // (NX * NC)
    place = jnp.stack([y, z]).astype(jnp.int32)
    by_offset = np.array(offsets(), np.int32)
    ranks = ((by_offset[:, 0] + y) % NY * NZ + (by_offset[:, 1] + z) % NZ).astype(jnp.int32)

    kv = jnp.concatenate([keys, values])
    centres = first_round(kv)
    plan = planned(place, ranks, block_order, doc_lengths, reveal_step, train_step)
    weight_1 = swapped(out_weight, "core")
    centres, weight_1, plan = lax.optimization_barrier((centres, weight_1, plan))
    out_weight, plan = lax.optimization_barrier((out_weight, plan))
    beside = from_both_sides(lax.dynamic_slice_in_dim(out_weight, (1 - x) * NC * width, NC * width, 1))
    near = second_round(centres)
    last = third_round(near, kv.shape[0])
    running = attention(0, plan, doc_lengths.shape[0], queries, jnp.concatenate(near))
    beside, last, running = lax.optimization_barrier((beside, last, running))
    beside_1 = swapped(beside, "core")
    heads = attention(1, plan, doc_lengths.shape[0], queries, jnp.concatenate(last), running)
    heads_beside = swapped(heads, "x")
    heads_1 = swapped(heads, "core")
    total = projected(heads, out_weight, x * NC + core, width, jnp.float32)
    total = projected(heads_1, weight_1, x * NC + core, width, jnp.float32, [total])
    heads_beside, total = lax.optimization_barrier((heads_beside, total))
    heads_beside_1 = swapped(heads_beside, "core")
    total = projected(heads_beside, beside, core, width, jnp.float32, [total])
    return projected(heads_beside_1, beside_1, core, width, jnp.bfloat16, [total])


def solution(mesh):
    fine = Mesh(mesh.devices.reshape(mesh.devices.shape[0], NY, NZ, NX, NC), ("dp", "y", "z", "x", "core"))
    rows, heads = ("dp", "y", "z"), ("x", "core")
    in_specs = (
        P(rows, heads),
        P(rows, heads),
        P(rows, heads),
        P(heads, None),
        P("dp"),
        P("dp"),
        P("dp", None),
        P("dp"),
    )
    return jax.shard_map(per_device, mesh=fine, in_specs=in_specs, out_specs=P(rows, heads), check_vma=False)
```

time: 138 us -> 91.1 us (0.66)
  the two profiles are of different devices: /device:TPU:1 before, /device:TPU:71 now
where the time goes in v2:
time: 91.1 us; the launch traced here: 90 us
  waiting for transfers between devices  29.9 us (33%)
  starting transfers between devices  25.9 us (28%)
  Pallas kernels  22.2 us (24%)
  local copies, waits for them, and re-layouts  9.02 us (10%)
  other arithmetic  2.1 us (2%)
    ppermute x11, starting transfers between devices, moved(): return lax.ppermute(x, ('y', 'z'), route)  18.5 us
    ppermute x11, waiting for transfers between devices, moved(): return lax.ppermute(x, ('y', 'z'), route)  16.1 us
    ppermute x1, waiting for transfers between devices, from_both_sides(): return lax.ppermute(x, ('dp', 'x', 'core'), route)  13 us
    pallas_call x4, Pallas kernels, projected(): pl.pallas_call(project_kernel, out_shape=jax.ShapeDtypeStruct((rows, widt...  10.5 us
    pallas_call x2, Pallas kernels, attention(): pl.pallas_call(functools.partial(attention_kernel, stage=stage, docs=docs...  8.02 us
    ppermute x5, starting transfers between devices, swapped(): return lax.ppermute(x, axis, [(0, 1), (1, 0)])  7.12 us
    unnamed x15, local copies, waits for them, and re-layouts  5.86 us
    pallas_call x1, Pallas kernels, planned(): pl.pallas_call(plan_kernel, out_shape=jax.ShapeDtypeStruct((listed(4, 0,...  3.69 us
  transfers between devices with their start and end apart: 17, of which 8 were waited for; matrix products, arithmetic and copies ran while one was open for 6% of the time, Pallas kernels for 21%

profile of v2, /device:TPU:71, one launch (start us, length us, event | category | flops | bytes accessed | tf_op | source)
XLA Modules:
  0.0 90.0 jit_solution(3414280084223292655)
XLA Ops:
  0.0 0.7 collective-permute-start.3
  0.7 0.9 constant_dynamic-update-slice_fusion.1
  1.5 0.9 constant_dynamic-update-slice_fusion
  2.4 6.9 %collective-permute-start.2 = (bf16[512,128]{1,0:T(8,128)(2,1)S(1)}, bf16[512,128]{1,0:T(8,128)(2,1)S(1)}, u32[]{:S(2)}, u32[]{:S(2)}) collective-permute-start(bf16[512,128]{1,0:T(8,128)(2,1)S(1)} %get-tuple-element.51), channel_id=1, source_target_pairs={{88,0},{92,4},{64,8},{68,12},{72,16},{76,20},{80,24},{84,28},{120,... | collective-permute-start | bytes 393224 | tf_op jit(solution)/shard_map/ppermute | solution.py:40
  9.3 3.0 %collective-permute-start = (bf16[512,128]{1,0:T(8,128)(2,1)S(1)}, bf16[512,128]{1,0:T(8,128)(2,1)S(1)}, u32[]{:S(2)}, u32[]{:S(2)}) collective-permute-start(bf16[512,128]{1,0:T(8,128)(2,1)S(1)} %get-tuple-element.51), channel_id=1, source_target_pairs={{16,0},{20,4},{24,8},{28,12},{0,16},{4,20},{8,24},{12,28},{48,32},... | collective-permute-start | bytes 393224 | tf_op jit(solution)/shard_map/ppermute | solution.py:40
  12.4 1.2 %fusion.ranks = s32[32]{0:T(128)} fusion(s32[32]{0:T(128)} %constant.58.clone, s32[32]{0:T(128)} %constant.59.clone, s32[]{:T(128)} %axis_index.48, s32[]{:T(128)} %axis_index.45), kind=kLoop, calls=%fused_computation.23 | loop fusion | flops 832 | bytes 392 | tf_op jit(solution)/shard_map/add | solution.py:279
  14.9 3.7 %plan.1 = s32[1120]{0:T(1024)} custom-call(s32[2]{0:T(128)} %pad_add_fusion.place, s32[32]{0:T(128)} %fusion.ranks, s32[64]{0:T(128)} %order.1, s32[8]{0:T(128)} %lengths.1, s32[64,64]{1,0:T(8,128)} %reveal.1, s32[1]{0:T(128)S(6)} %copy.20.step), custom_call_target="tpu_custom_call" | custom-call | tf_op jit(solution)/shard_map/plan/pallas_call | solution.py:213
  18.6 3.4 %collective-permute-done = bf16[512,128]{1,0:T(8,128)(2,1)S(1)} collective-permute-done((bf16[512,128]{1,0:T(8,128)(2,1)S(1)}, bf16[512,128]{1,0:T(8,128)(2,1)S(1)}, u32[]{:S(2)}, u32[]{:S(2)}) %collective-permute-start) | collective-permute-done | bytes 131104 | tf_op jit(solution)/shard_map/ppermute | solution.py:40
  21.9 3.2 %collective-permute-done.1 = bf16[512,128]{1,0:T(8,128)(2,1)S(1)} collective-permute-done((bf16[512,128]{1,0:T(8,128)(2,1)S(1)}, bf16[512,128]{1,0:T(8,128)(2,1)S(1)}, u32[]{:S(2)}, u32[]{:S(2)}) %collective-permute-start.1) | collective-permute-done | bytes 131104 | tf_op jit(solution)/shard_map/ppermute | solution.py:40
  25.2 0.8 copy-done.3
  26.0 2.1 %constant_dynamic-slice_fusion = bf16[640,2560]{1,0:T(8,128)(2,1)S(1)} fusion(bf16[640,5120]{1,0:T(8,128)(2,1)} %weight, s32[]{:T(128)S(6)} %select_n.16), kind=kLoop, calls=%fused_computation.28 | loop fusion | bytes 6553604 | tf_op jit(solution)/shard_map/dynamic_slice | solution.py:287
  28.8 1.4 %collective-permute-start.9 = (bf16[2048,128]{1,0:T(8,128)(2,1)}, bf16[2048,128]{1,0:T(8,128)(2,1)S(1)}, u32[]{:S(2)}, u32[]{:S(2)}) collective-permute-start(bf16[2048,128]{1,0:T(8,128)(2,1)} %copy-done.3), channel_id=1, source_target_pairs={{96,0},{100,4},{104,8},{108,12},{112,16},{116,20},{120,24},{124,28... | collective-permute-start | bytes 1572872 | tf_op jit(solution)/shard_map/ppermute | solution.py:40
  30.3 1.7 %collective-permute-start.7 = (bf16[2048,128]{1,0:T(8,128)(2,1)}, bf16[2048,128]{1,0:T(8,128)(2,1)S(1)}, u32[]{:S(2)}, u32[]{:S(2)}) collective-permute-start(bf16[2048,128]{1,0:T(8,128)(2,1)} %copy-done.3), channel_id=1, source_target_pairs={{32,0},{36,4},{40,8},{44,12},{48,16},{52,20},{56,24},{60,28},{64,3... | collective-permute-start | bytes 1572872 | tf_op jit(solution)/shard_map/ppermute | solution.py:40
  32.6 1.1 %constant_dynamic-update-slice_fusion.11 = bf16[10240,128]{1,0:T(8,128)(2,1)S(1)} fusion(bf16[2048,128]{1,0:T(8,128)(2,1)} %copy-done.3), kind=kLoop, calls=%fused_computation.16 | loop fusion | bytes 1048576
  33.7 4.7 %collective-permute-done.5 = bf16[2048,128]{1,0:T(8,128)(2,1)S(1)} collective-permute-done((bf16[2048,128]{1,0:T(8,128)(2,1)}, bf16[2048,128]{1,0:T(8,128)(2,1)S(1)}, u32[]{:S(2)}, u32[]{:S(2)}) %collective-permute-start.5) | collective-permute-done | bytes 524320 | tf_op jit(solution)/shard_map/ppermute | solution.py:40
  38.4 3.0 %collective-permute-done.9 = bf16[2048,128]{1,0:T(8,128)(2,1)S(1)} collective-permute-done((bf16[2048,128]{1,0:T(8,128)(2,1)}, bf16[2048,128]{1,0:T(8,128)(2,1)S(1)}, u32[]{:S(2)}, u32[]{:S(2)}) %collective-permute-start.9) | collective-permute-done | bytes 524320 | tf_op jit(solution)/shard_map/ppermute | solution.py:40
  41.5 0.8 collective-permute-done.6
  42.5 1.7 %collective-permute-start.11 = (bf16[1536,128]{1,0:T(8,128)(2,1)S(1)}, bf16[1536,128]{1,0:T(8,128)(2,1)S(1)}, u32[]{:S(2)}, u32[]{:S(2)}) collective-permute-start(bf16[1536,128]{1,0:T(8,128)(2,1)S(1)} %get-tuple-element.47), channel_id=1, source_target_pairs={{4,0},{8,4},{12,8},{16,12},{20,16},{24,20},{28,24},{0,28},{36,32},... | collective-permute-start | bytes 1179656 | tf_op jit(solution)/shard_map/ppermute | solution.py:40
  44.2 0.8 collective-permute-start.12
  45.0 1.9 %collective-permute-start.8 = (bf16[1536,128]{1,0:T(8,128)(2,1)S(1)}, bf16[1536,128]{1,0:T(8,128)(2,1)S(1)}, u32[]{:S(2)}, u32[]{:S(2)}) collective-permute-start(bf16[1536,128]{1,0:T(8,128)(2,1)S(1)} %get-tuple-element.50), channel_id=1, source_target_pairs={{32,0},{36,4},{40,8},{44,12},{48,16},{52,20},{56,24},{60,28},{64,3... | collective-permute-start | bytes 1179656 | tf_op jit(solution)/shard_map/ppermute | solution.py:40
  47.2 4.9 %attention_0.1 = (f32[2,640,128]{2,1,0:T(8,128)S(1)}, f32[2,640,128]{2,1,0:T(8,128)S(1)}, f32[2,640,128]{2,1,0:T(8,128)S(1)}) custom-call(s32[1120]{0:T(1024)S(1)} %copy-done.1, bf16[256,640]{1,0:T(8,128)(2,1)S(1)} %copy-done.2, bf16[10240,128]{1,0:T(8,128)(2,1)S(1)} %constant_dynamic-update-slice_fusion.7.kv), custom_call_target="tpu_custom_call" | custom-call | flops 1000000000 | bytes 10000000 | tf_op jit(solution)/shard_map/attention_0/pallas_call | solution.py:226
  52.1 0.9 %collective-permute-done.10 = bf16[1536,128]{1,0:T(8,128)(2,1)S(1)} collective-permute-done((bf16[1536,128]{1,0:T(8,128)(2,1)S(1)}, bf16[1536,128]{1,0:T(8,128)(2,1)S(1)}, u32[]{:S(2)}, u32[]{:S(2)}) %collective-permute-start.10) | collective-permute-done | bytes 393248 | tf_op jit(solution)/shard_map/ppermute | solution.py:40
  53.1 13.0 %collective-permute-done.4.weight = bf16[640,2560]{1,0:T(8,128)(2,1)S(1)} collective-permute-done((bf16[640,2560]{1,0:T(8,128)(2,1)S(1)}, bf16[640,2560]{1,0:T(8,128)(2,1)S(1)}, u32[]{:S(2)}, u32[]{:S(2)}) %collective-permute-start.4) | collective-permute-done | bytes 3276832 | tf_op jit(solution)/shard_map/ppermute | solution.py:245
  66.0 5.1 %collective-permute-start.16 = (bf16[640,2560]{1,0:T(8,128)(2,1)S(1)}, bf16[640,2560]{1,0:T(8,128)(2,1)}, u32[]{:S(2)}, u32[]{:S(2)}) collective-permute-start(bf16[640,2560]{1,0:T(8,128)(2,1)S(1)} %collective-permute-done.4.weight), channel_id=1, source_target_pairs={{0,1},{1,0},{2,3},{3,2},{4,5},{5,4},{6,7},{7,6},{8,9},{9,8},{10,11... | collective-permute-start | bytes 9830408 | tf_op jit(solution)/shard_map/ppermute | solution.py:239
  71.2 3.1 %attention_1.1.heads = bf16[256,640]{1,0:T(8,128)(2,1)} custom-call(s32[1120]{0:T(1024)S(1)} %copy-done.1, bf16[256,640]{1,0:T(8,128)(2,1)S(1)} %copy-done.2, bf16[6144,128]{1,0:T(8,128)(2,1)S(1)} %pad_maximum_fusion.kv, f32[2,640,128]{2,1,0:T(8,128)S(1)} %get-tuple-element.34.refs_0_, f32[2,640,128]{2,1,0:T(8,128)S(1)} %get-tuple-element.35.refs_1_, ...), custom_call_target="tpu_custom_call" | custom-call | flops 1000000000 | bytes 10000000 | tf_op jit(solution)/shard_map/attention_1/pallas_call | solution.py:226
  74.4 2.9 %copy-done = bf16[640,5120]{1,0:T(8,128)(2,1)S(1)} copy-done((bf16[640,5120]{1,0:T(8,128)(2,1)S(1)}, bf16[640,5120]{1,0:T(8,128)(2,1)}, u32[]{:S(2)}) %copy-start) | copy-done | bytes 6553624
  77.2 1.7 %project.4.refs_0_ = f32[256,1280]{1,0:T(8,128)S(1)} custom-call(s32[1]{0:T(128)} %bitcast.3.at, bf16[256,640]{1,0:T(8,128)(2,1)} %attention_1.1.heads, bf16[640,5120]{1,0:T(8,128)(2,1)S(1)} %copy-done), custom_call_target="tpu_custom_call" | custom-call | flops 419430400 | bytes 1638400 | tf_op jit(solution)/shard_map/project/pallas_call | solution.py:260
  78.9 3.7 %project.5.refs_0_ = f32[256,1280]{1,0:T(8,128)S(1)} custom-call(s32[1]{0:T(128)} %bitcast.3.at, bf16[256,640]{1,0:T(8,128)(2,1)} %collective-permute-done.14.heads, bf16[640,5120]{1,0:T(8,128)(2,1)} %collective-permute-done.3.weight, f32[256,1280]{1,0:T(8,128)S(1)} %project.4.refs_0_), custom_call_target="tpu_custom_call" | custom-call | flops 419430400 | bytes 1638400 | tf_op jit(solution)/shard_map/project/pallas_call | solution.py:260
  82.6 0.9 collective-permute-done.13.heads
  83.5 1.3 %collective-permute-start.15 = (bf16[256,640]{1,0:T(8,128)(2,1)}, bf16[256,640]{1,0:T(8,128)(2,1)S(1)}, u32[]{:S(2)}, u32[]{:S(2)}) collective-permute-start(bf16[256,640]{1,0:T(8,128)(2,1)} %collective-permute-done.13.heads), channel_id=1, source_target_pairs={{0,1},{1,0},{2,3},{3,2},{4,5},{5,4},{6,7},{7,6},{8,9},{9,8},{10,11... | collective-permute-start | bytes 983048 | tf_op jit(solution)/shard_map/ppermute | solution.py:239
  84.8 1.7 %project.6.refs_0_ = f32[256,1280]{1,0:T(8,128)S(1)} custom-call(s32[1]{0:T(128)} %bitcast.at, bf16[256,640]{1,0:T(8,128)(2,1)} %collective-permute-done.13.heads, bf16[640,2560]{1,0:T(8,128)(2,1)S(1)} %collective-permute-done.4.weight, f32[256,1280]{1,0:T(8,128)S(1)} %project.5.refs_0_), custom_call_target="tpu_custom_call" | custom-call | flops 419430400 | bytes 1638400 | tf_op jit(solution)/shard_map/project/pallas_call | solution.py:260
  86.5 3.5 %project.7 = bf16[256,1280]{1,0:T(8,128)(2,1)} custom-call(s32[1]{0:T(128)} %bitcast.at, bf16[256,640]{1,0:T(8,128)(2,1)S(1)} %collective-permute-done.15.heads, bf16[640,2560]{1,0:T(8,128)(2,1)} %collective-permute-done.16.weight, f32[256,1280]{1,0:T(8,128)S(1)} %project.6.refs_0_), custom_call_target="tpu_custom_call" | custom-call | flops 419430400 | bytes 1638400 | tf_op jit(solution)/shard_map/project/pallas_call | solution.py:260
  (36 shorter events, 2.6 us)
Async XLA Ops:
  0.0 25.2 %collective-permute-start.3 = (bf16[640,5120]{1,0:T(8,128)(2,1)}, bf16[640,5120]{1,0:T(8,128)(2,1)}, u32[]{:S(2)}, u32[]{:S(2)}) collective-permute-start(bf16[640,5120]{1,0:T(8,128)(2,1)} %weight), channel_id=1, source_target_pairs={{0,1},{1,0},{2,3},{3,2},{4,5},{5,4},{6,7},{7,6},{8,9},{9,8},{10,11... | collective-permute-start | bytes 19660808 | tf_op jit(solution)/shard_map/ppermute | solution.py:239
  2.4 22.8 %collective-permute-start.2 = (bf16[512,128]{1,0:T(8,128)(2,1)S(1)}, bf16[512,128]{1,0:T(8,128)(2,1)S(1)}, u32[]{:S(2)}, u32[]{:S(2)}) collective-permute-start(bf16[512,128]{1,0:T(8,128)(2,1)S(1)} %get-tuple-element.51), channel_id=1, source_target_pairs={{88,0},{92,4},{64,8},{68,12},{72,16},{76,20},{80,24},{84,28},{120,... | collective-permute-start | bytes 393224 | tf_op jit(solution)/shard_map/ppermute | solution.py:40
  9.3 15.8 %collective-permute-start.1 = (bf16[512,128]{1,0:T(8,128)(2,1)S(1)}, bf16[512,128]{1,0:T(8,128)(2,1)S(1)}, u32[]{:S(2)}, u32[]{:S(2)}) collective-permute-start(bf16[512,128]{1,0:T(8,128)(2,1)S(1)} %get-tuple-element.51), channel_id=1, source_target_pairs={{72,0},{76,4},{80,8},{84,12},{88,16},{92,20},{64,24},{68,28},{104,... | collective-permute-start | bytes 393224 | tf_op jit(solution)/shard_map/ppermute | solution.py:40
  9.3 12.6 %collective-permute-start = (bf16[512,128]{1,0:T(8,128)(2,1)S(1)}, bf16[512,128]{1,0:T(8,128)(2,1)S(1)}, u32[]{:S(2)}, u32[]{:S(2)}) collective-permute-start(bf16[512,128]{1,0:T(8,128)(2,1)S(1)} %get-tuple-element.51), channel_id=1, source_target_pairs={{16,0},{20,4},{24,8},{28,12},{0,16},{4,20},{8,24},{12,28},{48,32},... | collective-permute-start | bytes 393224 | tf_op jit(solution)/shard_map/ppermute | solution.py:40
  25.2 0.8 copy-start.3
  28.1 37.9 %collective-permute-start.4 = (bf16[640,2560]{1,0:T(8,128)(2,1)S(1)}, bf16[640,2560]{1,0:T(8,128)(2,1)S(1)}, u32[]{:S(2)}, u32[]{:S(2)}) collective-permute-start(bf16[640,2560]{1,0:T(8,128)(2,1)S(1)} %constant_dynamic-slice_fusion), channel_id=1, source_target_pairs={{2,0},{131,1},{128,2},{1,3},{130,128},{3,129},{0,130},{129,131},{6... | collective-permute-start | bytes 9830408 | tf_op jit(solution)/shard_map/ppermute | solution.py:245
  28.4 10.0 %collective-permute-start.5 = (bf16[2048,128]{1,0:T(8,128)(2,1)}, bf16[2048,128]{1,0:T(8,128)(2,1)S(1)}, u32[]{:S(2)}, u32[]{:S(2)}) collective-permute-start(bf16[2048,128]{1,0:T(8,128)(2,1)} %copy-done.3), channel_id=1, source_target_pairs={{4,0},{8,4},{12,8},{16,12},{20,16},{24,20},{28,24},{0,28},{36,32},... | collective-permute-start | bytes 1572872 | tf_op jit(solution)/shard_map/ppermute | solution.py:40
  28.8 12.6 %collective-permute-start.9 = (bf16[2048,128]{1,0:T(8,128)(2,1)}, bf16[2048,128]{1,0:T(8,128)(2,1)S(1)}, u32[]{:S(2)}, u32[]{:S(2)}) collective-permute-start(bf16[2048,128]{1,0:T(8,128)(2,1)} %copy-done.3), channel_id=1, source_target_pairs={{96,0},{100,4},{104,8},{108,12},{112,16},{116,20},{120,24},{124,28... | collective-permute-start | bytes 1572872 | tf_op jit(solution)/shard_map/ppermute | solution.py:40
  30.3 11.2 %collective-permute-start.7 = (bf16[2048,128]{1,0:T(8,128)(2,1)}, bf16[2048,128]{1,0:T(8,128)(2,1)S(1)}, u32[]{:S(2)}, u32[]{:S(2)}) collective-permute-start(bf16[2048,128]{1,0:T(8,128)(2,1)} %copy-done.3), channel_id=1, source_target_pairs={{32,0},{36,4},{40,8},{44,12},{48,16},{52,20},{56,24},{60,28},{64,3... | collective-permute-start | bytes 1572872 | tf_op jit(solution)/shard_map/ppermute | solution.py:40
  32.0 10.3 %collective-permute-start.6 = (bf16[2048,128]{1,0:T(8,128)(2,1)}, bf16[2048,128]{1,0:T(8,128)(2,1)S(1)}, u32[]{:S(2)}, u32[]{:S(2)}) collective-permute-start(bf16[2048,128]{1,0:T(8,128)(2,1)} %copy-done.3), channel_id=1, source_target_pairs={{28,0},{0,4},{4,8},{8,12},{12,16},{16,20},{20,24},{24,28},{60,32},... | collective-permute-start | bytes 1572872 | tf_op jit(solution)/shard_map/ppermute | solution.py:40
  42.5 4.7 %copy-start.1 = (s32[1120]{0:T(1024)S(1)}, s32[1120]{0:T(1024)}, u32[]{:S(2)}) copy-start(s32[1120]{0:T(1024)} %plan.1) | copy-start | bytes 13444
  42.5 4.7 %copy-start.2 = (bf16[256,640]{1,0:T(8,128)(2,1)S(1)}, bf16[256,640]{1,0:T(8,128)(2,1)}, u32[]{:S(2)}) copy-start(bf16[256,640]{1,0:T(8,128)(2,1)} %q_ref.3) | copy-start | bytes 983044
  42.5 9.6 %collective-permute-start.11 = (bf16[1536,128]{1,0:T(8,128)(2,1)S(1)}, bf16[1536,128]{1,0:T(8,128)(2,1)S(1)}, u32[]{:S(2)}, u32[]{:S(2)}) collective-permute-start(bf16[1536,128]{1,0:T(8,128)(2,1)S(1)} %get-tuple-element.47), channel_id=1, source_target_pairs={{4,0},{8,4},{12,8},{16,12},{20,16},{24,20},{28,24},{0,28},{36,32},... | collective-permute-start | bytes 1179656 | tf_op jit(solution)/shard_map/ppermute | solution.py:40
  44.2 8.9 %collective-permute-start.10 = (bf16[1536,128]{1,0:T(8,128)(2,1)S(1)}, bf16[1536,128]{1,0:T(8,128)(2,1)S(1)}, u32[]{:S(2)}, u32[]{:S(2)}) collective-permute-start(bf16[1536,128]{1,0:T(8,128)(2,1)S(1)} %get-tuple-element.48), channel_id=1, source_target_pairs={{96,0},{100,4},{104,8},{108,12},{112,16},{116,20},{120,24},{124,28... | collective-permute-start | bytes 1179656 | tf_op jit(solution)/shard_map/ppermute | solution.py:40
  44.2 8.9 %collective-permute-start.12 = (bf16[1536,128]{1,0:T(8,128)(2,1)S(1)}, bf16[1536,128]{1,0:T(8,128)(2,1)S(1)}, u32[]{:S(2)}, u32[]{:S(2)}) collective-permute-start(bf16[1536,128]{1,0:T(8,128)(2,1)S(1)} %get-tuple-element.49), channel_id=1, source_target_pairs={{28,0},{0,4},{4,8},{8,12},{12,16},{16,20},{20,24},{24,28},{60,32},... | collective-permute-start | bytes 1179656 | tf_op jit(solution)/shard_map/ppermute | solution.py:40
  45.0 8.1 %collective-permute-start.8 = (bf16[1536,128]{1,0:T(8,128)(2,1)S(1)}, bf16[1536,128]{1,0:T(8,128)(2,1)S(1)}, u32[]{:S(2)}, u32[]{:S(2)}) collective-permute-start(bf16[1536,128]{1,0:T(8,128)(2,1)S(1)} %get-tuple-element.50), channel_id=1, source_target_pairs={{32,0},{36,4},{40,8},{44,12},{48,16},{52,20},{56,24},{60,28},{64,3... | collective-permute-start | bytes 1179656 | tf_op jit(solution)/shard_map/ppermute | solution.py:40
  66.0 20.5 %collective-permute-start.16 = (bf16[640,2560]{1,0:T(8,128)(2,1)S(1)}, bf16[640,2560]{1,0:T(8,128)(2,1)}, u32[]{:S(2)}, u32[]{:S(2)}) collective-permute-start(bf16[640,2560]{1,0:T(8,128)(2,1)S(1)} %collective-permute-done.4.weight), channel_id=1, source_target_pairs={{0,1},{1,0},{2,3},{3,2},{4,5},{5,4},{6,7},{7,6},{8,9},{9,8},{10,11... | collective-permute-start | bytes 9830408 | tf_op jit(solution)/shard_map/ppermute | solution.py:239
  74.4 4.6 %collective-permute-start.14 = (bf16[256,640]{1,0:T(8,128)(2,1)}, bf16[256,640]{1,0:T(8,128)(2,1)}, u32[]{:S(2)}, u32[]{:S(2)}) collective-permute-start(bf16[256,640]{1,0:T(8,128)(2,1)} %attention_1.1.heads), channel_id=1, source_target_pairs={{0,1},{1,0},{2,3},{3,2},{4,5},{5,4},{6,7},{7,6},{8,9},{9,8},{10,11... | collective-permute-start | bytes 983048 | tf_op jit(solution)/shard_map/ppermute | solution.py:239
  74.4 9.1 %collective-permute-start.13 = (bf16[256,640]{1,0:T(8,128)(2,1)}, bf16[256,640]{1,0:T(8,128)(2,1)}, u32[]{:S(2)}, u32[]{:S(2)}) collective-permute-start(bf16[256,640]{1,0:T(8,128)(2,1)} %attention_1.1.heads), channel_id=1, source_target_pairs={{0,2},{2,0},{1,3},{3,1},{4,6},{6,4},{5,7},{7,5},{8,10},{10,8},{9,1... | collective-permute-start | bytes 983048 | tf_op jit(solution)/shard_map/ppermute | solution.py:239
  74.4 2.9 %copy-start = (bf16[640,5120]{1,0:T(8,128)(2,1)S(1)}, bf16[640,5120]{1,0:T(8,128)(2,1)}, u32[]{:S(2)}) copy-start(bf16[640,5120]{1,0:T(8,128)(2,1)} %weight) | copy-start | bytes 19660804
  83.5 3.0 %collective-permute-start.15 = (bf16[256,640]{1,0:T(8,128)(2,1)}, bf16[256,640]{1,0:T(8,128)(2,1)S(1)}, u32[]{:S(2)}, u32[]{:S(2)}) collective-permute-start(bf16[256,640]{1,0:T(8,128)(2,1)} %collective-permute-done.13.heads), channel_id=1, source_target_pairs={{0,1},{1,0},{2,3},{3,2},{4,5},{5,4},{6,7},{7,6},{8,9},{9,8},{10,11... | collective-permute-start | bytes 983048 | tf_op jit(solution)/shard_map/ppermute | solution.py:239

commit v3 on v2

v3 whole, which is shorter than its diff:
```python
import functools
import math

import jax
import jax.numpy as jnp
from jax import lax
from jax.experimental import pallas as pl
from jax.experimental.pallas import tpu as pltpu
from jax.sharding import Mesh
from jax.sharding import PartitionSpec as P

HEAD_WIDTH = 128
BLK = 128
NY, NZ, NX, NC = 4, 8, 2, 2
RANKS = NY * NZ
SLOTS = 2 * RANKS
CENTRES = ((0, 0), (0, 4), (2, 2), (2, -2))
STEPS = ((1, 0), (-1, 0), (0, 1), (0, -1))
PICKS = (((3, 0), (4, 0), (1, 0)), ((4, 1), (3, 0), (2, 1)), ((1, 1), (2, 1), (3, 0)), ((2, 0), (1, 1), (4, 0)))


def offsets():
    near = [[(cy + sy, cz + sz) for cy, cz in CENTRES] for sy, sz in ((0, 0), *STEPS)]
    last = [(near[n][m][0] + sy, near[n][m][1] + sz) for (sy, sz), picks in zip(STEPS, PICKS) for n, m in picks]
    every = [(dy % NY, dz % NZ) for dy, dz in [o for group in near for o in group] + last]
    assert sorted(every) == [(dy, dz) for dy in range(NY) for dz in range(NZ)]
    return every


NEAR = 20


MASKED = -1e30
LOWEST = -1e20


def moved(x, dy, dz):
    route = [(((i // NZ + dy) % NY) * NZ + (i % NZ + dz) % NZ, i) for i in range(RANKS)]
    return lax.ppermute(x, ("y", "z"), route)


def first_round(kv):
    return jnp.concatenate([kv] + [moved(kv, *c) for c in CENTRES[1:]])


def second_round(centres):
    return [centres] + [moved(centres, *s) for s in STEPS]


def third_round(near, rows):
    return [
        moved(jnp.concatenate([near[n][m * rows : (m + 1) * rows] for n, m in picks]), *step)
        for step, picks in zip(STEPS, PICKS)
    ]


COUNTS, OWN, ENDS, LISTS = 0, 4, 16, 64
CHUNK = 2
LONGEST = SLOTS + 2 * CHUNK


def listed(l, which, at):
    return LISTS + (2 * l + which) * LONGEST + at


def cosets_rank(y, z, dy, dz):
    return jnp.bitwise_and(y + dy, NY - 1) * NZ + jnp.bitwise_and(z + dz, NZ - 1)


def plan_kernel(order, lengths, reveal, step, plan):
    y, z = lax.axis_index("y"), lax.axis_index("z")
    now = step[0]
    own, low, high = [], [], []
    for t in range(2):
        block = order[2 * (y * NZ + z) + t]
        first, last = block * BLK, block * BLK + BLK - 1
        begin = jnp.int32(0)
        low_t, high_t = jnp.int32(0), jnp.int32(0)
        for d in range(lengths.shape[0]):
            end = begin + lengths[d]
            plan[ENDS + d] = end
            low_t = jnp.where((begin <= first) & (first < end), begin, low_t)
            high_t = jnp.where((begin <= last) & (last < end), end, high_t)
            begin = end
        plan[OWN + t] = block
        own.append(block)
        low.append(low_t)
        high.append(high_t)
    n = [jnp.int32(0)] * 4
    for i, (dy, dz) in enumerate(offsets()):
        rank = cosets_rank(y, z, dy, dz)
        stage = int(i >= NEAR)
        for e in range(2):
            key_block = order[2 * rank + e]
            row = (i - stage * NEAR) * (4 * BLK) + e * BLK
            begin = key_block * BLK
            for t in range(2):
                l = 2 * stage + t
                seen = (begin < high[t]) & (begin + BLK > low[t]) & (reveal[own[t], key_block] <= now)
                plan[listed(l, 0, n[l])] = row
                plan[listed(l, 1, n[l])] = key_block
                n[l] = n[l] + seen.astype(jnp.int32)
    for l in range(4):
        for i in range(2 * CHUNK - 1):
            plan[listed(l, 0, n[l] + i)] = 0
            plan[listed(l, 1, n[l] + i)] = SLOTS
        plan[COUNTS + l] = lax.div(n[l] + (CHUNK - 1), CHUNK)


def attention_kernel(plan, q_ref, kv, *refs, stage, docs):
    heads = q_ref.shape[1] // HEAD_WIDTH
    scale = math.log2(math.e) / math.sqrt(HEAD_WIDTH)
    if stage == 0:
        top_ref, total_ref, acc_ref, scores, probs = refs
    else:
        top_in, total_in, acc_in, out_ref, acc_ref, scores, probs = refs
    columns = heads * BLK

    for t in range(2):
        l = 2 * stage + t
        rows = pl.ds(t * BLK, BLK)
        q = jnp.concatenate([q_ref[rows, h * HEAD_WIDTH : (h + 1) * HEAD_WIDTH] for h in range(heads)])
        q = jnp.transpose(q)
        pos = plan[OWN + t] * BLK + lax.broadcasted_iota(jnp.int32, (1, BLK), 1)
        low, high = jnp.zeros((1, BLK), jnp.int32), jnp.zeros((1, BLK), jnp.int32)
        for d in reversed(range(docs)):
            high = jnp.where(pos < plan[ENDS + d], plan[ENDS + d], high)
        for d in range(docs):
            low = jnp.where(pos >= plan[ENDS + d], plan[ENDS + d], low)
        down = lax.broadcasted_iota(jnp.int32, (BLK, BLK), 0)
        if stage == 0:
            acc = acc_ref.at[t]
            acc[...] = jnp.zeros(acc.shape, jnp.float32)
            carry = jnp.full((1, columns), LOWEST, jnp.float32), jnp.zeros((8, columns), jnp.float32)
        else:
            acc = acc_ref
            acc[...] = acc_in[t]
            carry = top_in[t], total_in[t]

        def chunk_rows(i, start):
            return jnp.concatenate(
                [kv[pl.ds(pl.multiple_of(plan[listed(l, 0, CHUNK * i + e)] + start, BLK), BLK), :] for e in range(CHUNK)]
            )

        def score(i):
            s = jnp.dot(chunk_rows(i, 0), q, preferred_element_type=jnp.float32)
            for e in range(CHUNK):
                key = down + plan[listed(l, 1, CHUNK * i + e)] * BLK
                allowed = (key >= low) & (key < high)
                for h in range(heads):
                    part = s[e * BLK : (e + 1) * BLK, h * BLK : (h + 1) * BLK]
                    scores[i % 2, pl.ds(e * BLK, BLK), pl.ds(h * BLK, BLK)] = jnp.where(allowed, part, MASKED)

        def weigh(i, factor):
            acc[...] = acc[...] * factor + lax.dot_general(
                chunk_rows(jnp.maximum(i, 0), 2 * BLK),
                probs[...],
                (((0,), (0,)), ((), ())),
                preferred_element_type=jnp.float32,
            )

        def chunk(i, carry):
            top, total, factor = carry
            s = scores[i % 2]
            weigh(i - 1, factor)
            best = jnp.maximum(top, jnp.max(s, axis=0, keepdims=True))
            p = jnp.exp2(s * scale - best * scale)
            factor = jnp.exp2((top - best) * scale)
            probs[...] = p.astype(jnp.bfloat16)
            score(i + 1)
            return best, total * factor + jnp.sum(p.reshape(-1, 8, columns), axis=0), factor

        n = plan[COUNTS + l]
        score(0)
        probs[...] = jnp.zeros(probs.shape, jnp.bfloat16)
        top, total, factor = lax.fori_loop(0, n, chunk, (*carry, jnp.ones((1, columns), jnp.float32)))
        weigh(n - 1, factor)
        if stage == 0:
            top_ref[t] = top
            total_ref[t] = total
        else:
            out = acc[...] / jnp.sum(total, axis=0, keepdims=True)
            for h in range(heads):
                head = jnp.transpose(out[:, h * BLK : (h + 1) * BLK])
                out_ref[rows, h * HEAD_WIDTH : (h + 1) * HEAD_WIDTH] = head.astype(jnp.bfloat16)


SMEM = pl.BlockSpec(memory_space=pltpu.SMEM)
VMEM = pl.BlockSpec(memory_space=pltpu.VMEM)


def planned(block_order, doc_lengths, reveal_step, train_step):
    return pl.pallas_call(
        plan_kernel,
        out_shape=jax.ShapeDtypeStruct((listed(4, 0, 0),), jnp.int32),
        in_specs=[SMEM] * 4,
        out_specs=SMEM,
        name="plan",
    )(block_order, doc_lengths, reveal_step, train_step)


def attention(stage, plan, docs, queries, kv, before=()):
    columns = queries.shape[1] // HEAD_WIDTH * BLK
    running = [jax.ShapeDtypeStruct((2, r, columns), jnp.float32) for r in (1, 8, HEAD_WIDTH)]
    return pl.pallas_call(
        functools.partial(attention_kernel, stage=stage, docs=docs),
        out_shape=running if stage == 0 else jax.ShapeDtypeStruct(queries.shape, jnp.bfloat16),
        in_specs=[SMEM] + [VMEM] * (2 + len(before)),
        out_specs=[VMEM] * 3 if stage == 0 else VMEM,
        scratch_shapes=([] if stage == 0 else [pltpu.VMEM((HEAD_WIDTH, columns), jnp.float32)])
        + [
            pltpu.VMEM((2, CHUNK * BLK, columns), jnp.float32),
            pltpu.VMEM((CHUNK * BLK, columns), jnp.bfloat16),
        ],
        compiler_params=pltpu.CompilerParams(vmem_limit_bytes=7 * 2**20),
        cost_estimate=pl.CostEstimate(flops=10**9, bytes_accessed=10**7, transcendentals=3 * 10**6),
        name="attention_%d" % stage,
    )(plan, queries, kv, *before)


def swapped(x, axis):
    return lax.ppermute(x, axis, [(0, 1), (1, 0)])


def from_both_sides(x):
    ring = 2 * NX
    route = [(((i + (1, -1)[c]) % ring) * NC + c, i * NC + c) for i in range(ring) for c in range(NC)]
    return lax.ppermute(x, ("dp", "x", "core"), route)


def columns_of(weight, column, width):
    return lax.dynamic_slice_in_dim(weight, column * width, width, 1)


def project_kernel(heads, weight, *refs):
    *before, out_ref = refs
    total = jnp.dot(heads[...], weight[...], preferred_element_type=jnp.float32)
    if before:
        total = before[0][...] + total
    out_ref[...] = total.astype(out_ref.dtype)


def projected(heads, weight, dtype, before=()):
    rows, depth = heads.shape
    width = weight.shape[1]
    return pl.pallas_call(
        project_kernel,
        out_shape=jax.ShapeDtypeStruct((rows, width), dtype),
        in_specs=[VMEM] * (2 + len(before)),
        out_specs=VMEM,
        compiler_params=pltpu.CompilerParams(vmem_limit_bytes=6 * 2**20),
        cost_estimate=pl.CostEstimate(
            flops=2 * rows * width * depth, bytes_accessed=2 * width * depth, transcendentals=0
        ),
        name="project",
    )(heads, weight, *before)


def per_device(queries, keys, values, out_weight, block_order, doc_lengths, reveal_step, train_step):
    x, core = lax.axis_index("x"), lax.axis_index("core")
    width = out_weight.shape[1] // (NX * NC)
    rows = keys.shape[0]
    kv = jnp.where(
        lax.broadcasted_iota(jnp.int32, (2 * rows, 1), 0) < rows,
        jnp.pad(keys, ((0, rows), (0, 0))),
        jnp.pad(values, ((rows, 0), (0, 0))),
    )
    docs = doc_lengths.shape[0]
    beside = from_both_sides(columns_of(out_weight, 1 - x, NC * width))
    centres = first_round(kv)
    plan = planned(block_order, doc_lengths, reveal_step, train_step)
    weight_1 = swapped(out_weight, "core")
    centres, weight_1, plan = lax.optimization_barrier((centres, weight_1, plan))
    near = second_round(centres)
    own_columns = [columns_of(w, x * NC + core, width) for w in (out_weight, weight_1)]
    last = third_round(near, kv.shape[0])
    plan, *own_columns = lax.optimization_barrier((plan, *own_columns))
    running = attention(0, plan, docs, queries, jnp.concatenate(near))
    beside, last, running = lax.optimization_barrier((beside, last, running))
    beside_1 = swapped(beside, "core")
    heads = attention(1, plan, docs, queries, jnp.concatenate(last), running)
    heads_beside = swapped(heads, "x")
    heads_1 = swapped(heads, "core")
    total = projected(heads, own_columns[0], jnp.float32)
    total = projected(heads_1, own_columns[1], jnp.float32, [total])
    beside_columns = [columns_of(w, core, width) for w in (beside, beside_1)]
    heads_beside, total, *beside_columns = lax.optimization_barrier((heads_beside, total, *beside_columns))
    heads_beside_1 = swapped(heads_beside, "core")
    total = projected(heads_beside, beside_columns[0], jnp.float32, [total])
    return projected(heads_beside_1, beside_columns[1], jnp.bfloat16, [total])


def solution(mesh):
    fine = Mesh(mesh.devices.reshape(mesh.devices.shape[0], NY, NZ, NX, NC), ("dp", "y", "z", "x", "core"))
    rows, heads = ("dp", "y", "z"), ("x", "core")
    in_specs = (
        P(rows, heads),
        P(rows, heads),
        P(rows, heads),
        P(heads, None),
        P("dp"),
        P("dp"),
        P("dp", None),
        P("dp"),
    )
    return jax.shard_map(per_device, mesh=fine, in_specs=in_specs, out_specs=P(rows, heads), check_vma=False)
```

time: 91.1 us -> 80.2 us (0.88)
  the two profiles are of different devices: /device:TPU:71 before, /device:TPU:1 now
where the time goes in v3:
time: 80.2 us; the launch traced here: 79.4 us
  starting transfers between devices  29.9 us (37%)
  waiting for transfers between devices  20.9 us (26%)
  Pallas kernels  13.6 us (17%)
  local copies, waits for them, and re-layouts  12.2 us (15%)
  other arithmetic  1.85 us (2%)
  between operations  0.92 us (1%)
    ppermute x11, starting transfers between devices, moved(): return lax.ppermute(x, ('y', 'z'), route)  19.3 us
    ppermute x11, waiting for transfers between devices, moved(): return lax.ppermute(x, ('y', 'z'), route)  17.1 us
    ppermute x5, starting transfers between devices, swapped(): return lax.ppermute(x, axis, [(0, 1), (1, 0)])  10.6 us
    dynamic_slice x5, local copies, waits for them, and re-layouts, columns_of(): return lax.dynamic_slice_in_dim(weight, column * width, width, 1)  10.1 us
    pallas_call x2, Pallas kernels, attention(): pl.pallas_call(functools.partial(attention_kernel, stage=stage, docs=docs...  7.34 us
    ppermute x5, waiting for transfers between devices, swapped(): return lax.ppermute(x, axis, [(0, 1), (1, 0)])  3.79 us
    pallas_call x4, Pallas kernels, projected(): pl.pallas_call(project_kernel, out_shape=jax.ShapeDtypeStruct((rows, widt...  3.62 us
    pallas_call x1, Pallas kernels, planned(): pl.pallas_call(plan_kernel, out_shape=jax.ShapeDtypeStruct((listed(4, 0,...  2.62 us
  transfers between devices with their start and end apart: 17, of which 7 were waited for; matrix products, arithmetic and copies ran while one was open for 16% of the time, Pallas kernels for 15%

profile of v3, /device:TPU:1, one launch (start us, length us, event | category | flops | bytes accessed | tf_op | source)
XLA Modules:
  0.0 79.4 jit_solution(5109337128748732728)
XLA Ops:
  0.0 3.2 %collective-permute-start.3 = (bf16[640,5120]{1,0:T(8,128)(2,1)}, bf16[640,5120]{1,0:T(8,128)(2,1)}, u32[]{:S(2)}, u32[]{:S(2)}) collective-permute-start(bf16[640,5120]{1,0:T(8,128)(2,1)} %param.11), channel_id=1, source_target_pairs={{0,1},{1,0},{2,3},{3,2},{4,5},{5,4},{6,7},{7,6},{8,9},{9,8},{10,11... | collective-permute-start | bytes 19660808 | tf_op jit(solution)/shard_map/ppermute | solution.py:222
  3.2 4.0 %constant_dynamic-slice_fusion.2 = bf16[640,2560]{1,0:T(8,128)(2,1)} fusion(bf16[640,5120]{1,0:T(8,128)(2,1)} %param.11, s32[]{:T(128)S(6)} %select_n.17), kind=kLoop, calls=%fused_computation.15 | loop fusion | bytes 6553604 | tf_op jit(solution)/shard_map/dynamic_slice | solution.py:232
  7.4 6.5 %collective-permute-start = (bf16[512,128]{1,0:T(8,128)(2,1)S(1)}, bf16[512,128]{1,0:T(8,128)(2,1)S(1)}, u32[]{:S(2)}, u32[]{:S(2)}) collective-permute-start(bf16[512,128]{1,0:T(8,128)(2,1)S(1)} %pad_select_fusion), channel_id=1, source_target_pairs={{16,0},{20,4},{24,8},{28,12},{0,16},{4,20},{8,24},{12,28},{48,32},... | collective-permute-start | bytes 393224 | tf_op jit(solution)/shard_map/ppermute | solution.py:39
  13.8 2.0 %collective-permute-start.1 = (bf16[512,128]{1,0:T(8,128)(2,1)S(1)}, bf16[512,128]{1,0:T(8,128)(2,1)S(1)}, u32[]{:S(2)}, u32[]{:S(2)}) collective-permute-start(bf16[512,128]{1,0:T(8,128)(2,1)S(1)} %pad_select_fusion), channel_id=1, source_target_pairs={{72,0},{76,4},{80,8},{84,12},{88,16},{92,20},{64,24},{68,28},{104,... | collective-permute-start | bytes 393224 | tf_op jit(solution)/shard_map/ppermute | solution.py:39
  15.8 2.8 %collective-permute-start.2 = (bf16[512,128]{1,0:T(8,128)(2,1)S(1)}, bf16[512,128]{1,0:T(8,128)(2,1)S(1)}, u32[]{:S(2)}, u32[]{:S(2)}) collective-permute-start(bf16[512,128]{1,0:T(8,128)(2,1)S(1)} %pad_select_fusion), channel_id=1, source_target_pairs={{88,0},{92,4},{64,8},{68,12},{72,16},{76,20},{80,24},{84,28},{120,... | collective-permute-start | bytes 393224 | tf_op jit(solution)/shard_map/ppermute | solution.py:39
  18.6 1.5 %constant_dynamic-slice_fusion.4.weight = bf16[640,1280]{1,0:T(8,128)(2,1)S(1)} fusion(bf16[640,5120]{1,0:T(8,128)(2,1)} %param.11, s32[]{:T(128)S(6)} %select_n.16), kind=kLoop, calls=%fused_computation.17 | loop fusion | bytes 3276804 | tf_op jit(solution)/shard_map/dynamic_slice | solution.py:232
  20.8 2.6 %plan.1 = s32[608]{0:T(1024)} custom-call(s32[64]{0:T(128)} %order.1, s32[8]{0:T(128)} %lengths.1, s32[64,64]{1,0:T(8,128)} %reveal.1, s32[1]{0:T(128)S(6)} %copy.13.step), custom_call_target="tpu_custom_call" | custom-call | tf_op jit(solution)/shard_map/plan/pallas_call | solution.py:193
  23.4 5.9 %collective-permute-done.1 = bf16[512,128]{1,0:T(8,128)(2,1)S(1)} collective-permute-done((bf16[512,128]{1,0:T(8,128)(2,1)S(1)}, bf16[512,128]{1,0:T(8,128)(2,1)S(1)}, u32[]{:S(2)}, u32[]{:S(2)}) %collective-permute-start.1) | collective-permute-done | bytes 131104 | tf_op jit(solution)/shard_map/ppermute | solution.py:39
  29.4 0.7 collective-permute-start.7
  30.1 0.8 %collective-permute-start.9 = (bf16[2048,128]{1,0:T(8,128)(2,1)S(1)}, bf16[2048,128]{1,0:T(8,128)(2,1)S(1)}, u32[]{:S(2)}, u32[]{:S(2)}) collective-permute-start(bf16[2048,128]{1,0:T(8,128)(2,1)S(1)} %pad_maximum_fusion.1), channel_id=1, source_target_pairs={{96,0},{100,4},{104,8},{108,12},{112,16},{116,20},{120,24},{124,28... | collective-permute-start | bytes 1572872 | tf_op jit(solution)/shard_map/ppermute | solution.py:39
  30.9 2.3 %collective-permute-start.5 = (bf16[2048,128]{1,0:T(8,128)(2,1)S(1)}, bf16[2048,128]{1,0:T(8,128)(2,1)S(1)}, u32[]{:S(2)}, u32[]{:S(2)}) collective-permute-start(bf16[2048,128]{1,0:T(8,128)(2,1)S(1)} %pad_maximum_fusion.1), channel_id=1, source_target_pairs={{4,0},{8,4},{12,8},{16,12},{20,16},{24,20},{28,24},{0,28},{36,32},... | collective-permute-start | bytes 1572872 | tf_op jit(solution)/shard_map/ppermute | solution.py:39
  33.3 1.5 %constant_dynamic-slice_fusion.3.weight = bf16[640,1280]{1,0:T(8,128)(2,1)S(1)} fusion(bf16[640,5120]{1,0:T(8,128)(2,1)} %collective-permute-done.3, s32[]{:T(128)S(6)} %select_n.16), kind=kLoop, calls=%fused_computation.16 | loop fusion | bytes 3276804 | tf_op jit(solution)/shard_map/dynamic_slice | solution.py:232
  34.8 8.5 %collective-permute-done.5 = bf16[2048,128]{1,0:T(8,128)(2,1)S(1)} collective-permute-done((bf16[2048,128]{1,0:T(8,128)(2,1)S(1)}, bf16[2048,128]{1,0:T(8,128)(2,1)S(1)}, u32[]{:S(2)}, u32[]{:S(2)}) %collective-permute-start.5) | collective-permute-done | bytes 524320 | tf_op jit(solution)/shard_map/ppermute | solution.py:39
  43.4 0.6 collective-permute-done.9
  44.0 2.0 %collective-permute-done.6 = bf16[2048,128]{1,0:T(8,128)(2,1)S(1)} collective-permute-done((bf16[2048,128]{1,0:T(8,128)(2,1)S(1)}, bf16[2048,128]{1,0:T(8,128)(2,1)S(1)}, u32[]{:S(2)}, u32[]{:S(2)}) %collective-permute-start.6) | collective-permute-done | bytes 524320 | tf_op jit(solution)/shard_map/ppermute | solution.py:39
  46.8 1.1 %collective-permute-start.12 = (bf16[1536,128]{1,0:T(8,128)(2,1)S(1)}, bf16[1536,128]{1,0:T(8,128)(2,1)}, u32[]{:S(2)}, u32[]{:S(2)}) collective-permute-start(bf16[1536,128]{1,0:T(8,128)(2,1)S(1)} %get-tuple-element.55), channel_id=1, source_target_pairs={{28,0},{0,4},{4,8},{8,12},{12,16},{16,20},{20,24},{24,28},{60,32},... | collective-permute-start | bytes 1179656 | tf_op jit(solution)/shard_map/ppermute | solution.py:39
  47.9 2.6 %collective-permute-start.8 = (bf16[1536,128]{1,0:T(8,128)(2,1)S(1)}, bf16[1536,128]{1,0:T(8,128)(2,1)S(1)}, u32[]{:S(2)}, u32[]{:S(2)}) collective-permute-start(bf16[1536,128]{1,0:T(8,128)(2,1)S(1)} %get-tuple-element.56), channel_id=1, source_target_pairs={{32,0},{36,4},{40,8},{44,12},{48,16},{52,20},{56,24},{60,28},{64,3... | collective-permute-start | bytes 1179656 | tf_op jit(solution)/shard_map/ppermute | solution.py:39
  50.8 4.0 %attention_0.1 = (f32[2,1,640]{2,1,0:T(1,128)S(1)}, f32[2,8,640]{2,1,0:T(8,128)S(1)}, f32[2,128,640]{2,1,0:T(8,128)S(1)}) custom-call(s32[608]{0:T(1024)S(1)} %copy-done, bf16[256,640]{1,0:T(8,128)(2,1)S(1)} %copy-done.1, bf16[10240,128]{1,0:T(8,128)(2,1)S(1)} %constant_dynamic-update-slice_fusion.kv), custom_call_target="tpu_custom_call" | custom-call | flops 1000000000 | bytes 10000000 | tf_op jit(solution)/shard_map/attention_0/pallas_call | solution.py:205
  54.8 0.8 %copy-done.3 = f32[2,128,640]{2,1,0:T(8,128)} copy-done((f32[2,128,640]{2,1,0:T(8,128)}, f32[2,128,640]{2,1,0:T(8,128)S(1)}, u32[]{:S(2)}) %copy-start.3) | copy-done | bytes 655384
  55.7 0.8 copy-done.5
  56.4 4.1 %collective-permute-start.15 = (bf16[640,2560]{1,0:T(8,128)(2,1)}, bf16[640,2560]{1,0:T(8,128)(2,1)}, u32[]{:S(2)}, u32[]{:S(2)}) collective-permute-start(bf16[640,2560]{1,0:T(8,128)(2,1)} %collective-permute-done.4), channel_id=1, source_target_pairs={{0,1},{1,0},{2,3},{3,2},{4,5},{5,4},{6,7},{7,6},{8,9},{9,8},{10,11... | collective-permute-start | bytes 9830408 | tf_op jit(solution)/shard_map/ppermute | solution.py:222
  60.5 1.5 %pad_maximum_fusion.kv = bf16[6144,128]{1,0:T(8,128)(2,1)S(1)} fusion(bf16[1536,128]{1,0:T(8,128)(2,1)} %collective-permute-done.12, bf16[1536,128]{1,0:T(8,128)(2,1)} %collective-permute-done.11, bf16[1536,128]{1,0:T(8,128)(2,1)} %collective-permute-done.10, bf16[1536,128]{1,0:T(8,128)(2,1)} %copy-done.5), kind=kLoop, calls=%fused_computation | loop fusion | flops 6291456 | bytes 3145728 | tf_op jit(solution)/shard_map/concatenate | solution.py:281
  62.2 3.4 %attention_1.1.heads = bf16[256,640]{1,0:T(8,128)(2,1)S(1)} custom-call(s32[608]{0:T(1024)S(1)} %copy-done, bf16[256,640]{1,0:T(8,128)(2,1)S(1)} %copy-done.2, bf16[6144,128]{1,0:T(8,128)(2,1)S(1)} %pad_maximum_fusion.kv, f32[2,1,640]{2,1,0:T(1,128)S(1)} %get-tuple-element.37.refs_0_, f32[2,8,640]{2,1,0:T(8,128)S(1)} %get-tuple-element.38.refs_1_, ...), custom_call_target="tpu_custom_call" | custom-call | flops 1000000000 | bytes 10000000 | tf_op jit(solution)/shard_map/attention_1/pallas_call | solution.py:205
  65.7 2.2 %collective-permute-start.13 = (bf16[256,640]{1,0:T(8,128)(2,1)S(1)}, bf16[256,640]{1,0:T(8,128)(2,1)S(1)}, u32[]{:S(2)}, u32[]{:S(2)}) collective-permute-start(bf16[256,640]{1,0:T(8,128)(2,1)S(1)} %attention_1.1.heads), channel_id=1, source_target_pairs={{0,2},{2,0},{1,3},{3,1},{4,6},{6,4},{5,7},{7,5},{8,10},{10,8},{9,1... | collective-permute-start | bytes 983048 | tf_op jit(solution)/shard_map/ppermute | solution.py:222
  67.9 0.7 project.4.refs_0_
  68.6 1.5 %constant_dynamic-slice_fusion.1.weight = bf16[640,1280]{1,0:T(8,128)(2,1)S(1)} fusion(bf16[640,2560]{1,0:T(8,128)(2,1)} %collective-permute-done.4, s32[]{:T(128)S(6)} %select_n.18), kind=kLoop, calls=%fused_computation.14 | loop fusion | bytes 3276804 | tf_op jit(solution)/shard_map/dynamic_slice | solution.py:232
  70.2 0.7 project.5.refs_0_
  70.9 1.5 %constant_dynamic-slice_fusion.weight = bf16[640,1280]{1,0:T(8,128)(2,1)S(1)} fusion(bf16[640,2560]{1,0:T(8,128)(2,1)} %collective-permute-done.15, s32[]{:T(128)S(6)} %select_n.18), kind=kLoop, calls=%fused_computation.13 | loop fusion | bytes 3276804 | tf_op jit(solution)/shard_map/dynamic_slice | solution.py:232
  72.4 3.2 %collective-permute-done.13.heads = bf16[256,640]{1,0:T(8,128)(2,1)S(1)} collective-permute-done((bf16[256,640]{1,0:T(8,128)(2,1)S(1)}, bf16[256,640]{1,0:T(8,128)(2,1)S(1)}, u32[]{:S(2)}, u32[]{:S(2)}) %collective-permute-start.13) | collective-permute-done | bytes 327712 | tf_op jit(solution)/shard_map/ppermute | solution.py:222
  75.6 0.9 %collective-permute-start.16 = (bf16[256,640]{1,0:T(8,128)(2,1)S(1)}, bf16[256,640]{1,0:T(8,128)(2,1)S(1)}, u32[]{:S(2)}, u32[]{:S(2)}) collective-permute-start(bf16[256,640]{1,0:T(8,128)(2,1)S(1)} %collective-permute-done.13.heads), channel_id=1, source_target_pairs={{0,1},{1,0},{2,3},{3,2},{4,5},{5,4},{6,7},{7,6},{8,9},{9,8},{10,11... | collective-permute-start | bytes 983048 | tf_op jit(solution)/shard_map/ppermute | solution.py:222
  76.6 0.7 project.6.refs_0_
  77.8 1.5 %project.7 = bf16[256,1280]{1,0:T(8,128)(2,1)} custom-call(bf16[256,640]{1,0:T(8,128)(2,1)S(1)} %collective-permute-done.16.heads, bf16[640,1280]{1,0:T(8,128)(2,1)S(1)} %constant_dynamic-slice_fusion.weight, f32[256,1280]{1,0:T(8,128)S(1)} %project.6.refs_0_), custom_call_target="tpu_custom_call" | custom-call | flops 419430400 | bytes 1638400 | tf_op jit(solution)/shard_map/project/pallas_call | solution.py:246
  (44 shorter events, 2.1 us)
Async XLA Ops:
  0.0 29.4 %collective-permute-start.3 = (bf16[640,5120]{1,0:T(8,128)(2,1)}, bf16[640,5120]{1,0:T(8,128)(2,1)}, u32[]{:S(2)}, u32[]{:S(2)}) collective-permute-start(bf16[640,5120]{1,0:T(8,128)(2,1)} %param.11), channel_id=1, source_target_pairs={{0,1},{1,0},{2,3},{3,2},{4,5},{5,4},{6,7},{7,6},{8,9},{9,8},{10,11... | collective-permute-start | bytes 19660808 | tf_op jit(solution)/shard_map/ppermute | solution.py:222
  3.2 4.0 %copy-start.6 = (bf16[256,128]{1,0:T(8,128)(2,1)S(1)}, bf16[256,128]{1,0:T(8,128)(2,1)}, u32[]{:S(2)}) copy-start(bf16[256,128]{1,0:T(8,128)(2,1)} %param.10) | copy-start | bytes 196612
  3.2 4.0 %copy-start.7 = (bf16[256,128]{1,0:T(8,128)(2,1)S(1)}, bf16[256,128]{1,0:T(8,128)(2,1)}, u32[]{:S(2)}) copy-start(bf16[256,128]{1,0:T(8,128)(2,1)} %param.9) | copy-start | bytes 196612
  7.2 48.4 %collective-permute-start.4 = (bf16[640,2560]{1,0:T(8,128)(2,1)}, bf16[640,2560]{1,0:T(8,128)(2,1)}, u32[]{:S(2)}, u32[]{:S(2)}) collective-permute-start(bf16[640,2560]{1,0:T(8,128)(2,1)} %constant_dynamic-slice_fusion.2), channel_id=1, source_target_pairs={{2,0},{131,1},{128,2},{1,3},{130,128},{3,129},{0,130},{129,131},{6... | collective-permute-start | bytes 9830408 | tf_op jit(solution)/shard_map/ppermute | solution.py:228
  7.4 16.0 %collective-permute-start = (bf16[512,128]{1,0:T(8,128)(2,1)S(1)}, bf16[512,128]{1,0:T(8,128)(2,1)S(1)}, u32[]{:S(2)}, u32[]{:S(2)}) collective-permute-start(bf16[512,128]{1,0:T(8,128)(2,1)S(1)} %pad_select_fusion), channel_id=1, source_target_pairs={{16,0},{20,4},{24,8},{28,12},{0,16},{4,20},{8,24},{12,28},{48,32},... | collective-permute-start | bytes 393224 | tf_op jit(solution)/shard_map/ppermute | solution.py:39
  13.8 15.5 %collective-permute-start.1 = (bf16[512,128]{1,0:T(8,128)(2,1)S(1)}, bf16[512,128]{1,0:T(8,128)(2,1)S(1)}, u32[]{:S(2)}, u32[]{:S(2)}) collective-permute-start(bf16[512,128]{1,0:T(8,128)(2,1)S(1)} %pad_select_fusion), channel_id=1, source_target_pairs={{72,0},{76,4},{80,8},{84,12},{88,16},{92,20},{64,24},{68,28},{104,... | collective-permute-start | bytes 393224 | tf_op jit(solution)/shard_map/ppermute | solution.py:39
  15.8 13.5 %collective-permute-start.2 = (bf16[512,128]{1,0:T(8,128)(2,1)S(1)}, bf16[512,128]{1,0:T(8,128)(2,1)S(1)}, u32[]{:S(2)}, u32[]{:S(2)}) collective-permute-start(bf16[512,128]{1,0:T(8,128)(2,1)S(1)} %pad_select_fusion), channel_id=1, source_target_pairs={{88,0},{92,4},{64,8},{68,12},{72,16},{76,20},{80,24},{84,28},{120,... | collective-permute-start | bytes 393224 | tf_op jit(solution)/shard_map/ppermute | solution.py:39
  29.4 14.6 %collective-permute-start.7 = (bf16[2048,128]{1,0:T(8,128)(2,1)S(1)}, bf16[2048,128]{1,0:T(8,128)(2,1)S(1)}, u32[]{:S(2)}, u32[]{:S(2)}) collective-permute-start(bf16[2048,128]{1,0:T(8,128)(2,1)S(1)} %pad_maximum_fusion.1), channel_id=1, source_target_pairs={{32,0},{36,4},{40,8},{44,12},{48,16},{52,20},{56,24},{60,28},{64,3... | collective-permute-start | bytes 1572872 | tf_op jit(solution)/shard_map/ppermute | solution.py:39
  30.1 13.8 %collective-permute-start.9 = (bf16[2048,128]{1,0:T(8,128)(2,1)S(1)}, bf16[2048,128]{1,0:T(8,128)(2,1)S(1)}, u32[]{:S(2)}, u32[]{:S(2)}) collective-permute-start(bf16[2048,128]{1,0:T(8,128)(2,1)S(1)} %pad_maximum_fusion.1), channel_id=1, source_target_pairs={{96,0},{100,4},{104,8},{108,12},{112,16},{116,20},{120,24},{124,28... | collective-permute-start | bytes 1572872 | tf_op jit(solution)/shard_map/ppermute | solution.py:39
  30.9 12.4 %collective-permute-start.5 = (bf16[2048,128]{1,0:T(8,128)(2,1)S(1)}, bf16[2048,128]{1,0:T(8,128)(2,1)S(1)}, u32[]{:S(2)}, u32[]{:S(2)}) collective-permute-start(bf16[2048,128]{1,0:T(8,128)(2,1)S(1)} %pad_maximum_fusion.1), channel_id=1, source_target_pairs={{4,0},{8,4},{12,8},{16,12},{20,16},{24,20},{28,24},{0,28},{36,32},... | collective-permute-start | bytes 1572872 | tf_op jit(solution)/shard_map/ppermute | solution.py:39
  33.3 12.8 %collective-permute-start.6 = (bf16[2048,128]{1,0:T(8,128)(2,1)S(1)}, bf16[2048,128]{1,0:T(8,128)(2,1)S(1)}, u32[]{:S(2)}, u32[]{:S(2)}) collective-permute-start(bf16[2048,128]{1,0:T(8,128)(2,1)S(1)} %pad_maximum_fusion.1), channel_id=1, source_target_pairs={{28,0},{0,4},{4,8},{8,12},{12,16},{16,20},{20,24},{24,28},{60,32},... | collective-permute-start | bytes 1572872 | tf_op jit(solution)/shard_map/ppermute | solution.py:39
  46.2 4.6 %copy-start = (s32[608]{0:T(1024)S(1)}, s32[608]{0:T(1024)}, u32[]{:S(2)}) copy-start(s32[608]{0:T(1024)} %plan.1) | copy-start | bytes 7300
  46.2 4.6 %copy-start.1 = (bf16[256,640]{1,0:T(8,128)(2,1)S(1)}, bf16[256,640]{1,0:T(8,128)(2,1)}, u32[]{:S(2)}) copy-start(bf16[256,640]{1,0:T(8,128)(2,1)} %q_ref.3) | copy-start | bytes 983044
  46.2 9.4 %collective-permute-start.10 = (bf16[1536,128]{1,0:T(8,128)(2,1)S(1)}, bf16[1536,128]{1,0:T(8,128)(2,1)}, u32[]{:S(2)}, u32[]{:S(2)}) collective-permute-start(bf16[1536,128]{1,0:T(8,128)(2,1)S(1)} %get-tuple-element.54), channel_id=1, source_target_pairs={{96,0},{100,4},{104,8},{108,12},{112,16},{116,20},{120,24},{124,28... | collective-permute-start | bytes 1179656 | tf_op jit(solution)/shard_map/ppermute | solution.py:39
  46.3 9.3 %collective-permute-start.11 = (bf16[1536,128]{1,0:T(8,128)(2,1)S(1)}, bf16[1536,128]{1,0:T(8,128)(2,1)}, u32[]{:S(2)}, u32[]{:S(2)}) collective-permute-start(bf16[1536,128]{1,0:T(8,128)(2,1)S(1)} %get-tuple-element.53), channel_id=1, source_target_pairs={{4,0},{8,4},{12,8},{16,12},{20,16},{24,20},{28,24},{0,28},{36,32},... | collective-permute-start | bytes 1179656 | tf_op jit(solution)/shard_map/ppermute | solution.py:39
  46.8 8.9 %collective-permute-start.12 = (bf16[1536,128]{1,0:T(8,128)(2,1)S(1)}, bf16[1536,128]{1,0:T(8,128)(2,1)}, u32[]{:S(2)}, u32[]{:S(2)}) collective-permute-start(bf16[1536,128]{1,0:T(8,128)(2,1)S(1)} %get-tuple-element.55), channel_id=1, source_target_pairs={{28,0},{0,4},{4,8},{8,12},{12,16},{16,20},{20,24},{24,28},{60,32},... | collective-permute-start | bytes 1179656 | tf_op jit(solution)/shard_map/ppermute | solution.py:39
  47.9 7.8 %collective-permute-start.8 = (bf16[1536,128]{1,0:T(8,128)(2,1)S(1)}, bf16[1536,128]{1,0:T(8,128)(2,1)S(1)}, u32[]{:S(2)}, u32[]{:S(2)}) collective-permute-start(bf16[1536,128]{1,0:T(8,128)(2,1)S(1)} %get-tuple-element.56), channel_id=1, source_target_pairs={{32,0},{36,4},{40,8},{44,12},{48,16},{52,20},{56,24},{60,28},{64,3... | collective-permute-start | bytes 1179656 | tf_op jit(solution)/shard_map/ppermute | solution.py:39
  54.7 0.8 %copy-start.3 = (f32[2,128,640]{2,1,0:T(8,128)}, f32[2,128,640]{2,1,0:T(8,128)S(1)}, u32[]{:S(2)}) copy-start(f32[2,128,640]{2,1,0:T(8,128)S(1)} %get-tuple-element.39.refs_2_) | copy-start | bytes 1966084
  55.7 0.8 copy-start.5
  56.4 14.4 %collective-permute-start.15 = (bf16[640,2560]{1,0:T(8,128)(2,1)}, bf16[640,2560]{1,0:T(8,128)(2,1)}, u32[]{:S(2)}, u32[]{:S(2)}) collective-permute-start(bf16[640,2560]{1,0:T(8,128)(2,1)} %collective-permute-done.4), channel_id=1, source_target_pairs={{0,1},{1,0},{2,3},{3,2},{4,5},{5,4},{6,7},{7,6},{8,9},{9,8},{10,11... | collective-permute-start | bytes 9830408 | tf_op jit(solution)/shard_map/ppermute | solution.py:222
  60.5 1.5 %copy-start.2 = (bf16[256,640]{1,0:T(8,128)(2,1)S(1)}, bf16[256,640]{1,0:T(8,128)(2,1)}, u32[]{:S(2)}) copy-start(bf16[256,640]{1,0:T(8,128)(2,1)} %q_ref.3) | copy-start | bytes 983044
  60.5 1.7 %copy-start.4 = (f32[2,128,640]{2,1,0:T(8,128)S(1)}, f32[2,128,640]{2,1,0:T(8,128)}, u32[]{:S(2)}) copy-start(f32[2,128,640]{2,1,0:T(8,128)} %copy-done.3) | copy-start | bytes 1966084
  65.6 4.6 %collective-permute-start.14 = (bf16[256,640]{1,0:T(8,128)(2,1)S(1)}, bf16[256,640]{1,0:T(8,128)(2,1)S(1)}, u32[]{:S(2)}, u32[]{:S(2)}) collective-permute-start(bf16[256,640]{1,0:T(8,128)(2,1)S(1)} %attention_1.1.heads), channel_id=1, source_target_pairs={{0,1},{1,0},{2,3},{3,2},{4,5},{5,4},{6,7},{7,6},{8,9},{9,8},{10,11... | collective-permute-start | bytes 983048 | tf_op jit(solution)/shard_map/ppermute | solution.py:222
  65.7 10.0 %collective-permute-start.13 = (bf16[256,640]{1,0:T(8,128)(2,1)S(1)}, bf16[256,640]{1,0:T(8,128)(2,1)S(1)}, u32[]{:S(2)}, u32[]{:S(2)}) collective-permute-start(bf16[256,640]{1,0:T(8,128)(2,1)S(1)} %attention_1.1.heads), channel_id=1, source_target_pairs={{0,2},{2,0},{1,3},{3,1},{4,6},{6,4},{5,7},{7,5},{8,10},{10,8},{9,1... | collective-permute-start | bytes 983048 | tf_op jit(solution)/shard_map/ppermute | solution.py:222
  75.6 2.2 %collective-permute-start.16 = (bf16[256,640]{1,0:T(8,128)(2,1)S(1)}, bf16[256,640]{1,0:T(8,128)(2,1)S(1)}, u32[]{:S(2)}, u32[]{:S(2)}) collective-permute-start(bf16[256,640]{1,0:T(8,128)(2,1)S(1)} %collective-permute-done.13.heads), channel_id=1, source_target_pairs={{0,1},{1,0},{2,3},{3,2},{4,5},{5,4},{6,7},{7,6},{8,9},{9,8},{10,11... | collective-permute-start | bytes 983048 | tf_op jit(solution)/shard_map/ppermute | solution.py:222

commit v4 on v3

--- a/solution.py
+++ b/solution.py
@@ -270,15 +270,15 @@
     centres = first_round(kv)
     plan = planned(block_order, doc_lengths, reveal_step, train_step)
     weight_1 = swapped(out_weight, "core")
-    centres, weight_1, plan = lax.optimization_barrier((centres, weight_1, plan))
+    centres, weight_1, plan, late_weight = lax.optimization_barrier((centres, weight_1, plan, out_weight))
     near = second_round(centres)
-    own_columns = [columns_of(w, x * NC + core, width) for w in (out_weight, weight_1)]
+    own_columns = [columns_of(w, x * NC + core, width) for w in (late_weight, weight_1)]
     last = third_round(near, kv.shape[0])
     plan, *own_columns = lax.optimization_barrier((plan, *own_columns))
     running = attention(0, plan, docs, queries, jnp.concatenate(near))
-    beside, last, running = lax.optimization_barrier((beside, last, running))
+    heads = attention(1, plan, docs, queries, jnp.concatenate(last), running)
+    beside, after = lax.optimization_barrier((beside, heads))
     beside_1 = swapped(beside, "core")
-    heads = attention(1, plan, docs, queries, jnp.concatenate(last), running)
     heads_beside = swapped(heads, "x")
     heads_1 = swapped(heads, "core")
     total = projected(heads, own_columns[0], jnp.float32)

time: 80.2 us -> 74.4 us (0.928)
  starting transfers between devices: 29.9 us -> 28.1 us
  Pallas kernels: 13.6 us -> 12.5 us
  local copies, waits for them, and re-layouts: 12.2 us -> 11.3 us
    ppermute x11, starting transfers between devices: 19.3 us -> 17.2 us  [moved(): return lax.ppermute(x, ('y', 'z'), route)]
    concatenate x1, other arithmetic: 1.54 us -> 0.1 us  [per_device(): heads = attention(1, plan, docs, queries, jnp.concatenate(last), running)]
    ppermute x1, starting transfers between devices: 0.01 us -> 1.21 us  [from_both_sides(): return lax.ppermute(x, ('dp', 'x', 'core'), route)]
    pallas_call x2, Pallas kernels: 7.34 us -> 6.22 us  [attention(): pl.pallas_call(functools.partial(attention_kernel, stage=stage, docs=docs...]
    ppermute x5, waiting for transfers between devices: 3.79 us -> 2.82 us  [swapped(): return lax.ppermute(x, axis, [(0, 1), (1, 0)])]
    dynamic_slice x5 -> x4, local copies, waits for them, and re-layouts: 10.1 us -> 9.15 us  [columns_of(): return lax.dynamic_slice_in_dim(weight, column * width, width, 1)]
    ppermute x1, waiting for transfers between devices: 0.01 us -> 0.93 us  [from_both_sides(): return lax.ppermute(x, ('dp', 'x', 'core'), route)]
    ppermute x5, starting transfers between devices: 10.6 us -> 9.68 us  [swapped(): return lax.ppermute(x, axis, [(0, 1), (1, 0)])]
  transfers between devices with their start and end apart: 17 -> 17, of which waited for: 7 -> 10; matrix products, arithmetic and copies ran while one was open for 16% -> 15% of each run, Pallas kernels for 15% -> 15%
where the time goes in v4:
time: 74.4 us
  starting transfers between devices  28.1 us (38%)
  waiting for transfers between devices  20.4 us (27%)
  Pallas kernels  12.5 us (17%)
  local copies, waits for them, and re-layouts  11.3 us (15%)
  other arithmetic  1.3 us (2%)
  between operations  0.88 us (1%)
    ppermute x11, starting transfers between devices, moved(): return lax.ppermute(x, ('y', 'z'), route)  17.2 us
    ppermute x11, waiting for transfers between devices, moved(): return lax.ppermute(x, ('y', 'z'), route)  16.6 us
    ppermute x5, starting transfers between devices, swapped(): return lax.ppermute(x, axis, [(0, 1), (1, 0)])  9.68 us
    dynamic_slice x4, local copies, waits for them, and re-layouts, columns_of(): return lax.dynamic_slice_in_dim(weight, column * width, width, 1)  9.15 us
    pallas_call x2, Pallas kernels, attention(): pl.pallas_call(functools.partial(attention_kernel, stage=stage, docs=docs...  6.22 us
    pallas_call x4, Pallas kernels, projected(): pl.pallas_call(project_kernel, out_shape=jax.ShapeDtypeStruct((rows, widt...  3.61 us
    ppermute x5, waiting for transfers between devices, swapped(): return lax.ppermute(x, axis, [(0, 1), (1, 0)])  2.82 us
    pallas_call x1, Pallas kernels, planned(): pl.pallas_call(plan_kernel, out_shape=jax.ShapeDtypeStruct((listed(4, 0,...  2.62 us
  transfers between devices with their start and end apart: 17, of which 10 were waited for; matrix products, arithmetic and copies ran while one was open for 15% of the time, Pallas kernels for 15%

profile of v4, /device:TPU:1, one launch (start us, length us, event | category | flops | bytes accessed | tf_op | source)
XLA Modules:
  0.0 74.4 jit_solution(12247760730369502994)
XLA Ops:
  0.0 3.2 %collective-permute-start.3 = (bf16[640,5120]{1,0:T(8,128)(2,1)}, bf16[640,5120]{1,0:T(8,128)(2,1)}, u32[]{:S(2)}, u32[]{:S(2)}) collective-permute-start(bf16[640,5120]{1,0:T(8,128)(2,1)} %param.11), channel_id=1, source_target_pairs={{0,1},{1,0},{2,3},{3,2},{4,5},{5,4},{6,7},{7,6},{8,9},{9,8},{10,11... | collective-permute-start | bytes 19660808 | tf_op jit(solution)/shard_map/ppermute | solution.py:222
  3.2 1.0 %pad_select_fusion = bf16[512,128]{1,0:T(8,128)(2,1)S(1)} fusion(bf16[256,128]{1,0:T(8,128)(2,1)} %param.10, bf16[256,128]{1,0:T(8,128)(2,1)} %param.9, pred[512]{0:T(512)(128)(4,1)S(1)} %iota_compare_fusion), kind=kLoop, calls=%fused_computation.6 | loop fusion | flops 65536 | bytes 262656 | tf_op jit(solution)/shard_map/jit(_where)/select_n | solution.py:263
  4.3 5.3 %collective-permute-start = (bf16[512,128]{1,0:T(8,128)(2,1)S(1)}, bf16[512,128]{1,0:T(8,128)(2,1)S(1)}, u32[]{:S(2)}, u32[]{:S(2)}) collective-permute-start(bf16[512,128]{1,0:T(8,128)(2,1)S(1)} %pad_select_fusion), channel_id=1, source_target_pairs={{16,0},{20,4},{24,8},{28,12},{0,16},{4,20},{8,24},{12,28},{48,32},... | collective-permute-start | bytes 393224 | tf_op jit(solution)/shard_map/ppermute | solution.py:39
  9.5 2.0 %collective-permute-start.1 = (bf16[512,128]{1,0:T(8,128)(2,1)S(1)}, bf16[512,128]{1,0:T(8,128)(2,1)S(1)}, u32[]{:S(2)}, u32[]{:S(2)}) collective-permute-start(bf16[512,128]{1,0:T(8,128)(2,1)S(1)} %pad_select_fusion), channel_id=1, source_target_pairs={{72,0},{76,4},{80,8},{84,12},{88,16},{92,20},{64,24},{68,28},{104,... | collective-permute-start | bytes 393224 | tf_op jit(solution)/shard_map/ppermute | solution.py:39
  11.5 2.8 %collective-permute-start.2 = (bf16[512,128]{1,0:T(8,128)(2,1)S(1)}, bf16[512,128]{1,0:T(8,128)(2,1)S(1)}, u32[]{:S(2)}, u32[]{:S(2)}) collective-permute-start(bf16[512,128]{1,0:T(8,128)(2,1)S(1)} %pad_select_fusion), channel_id=1, source_target_pairs={{88,0},{92,4},{64,8},{68,12},{72,16},{76,20},{80,24},{84,28},{120,... | collective-permute-start | bytes 393224 | tf_op jit(solution)/shard_map/ppermute | solution.py:39
  14.3 3.9 %constant_dynamic-slice_fusion.2 = bf16[640,2560]{1,0:T(8,128)(2,1)} fusion(bf16[640,5120]{1,0:T(8,128)(2,1)} %param.11, s32[]{:T(128)S(6)} %select_n.17), kind=kLoop, calls=%fused_computation.15 | loop fusion | bytes 6553604 | tf_op jit(solution)/shard_map/dynamic_slice | solution.py:232
  18.2 1.2 %collective-permute-start.14 = (bf16[640,2560]{1,0:T(8,128)(2,1)}, bf16[640,2560]{1,0:T(8,128)(2,1)}, u32[]{:S(2)}, u32[]{:S(2)}) collective-permute-start(bf16[640,2560]{1,0:T(8,128)(2,1)} %constant_dynamic-slice_fusion.2), channel_id=1, source_target_pairs={{2,0},{131,1},{128,2},{1,3},{130,128},{3,129},{0,130},{129,131},{6... | collective-permute-start | bytes 9830408 | tf_op jit(solution)/shard_map/ppermute | solution.py:228
  20.1 2.6 %plan.1 = s32[608]{0:T(1024)} custom-call(s32[64]{0:T(128)} %order.1, s32[8]{0:T(128)} %lengths.1, s32[64,64]{1,0:T(8,128)} %reveal.1, s32[1]{0:T(128)S(6)} %copy.13.step), custom_call_target="tpu_custom_call" | custom-call | tf_op jit(solution)/shard_map/plan/pallas_call | solution.py:193
  22.7 2.4 %collective-permute-done.1 = bf16[512,128]{1,0:T(8,128)(2,1)S(1)} collective-permute-done((bf16[512,128]{1,0:T(8,128)(2,1)S(1)}, bf16[512,128]{1,0:T(8,128)(2,1)S(1)}, u32[]{:S(2)}, u32[]{:S(2)}) %collective-permute-start.1) | collective-permute-done | bytes 131104 | tf_op jit(solution)/shard_map/ppermute | solution.py:39
  25.1 0.9 %collective-permute-start.6 = (bf16[2048,128]{1,0:T(8,128)(2,1)S(1)}, bf16[2048,128]{1,0:T(8,128)(2,1)S(1)}, u32[]{:S(2)}, u32[]{:S(2)}) collective-permute-start(bf16[2048,128]{1,0:T(8,128)(2,1)S(1)} %pad_maximum_fusion.1), channel_id=1, source_target_pairs={{32,0},{36,4},{40,8},{44,12},{48,16},{52,20},{56,24},{60,28},{64,3... | collective-permute-start | bytes 1572872 | tf_op jit(solution)/shard_map/ppermute | solution.py:39
  26.7 2.6 %collective-permute-start.4 = (bf16[2048,128]{1,0:T(8,128)(2,1)S(1)}, bf16[2048,128]{1,0:T(8,128)(2,1)S(1)}, u32[]{:S(2)}, u32[]{:S(2)}) collective-permute-start(bf16[2048,128]{1,0:T(8,128)(2,1)S(1)} %pad_maximum_fusion.1), channel_id=1, source_target_pairs={{4,0},{8,4},{12,8},{16,12},{20,16},{24,20},{28,24},{0,28},{36,32},... | collective-permute-start | bytes 1572872 | tf_op jit(solution)/shard_map/ppermute | solution.py:39
  29.3 2.1 %constant_dynamic-slice_fusion.3 = (bf16[640,1280]{1,0:T(8,128)(2,1)S(1)}, bf16[640,1280]{1,0:T(8,128)(2,1)S(1)}) fusion(bf16[640,5120]{1,0:T(8,128)(2,1)} %collective-permute-done.3, s32[]{:T(128)S(6)} %select_n.16, bf16[640,5120]{1,0:T(8,128)(2,1)} %param.11), kind=kLoop, calls=%fused_computation.16 | loop fusion | bytes 6553604 | tf_op jit(solution)/shard_map/dynamic_slice | solution.py:232
  31.5 7.5 %collective-permute-done.4 = bf16[2048,128]{1,0:T(8,128)(2,1)S(1)} collective-permute-done((bf16[2048,128]{1,0:T(8,128)(2,1)S(1)}, bf16[2048,128]{1,0:T(8,128)(2,1)S(1)}, u32[]{:S(2)}, u32[]{:S(2)}) %collective-permute-start.4) | collective-permute-done | bytes 524320 | tf_op jit(solution)/shard_map/ppermute | solution.py:39
  39.0 3.1 %collective-permute-done.5 = bf16[2048,128]{1,0:T(8,128)(2,1)S(1)} collective-permute-done((bf16[2048,128]{1,0:T(8,128)(2,1)S(1)}, bf16[2048,128]{1,0:T(8,128)(2,1)S(1)}, u32[]{:S(2)}, u32[]{:S(2)}) %collective-permute-start.5) | collective-permute-done | bytes 524320 | tf_op jit(solution)/shard_map/ppermute | solution.py:39
  42.7 1.1 %collective-permute-start.11 = (bf16[1536,128]{1,0:T(8,128)(2,1)S(1)}, bf16[1536,128]{1,0:T(8,128)(2,1)S(1)}, u32[]{:S(2)}, u32[]{:S(2)}) collective-permute-start(bf16[1536,128]{1,0:T(8,128)(2,1)S(1)} %get-tuple-element.43), channel_id=1, source_target_pairs={{28,0},{0,4},{4,8},{8,12},{12,16},{16,20},{20,24},{24,28},{60,32},... | collective-permute-start | bytes 1179656 | tf_op jit(solution)/shard_map/ppermute | solution.py:39
  43.9 1.0 %collective-permute-start.7 = (bf16[1536,128]{1,0:T(8,128)(2,1)S(1)}, bf16[1536,128]{1,0:T(8,128)(2,1)S(1)}, u32[]{:S(2)}, u32[]{:S(2)}) collective-permute-start(bf16[1536,128]{1,0:T(8,128)(2,1)S(1)} %get-tuple-element.44), channel_id=1, source_target_pairs={{32,0},{36,4},{40,8},{44,12},{48,16},{52,20},{56,24},{60,28},{64,3... | collective-permute-start | bytes 1179656 | tf_op jit(solution)/shard_map/ppermute | solution.py:39
  45.7 3.6 %attention_0.1 = (f32[2,1,640]{2,1,0:T(1,128)S(1)}, f32[2,8,640]{2,1,0:T(8,128)S(1)}, f32[2,128,640]{2,1,0:T(8,128)S(1)}) custom-call(s32[608]{0:T(1024)S(1)} %copy-done.2, bf16[256,640]{1,0:T(8,128)(2,1)S(1)} %copy-done.3, bf16[10240,128]{1,0:T(8,128)(2,1)S(1)} %constant_dynamic-update-slice_fusion.kv), custom_call_target="tpu_custom_call" | custom-call | flops 1000000000 | bytes 10000000 | tf_op jit(solution)/shard_map/attention_0/pallas_call | solution.py:205
  49.3 1.1 %collective-permute-done.10 = bf16[1536,128]{1,0:T(8,128)(2,1)S(1)} collective-permute-done((bf16[1536,128]{1,0:T(8,128)(2,1)S(1)}, bf16[1536,128]{1,0:T(8,128)(2,1)S(1)}, u32[]{:S(2)}, u32[]{:S(2)}) %collective-permute-start.10) | collective-permute-done | bytes 393248 | tf_op jit(solution)/shard_map/ppermute | solution.py:39
  50.4 1.4 %collective-permute-done.11 = bf16[1536,128]{1,0:T(8,128)(2,1)S(1)} collective-permute-done((bf16[1536,128]{1,0:T(8,128)(2,1)S(1)}, bf16[1536,128]{1,0:T(8,128)(2,1)S(1)}, u32[]{:S(2)}, u32[]{:S(2)}) %collective-permute-start.11) | collective-permute-done | bytes 393248 | tf_op jit(solution)/shard_map/ppermute | solution.py:39
  51.8 1.1 %collective-permute-done.9 = bf16[1536,128]{1,0:T(8,128)(2,1)S(1)} collective-permute-done((bf16[1536,128]{1,0:T(8,128)(2,1)S(1)}, bf16[1536,128]{1,0:T(8,128)(2,1)S(1)}, u32[]{:S(2)}, u32[]{:S(2)}) %collective-permute-start.9) | collective-permute-done | bytes 393248 | tf_op jit(solution)/shard_map/ppermute | solution.py:39
  53.1 2.6 %attention_1.1.heads = bf16[256,640]{1,0:T(8,128)(2,1)S(1)} custom-call(s32[608]{0:T(1024)S(1)} %copy-done.2, bf16[256,640]{1,0:T(8,128)(2,1)S(1)} %copy-done.3, bf16[6144,128]{1,0:T(8,128)(2,1)S(1)} %pad_maximum_fusion.kv, f32[2,1,640]{2,1,0:T(1,128)S(1)} %get-tuple-element.25.refs_0_, f32[2,8,640]{2,1,0:T(8,128)S(1)} %get-tuple-element.26.refs_1_, ...), custom_call_target="tpu_custom_call" | custom-call | flops 1000000000 | bytes 10000000 | tf_op jit(solution)/shard_map/attention_1/pallas_call | solution.py:205
  55.7 0.7 copy-done
  56.4 0.9 %collective-permute-done.14 = bf16[640,2560]{1,0:T(8,128)(2,1)} collective-permute-done((bf16[640,2560]{1,0:T(8,128)(2,1)}, bf16[640,2560]{1,0:T(8,128)(2,1)}, u32[]{:S(2)}, u32[]{:S(2)}) %collective-permute-start.14) | collective-permute-done | bytes 3276832 | tf_op jit(solution)/shard_map/ppermute | solution.py:228
  57.4 3.9 %collective-permute-start.15 = (bf16[640,2560]{1,0:T(8,128)(2,1)}, bf16[640,2560]{1,0:T(8,128)(2,1)}, u32[]{:S(2)}, u32[]{:S(2)}) collective-permute-start(bf16[640,2560]{1,0:T(8,128)(2,1)} %collective-permute-done.14), channel_id=1, source_target_pairs={{0,1},{1,0},{2,3},{3,2},{4,5},{5,4},{6,7},{7,6},{8,9},{9,8},{10,11... | collective-permute-start | bytes 9830408 | tf_op jit(solution)/shard_map/ppermute | solution.py:222
  61.2 1.2 %collective-permute-start.12 = (bf16[256,640]{1,0:T(8,128)(2,1)}, bf16[256,640]{1,0:T(8,128)(2,1)S(1)}, u32[]{:S(2)}, u32[]{:S(2)}) collective-permute-start(bf16[256,640]{1,0:T(8,128)(2,1)} %copy-done), channel_id=1, source_target_pairs={{0,2},{2,0},{1,3},{3,1},{4,6},{6,4},{5,7},{7,5},{8,10},{10,8},{9,1... | collective-permute-start | bytes 983048 | tf_op jit(solution)/shard_map/ppermute | solution.py:222
  62.4 1.0 %copy-done.1 = bf16[256,640]{1,0:T(8,128)(2,1)S(1)} copy-done((bf16[256,640]{1,0:T(8,128)(2,1)S(1)}, bf16[256,640]{1,0:T(8,128)(2,1)}, u32[]{:S(2)}) %copy-start.1) | copy-done | bytes 327704
  64.1 1.5 %constant_dynamic-slice_fusion.1.weight = bf16[640,1280]{1,0:T(8,128)(2,1)S(1)} fusion(bf16[640,2560]{1,0:T(8,128)(2,1)} %collective-permute-done.14, s32[]{:T(128)S(6)} %select_n.18), kind=kLoop, calls=%fused_computation.14 | loop fusion | bytes 3276804 | tf_op jit(solution)/shard_map/dynamic_slice | solution.py:232
  65.7 1.6 %collective-permute-done.13.heads = bf16[256,640]{1,0:T(8,128)(2,1)S(1)} collective-permute-done((bf16[256,640]{1,0:T(8,128)(2,1)}, bf16[256,640]{1,0:T(8,128)(2,1)S(1)}, u32[]{:S(2)}, u32[]{:S(2)}) %collective-permute-start.13) | collective-permute-done | bytes 327712 | tf_op jit(solution)/shard_map/ppermute | solution.py:222
  67.2 0.7 project.5.refs_0_
  68.0 1.5 %constant_dynamic-slice_fusion.weight = bf16[640,1280]{1,0:T(8,128)(2,1)S(1)} fusion(bf16[640,2560]{1,0:T(8,128)(2,1)} %collective-permute-done.15, s32[]{:T(128)S(6)} %select_n.18), kind=kLoop, calls=%fused_computation.13 | loop fusion | bytes 3276804 | tf_op jit(solution)/shard_map/dynamic_slice | solution.py:232
  70.2 1.4 %collective-permute-start.16 = (bf16[256,640]{1,0:T(8,128)(2,1)S(1)}, bf16[256,640]{1,0:T(8,128)(2,1)S(1)}, u32[]{:S(2)}, u32[]{:S(2)}) collective-permute-start(bf16[256,640]{1,0:T(8,128)(2,1)S(1)} %collective-permute-done.12.heads), channel_id=1, source_target_pairs={{0,1},{1,0},{2,3},{3,2},{4,5},{5,4},{6,7},{7,6},{8,9},{9,8},{10,11... | collective-permute-start | bytes 983048 | tf_op jit(solution)/shard_map/ppermute | solution.py:222
  72.8 1.5 %project.7 = bf16[256,1280]{1,0:T(8,128)(2,1)} custom-call(bf16[256,640]{1,0:T(8,128)(2,1)S(1)} %collective-permute-done.16.heads, bf16[640,1280]{1,0:T(8,128)(2,1)S(1)} %constant_dynamic-slice_fusion.weight, f32[256,1280]{1,0:T(8,128)S(1)} %project.6.refs_0_), custom_call_target="tpu_custom_call" | custom-call | flops 419430400 | bytes 1638400 | tf_op jit(solution)/shard_map/project/pallas_call | solution.py:246
  (35 shorter events, 4.9 us)
Async XLA Ops:
  0.0 25.1 %collective-permute-start.3 = (bf16[640,5120]{1,0:T(8,128)(2,1)}, bf16[640,5120]{1,0:T(8,128)(2,1)}, u32[]{:S(2)}, u32[]{:S(2)}) collective-permute-start(bf16[640,5120]{1,0:T(8,128)(2,1)} %param.11), channel_id=1, source_target_pairs={{0,1},{1,0},{2,3},{3,2},{4,5},{5,4},{6,7},{7,6},{8,9},{9,8},{10,11... | collective-permute-start | bytes 19660808 | tf_op jit(solution)/shard_map/ppermute | solution.py:222
  4.3 18.4 %collective-permute-start = (bf16[512,128]{1,0:T(8,128)(2,1)S(1)}, bf16[512,128]{1,0:T(8,128)(2,1)S(1)}, u32[]{:S(2)}, u32[]{:S(2)}) collective-permute-start(bf16[512,128]{1,0:T(8,128)(2,1)S(1)} %pad_select_fusion), channel_id=1, source_target_pairs={{16,0},{20,4},{24,8},{28,12},{0,16},{4,20},{8,24},{12,28},{48,32},... | collective-permute-start | bytes 393224 | tf_op jit(solution)/shard_map/ppermute | solution.py:39
  9.5 15.5 %collective-permute-start.1 = (bf16[512,128]{1,0:T(8,128)(2,1)S(1)}, bf16[512,128]{1,0:T(8,128)(2,1)S(1)}, u32[]{:S(2)}, u32[]{:S(2)}) collective-permute-start(bf16[512,128]{1,0:T(8,128)(2,1)S(1)} %pad_select_fusion), channel_id=1, source_target_pairs={{72,0},{76,4},{80,8},{84,12},{88,16},{92,20},{64,24},{68,28},{104,... | collective-permute-start | bytes 393224 | tf_op jit(solution)/shard_map/ppermute | solution.py:39
  11.5 13.5 %collective-permute-start.2 = (bf16[512,128]{1,0:T(8,128)(2,1)S(1)}, bf16[512,128]{1,0:T(8,128)(2,1)S(1)}, u32[]{:S(2)}, u32[]{:S(2)}) collective-permute-start(bf16[512,128]{1,0:T(8,128)(2,1)S(1)} %pad_select_fusion), channel_id=1, source_target_pairs={{88,0},{92,4},{64,8},{68,12},{72,16},{76,20},{80,24},{84,28},{120,... | collective-permute-start | bytes 393224 | tf_op jit(solution)/shard_map/ppermute | solution.py:39
  18.2 39.2 %collective-permute-start.14 = (bf16[640,2560]{1,0:T(8,128)(2,1)}, bf16[640,2560]{1,0:T(8,128)(2,1)}, u32[]{:S(2)}, u32[]{:S(2)}) collective-permute-start(bf16[640,2560]{1,0:T(8,128)(2,1)} %constant_dynamic-slice_fusion.2), channel_id=1, source_target_pairs={{2,0},{131,1},{128,2},{1,3},{130,128},{3,129},{0,130},{129,131},{6... | collective-permute-start | bytes 9830408 | tf_op jit(solution)/shard_map/ppermute | solution.py:228
  25.1 13.8 %collective-permute-start.6 = (bf16[2048,128]{1,0:T(8,128)(2,1)S(1)}, bf16[2048,128]{1,0:T(8,128)(2,1)S(1)}, u32[]{:S(2)}, u32[]{:S(2)}) collective-permute-start(bf16[2048,128]{1,0:T(8,128)(2,1)S(1)} %pad_maximum_fusion.1), channel_id=1, source_target_pairs={{32,0},{36,4},{40,8},{44,12},{48,16},{52,20},{56,24},{60,28},{64,3... | collective-permute-start | bytes 1572872 | tf_op jit(solution)/shard_map/ppermute | solution.py:39
  26.0 16.1 %collective-permute-start.8 = (bf16[2048,128]{1,0:T(8,128)(2,1)S(1)}, bf16[2048,128]{1,0:T(8,128)(2,1)S(1)}, u32[]{:S(2)}, u32[]{:S(2)}) collective-permute-start(bf16[2048,128]{1,0:T(8,128)(2,1)S(1)} %pad_maximum_fusion.1), channel_id=1, source_target_pairs={{96,0},{100,4},{104,8},{108,12},{112,16},{116,20},{120,24},{124,28... | collective-permute-start | bytes 1572872 | tf_op jit(solution)/shard_map/ppermute | solution.py:39
  26.7 12.3 %collective-permute-start.4 = (bf16[2048,128]{1,0:T(8,128)(2,1)S(1)}, bf16[2048,128]{1,0:T(8,128)(2,1)S(1)}, u32[]{:S(2)}, u32[]{:S(2)}) collective-permute-start(bf16[2048,128]{1,0:T(8,128)(2,1)S(1)} %pad_maximum_fusion.1), channel_id=1, source_target_pairs={{4,0},{8,4},{12,8},{16,12},{20,16},{24,20},{28,24},{0,28},{36,32},... | collective-permute-start | bytes 1572872 | tf_op jit(solution)/shard_map/ppermute | solution.py:39
  29.3 12.8 %collective-permute-start.5 = (bf16[2048,128]{1,0:T(8,128)(2,1)S(1)}, bf16[2048,128]{1,0:T(8,128)(2,1)S(1)}, u32[]{:S(2)}, u32[]{:S(2)}) collective-permute-start(bf16[2048,128]{1,0:T(8,128)(2,1)S(1)} %pad_maximum_fusion.1), channel_id=1, source_target_pairs={{28,0},{0,4},{4,8},{8,12},{12,16},{16,20},{20,24},{24,28},{60,32},... | collective-permute-start | bytes 1572872 | tf_op jit(solution)/shard_map/ppermute | solution.py:39
  42.3 3.3 %copy-start.2 = (s32[608]{0:T(1024)S(1)}, s32[608]{0:T(1024)}, u32[]{:S(2)}) copy-start(s32[608]{0:T(1024)} %plan.1) | copy-start | bytes 7300
  42.3 3.3 %copy-start.3 = (bf16[256,640]{1,0:T(8,128)(2,1)S(1)}, bf16[256,640]{1,0:T(8,128)(2,1)}, u32[]{:S(2)}) copy-start(bf16[256,640]{1,0:T(8,128)(2,1)} %q_ref.3) | copy-start | bytes 983044
  42.3 8.0 %collective-permute-start.10 = (bf16[1536,128]{1,0:T(8,128)(2,1)S(1)}, bf16[1536,128]{1,0:T(8,128)(2,1)S(1)}, u32[]{:S(2)}, u32[]{:S(2)}) collective-permute-start(bf16[1536,128]{1,0:T(8,128)(2,1)S(1)} %get-tuple-element.42), channel_id=1, source_target_pairs={{4,0},{8,4},{12,8},{16,12},{20,16},{24,20},{28,24},{0,28},{36,32},... | collective-permute-start | bytes 1179656 | tf_op jit(solution)/shard_map/ppermute | solution.py:39
  42.7 9.1 %collective-permute-start.11 = (bf16[1536,128]{1,0:T(8,128)(2,1)S(1)}, bf16[1536,128]{1,0:T(8,128)(2,1)S(1)}, u32[]{:S(2)}, u32[]{:S(2)}) collective-permute-start(bf16[1536,128]{1,0:T(8,128)(2,1)S(1)} %get-tuple-element.43), channel_id=1, source_target_pairs={{28,0},{0,4},{4,8},{8,12},{12,16},{16,20},{20,24},{24,28},{60,32},... | collective-permute-start | bytes 1179656 | tf_op jit(solution)/shard_map/ppermute | solution.py:39
  43.9 7.9 %collective-permute-start.7 = (bf16[1536,128]{1,0:T(8,128)(2,1)S(1)}, bf16[1536,128]{1,0:T(8,128)(2,1)S(1)}, u32[]{:S(2)}, u32[]{:S(2)}) collective-permute-start(bf16[1536,128]{1,0:T(8,128)(2,1)S(1)} %get-tuple-element.44), channel_id=1, source_target_pairs={{32,0},{36,4},{40,8},{44,12},{48,16},{52,20},{56,24},{60,28},{64,3... | collective-permute-start | bytes 1179656 | tf_op jit(solution)/shard_map/ppermute | solution.py:39
  44.8 8.1 %collective-permute-start.9 = (bf16[1536,128]{1,0:T(8,128)(2,1)S(1)}, bf16[1536,128]{1,0:T(8,128)(2,1)S(1)}, u32[]{:S(2)}, u32[]{:S(2)}) collective-permute-start(bf16[1536,128]{1,0:T(8,128)(2,1)S(1)} %get-tuple-element.41), channel_id=1, source_target_pairs={{96,0},{100,4},{104,8},{108,12},{112,16},{116,20},{120,24},{124,28... | collective-permute-start | bytes 1179656 | tf_op jit(solution)/shard_map/ppermute | solution.py:39
  55.7 0.7 copy-start
  57.4 10.6 %collective-permute-start.15 = (bf16[640,2560]{1,0:T(8,128)(2,1)}, bf16[640,2560]{1,0:T(8,128)(2,1)}, u32[]{:S(2)}, u32[]{:S(2)}) collective-permute-start(bf16[640,2560]{1,0:T(8,128)(2,1)} %collective-permute-done.14), channel_id=1, source_target_pairs={{0,1},{1,0},{2,3},{3,2},{4,5},{5,4},{6,7},{7,6},{8,9},{9,8},{10,11... | collective-permute-start | bytes 9830408 | tf_op jit(solution)/shard_map/ppermute | solution.py:222
  61.2 6.0 %collective-permute-start.13 = (bf16[256,640]{1,0:T(8,128)(2,1)}, bf16[256,640]{1,0:T(8,128)(2,1)S(1)}, u32[]{:S(2)}, u32[]{:S(2)}) collective-permute-start(bf16[256,640]{1,0:T(8,128)(2,1)} %copy-done), channel_id=1, source_target_pairs={{0,1},{1,0},{2,3},{3,2},{4,5},{5,4},{6,7},{7,6},{8,9},{9,8},{10,11... | collective-permute-start | bytes 983048 | tf_op jit(solution)/shard_map/ppermute | solution.py:222
  61.2 9.0 %collective-permute-start.12 = (bf16[256,640]{1,0:T(8,128)(2,1)}, bf16[256,640]{1,0:T(8,128)(2,1)S(1)}, u32[]{:S(2)}, u32[]{:S(2)}) collective-permute-start(bf16[256,640]{1,0:T(8,128)(2,1)} %copy-done), channel_id=1, source_target_pairs={{0,2},{2,0},{1,3},{3,1},{4,6},{6,4},{5,7},{7,5},{8,10},{10,8},{9,1... | collective-permute-start | bytes 983048 | tf_op jit(solution)/shard_map/ppermute | solution.py:222
  62.4 1.0 %copy-start.1 = (bf16[256,640]{1,0:T(8,128)(2,1)S(1)}, bf16[256,640]{1,0:T(8,128)(2,1)}, u32[]{:S(2)}) copy-start(bf16[256,640]{1,0:T(8,128)(2,1)} %copy-done) | copy-start | bytes 983044
  70.2 2.6 %collective-permute-start.16 = (bf16[256,640]{1,0:T(8,128)(2,1)S(1)}, bf16[256,640]{1,0:T(8,128)(2,1)S(1)}, u32[]{:S(2)}, u32[]{:S(2)}) collective-permute-start(bf16[256,640]{1,0:T(8,128)(2,1)S(1)} %collective-permute-done.12.heads), channel_id=1, source_target_pairs={{0,1},{1,0},{2,3},{3,2},{4,5},{5,4},{6,7},{7,6},{8,9},{9,8},{10,11... | collective-permute-start | bytes 983048 | tf_op jit(solution)/shard_map/ppermute | solution.py:222

commit v5 on v4

--- a/solution.py
+++ b/solution.py
@@ -14,9 +14,9 @@
 NY, NZ, NX, NC = 4, 8, 2, 2
 RANKS = NY * NZ
 SLOTS = 2 * RANKS
-CENTRES = ((0, 0), (0, 4), (2, 2), (2, -2))
-STEPS = ((1, 0), (-1, 0), (0, 1), (0, -1))
-PICKS = (((3, 0), (4, 0), (1, 0)), ((4, 1), (3, 0), (2, 1)), ((1, 1), (2, 1), (3, 0)), ((2, 0), (1, 1), (4, 0)))
+CENTRES = ((0, 0), (2, 2), (2, -2), (0, 4))
+STEPS = ((0, 1), (0, -1), (1, 0), (-1, 0))
+PICKS = (((3, 3), (4, 3), (1, 0)), ((4, 0), (3, 3), (2, 0)), ((1, 0), (2, 0), (3, 0)), ((2, 3), (1, 0), (4, 3)))
 
 
 def offsets():
@@ -116,73 +116,75 @@
         top_in, total_in, acc_in, out_ref, acc_ref, scores, probs = refs
     columns = heads * BLK
 
+    down = lax.broadcasted_iota(jnp.int32, (BLK, BLK), 0)
+    queries, bounds, start, n = [], [], [], []
     for t in range(2):
-        l = 2 * stage + t
         rows = pl.ds(t * BLK, BLK)
         q = jnp.concatenate([q_ref[rows, h * HEAD_WIDTH : (h + 1) * HEAD_WIDTH] for h in range(heads)])
-        q = jnp.transpose(q)
+        queries.append(jnp.transpose(q))
         pos = plan[OWN + t] * BLK + lax.broadcasted_iota(jnp.int32, (1, BLK), 1)
         low, high = jnp.zeros((1, BLK), jnp.int32), jnp.zeros((1, BLK), jnp.int32)
         for d in reversed(range(docs)):
             high = jnp.where(pos < plan[ENDS + d], plan[ENDS + d], high)
         for d in range(docs):
             low = jnp.where(pos >= plan[ENDS + d], plan[ENDS + d], low)
-        down = lax.broadcasted_iota(jnp.int32, (BLK, BLK), 0)
+        bounds.append((low, high))
         if stage == 0:
-            acc = acc_ref.at[t]
-            acc[...] = jnp.zeros(acc.shape, jnp.float32)
-            carry = jnp.full((1, columns), LOWEST, jnp.float32), jnp.zeros((8, columns), jnp.float32)
+            acc_ref[t] = jnp.zeros(acc_ref.shape[1:], jnp.float32)
+            first = jnp.full((1, columns), LOWEST, jnp.float32), jnp.zeros((8, columns), jnp.float32)
         else:
-            acc = acc_ref
-            acc[...] = acc_in[t]
-            carry = top_in[t], total_in[t]
-
-        def chunk_rows(i, start):
-            return jnp.concatenate(
-                [kv[pl.ds(pl.multiple_of(plan[listed(l, 0, CHUNK * i + e)] + start, BLK), BLK), :] for e in range(CHUNK)]
-            )
-
-        def score(i):
-            s = jnp.dot(chunk_rows(i, 0), q, preferred_element_type=jnp.float32)
-            for e in range(CHUNK):
-                key = down + plan[listed(l, 1, CHUNK * i + e)] * BLK
-                allowed = (key >= low) & (key < high)
-                for h in range(heads):
-                    part = s[e * BLK : (e + 1) * BLK, h * BLK : (h + 1) * BLK]
-                    scores[i % 2, pl.ds(e * BLK, BLK), pl.ds(h * BLK, BLK)] = jnp.where(allowed, part, MASKED)
-
-        def weigh(i, factor):
-            acc[...] = acc[...] * factor + lax.dot_general(
-                chunk_rows(jnp.maximum(i, 0), 2 * BLK),
-                probs[...],
-                (((0,), (0,)), ((), ())),
-                preferred_element_type=jnp.float32,
-            )
-
-        def chunk(i, carry):
-            top, total, factor = carry
-            s = scores[i % 2]
-            weigh(i - 1, factor)
-            best = jnp.maximum(top, jnp.max(s, axis=0, keepdims=True))
-            p = jnp.exp2(s * scale - best * scale)
-            factor = jnp.exp2((top - best) * scale)
-            probs[...] = p.astype(jnp.bfloat16)
-            score(i + 1)
-            return best, total * factor + jnp.sum(p.reshape(-1, 8, columns), axis=0), factor
-
-        n = plan[COUNTS + l]
-        score(0)
-        probs[...] = jnp.zeros(probs.shape, jnp.bfloat16)
-        top, total, factor = lax.fori_loop(0, n, chunk, (*carry, jnp.ones((1, columns), jnp.float32)))
-        weigh(n - 1, factor)
+            acc_ref[t] = acc_in[t]
+            first = top_in[t], total_in[t]
+        start.append((*first, jnp.ones((1, columns), jnp.float32)))
+        n.append(plan[COUNTS + 2 * stage + t])
+
+    def chunk_rows(t, i, after):
+        l = 2 * stage + t
+        at = [plan[listed(l, 0, CHUNK * i + e)] + after for e in range(CHUNK)]
+        return jnp.concatenate([kv[pl.ds(pl.multiple_of(a, BLK), BLK), :] for a in at])
+
+    def score(t, i):
+        s = jnp.dot(chunk_rows(t, i, 0), queries[t], preferred_element_type=jnp.float32)
+        low, high = bounds[t]
+        for e in range(CHUNK):
+            key = down + plan[listed(2 * stage + t, 1, CHUNK * i + e)] * BLK
+            allowed = (key >= low) & (key < high)
+            for h in range(heads):
+                part = s[e * BLK : (e + 1) * BLK, h * BLK : (h + 1) * BLK]
+                scores[t, i % 2, pl.ds(e * BLK, BLK), pl.ds(h * BLK, BLK)] = jnp.where(allowed, part, MASKED)
+
+    def weigh(t, i, factor):
+        j = jnp.maximum(i, 0)
+        acc_ref[t] = acc_ref[t] * factor + lax.dot_general(
+            chunk_rows(t, j, 2 * BLK), probs[t], (((0,), (0,)), ((), ())), preferred_element_type=jnp.float32
+        )
+
+    def chunk(t, i, carry):
+        top, total, factor = carry
+        s = scores[t, i % 2]
+        weigh(t, i - 1, factor)
+        best = jnp.maximum(top, jnp.max(s, axis=0, keepdims=True))
+        p = jnp.exp2(s * scale - best * scale)
+        factor = jnp.exp2((top - best) * scale)
+        probs[t] = p.astype(jnp.bfloat16)
+        score(t, i + 1)
+        return best, total * factor + jnp.sum(p.reshape(-1, 8, columns), axis=0), factor
+
+    for t in range(2):
+        score(t, 0)
+        probs[t] = jnp.zeros(probs.shape[1:], jnp.bfloat16)
+    end = [lax.fori_loop(0, n[t], functools.partial(chunk, t), start[t]) for t in range(2)]
+    for t in range(2):
+        top, total, factor = end[t]
+        weigh(t, n[t] - 1, factor)
         if stage == 0:
             top_ref[t] = top
             total_ref[t] = total
         else:
-            out = acc[...] / jnp.sum(total, axis=0, keepdims=True)
+            out = acc_ref[t] / jnp.sum(total, axis=0, keepdims=True)
             for h in range(heads):
                 head = jnp.transpose(out[:, h * BLK : (h + 1) * BLK])
-                out_ref[rows, h * HEAD_WIDTH : (h + 1) * HEAD_WIDTH] = head.astype(jnp.bfloat16)
+                out_ref[t * BLK : (t + 1) * BLK, h * HEAD_WIDTH : (h + 1) * HEAD_WIDTH] = head.astype(jnp.bfloat16)
 
 
 SMEM = pl.BlockSpec(memory_space=pltpu.SMEM)
@@ -207,12 +209,12 @@
         out_shape=running if stage == 0 else jax.ShapeDtypeStruct(queries.shape, jnp.bfloat16),
         in_specs=[SMEM] + [VMEM] * (2 + len(before)),
         out_specs=[VMEM] * 3 if stage == 0 else VMEM,
-        scratch_shapes=([] if stage == 0 else [pltpu.VMEM((HEAD_WIDTH, columns), jnp.float32)])
+        scratch_shapes=([] if stage == 0 else [pltpu.VMEM((2, HEAD_WIDTH, columns), jnp.float32)])
         + [
-            pltpu.VMEM((2, CHUNK * BLK, columns), jnp.float32),
-            pltpu.VMEM((CHUNK * BLK, columns), jnp.bfloat16),
+            pltpu.VMEM((2, 2, CHUNK * BLK, columns), jnp.float32),
+            pltpu.VMEM((2, CHUNK * BLK, columns), jnp.bfloat16),
         ],
-        compiler_params=pltpu.CompilerParams(vmem_limit_bytes=7 * 2**20),
+        compiler_params=pltpu.CompilerParams(vmem_limit_bytes=9 * 2**20),
         cost_estimate=pl.CostEstimate(flops=10**9, bytes_accessed=10**7, transcendentals=3 * 10**6),
         name="attention_%d" % stage,
     )(plan, queries, kv, *before)

time: 74.4 us -> 74.7 us (level); the launches traced: 74.4 us -> 73.7 us
  waiting for transfers between devices: 20.4 us -> 17.4 us
  Pallas kernels: 12.5 us -> 13.8 us
  starting transfers between devices: 28.1 us -> 29.1 us
    ppermute x11, waiting for transfers between devices: 16.6 us -> 12.8 us  [moved(): return lax.ppermute(x, ('y', 'z'), route)]
    ppermute x11, starting transfers between devices: 17.2 us -> 18.8 us  [moved(): return lax.ppermute(x, ('y', 'z'), route)]
    pallas_call x2, Pallas kernels: 6.22 us -> 7.56 us  [attention(): pl.pallas_call(functools.partial(attention_kernel, stage=stage, docs=docs...]
    ppermute x1, waiting for transfers between devices: 0.93 us -> 1.75 us  [from_both_sides(): return lax.ppermute(x, ('dp', 'x', 'core'), route)]
  transfers between devices with their start and end apart: 17 -> 17, of which waited for: 10 -> 11; matrix products, arithmetic and copies ran while one was open for 15% -> 15% of each run, Pallas kernels for 15% -> 17%
where the time goes in v5:
time: 74.7 us; the launch traced here: 73.7 us
  starting transfers between devices  29.1 us (39%)
  waiting for transfers between devices  17.4 us (23%)
  Pallas kernels  13.8 us (18%)
  local copies, waits for them, and re-layouts  11.3 us (15%)
  other arithmetic  1.29 us (2%)
  between operations  0.89 us (1%)
    ppermute x11, starting transfers between devices, moved(): return lax.ppermute(x, ('y', 'z'), route)  18.8 us
    ppermute x11, waiting for transfers between devices, moved(): return lax.ppermute(x, ('y', 'z'), route)  12.8 us
    ppermute x5, starting transfers between devices, swapped(): return lax.ppermute(x, axis, [(0, 1), (1, 0)])  9.16 us
    dynamic_slice x4, local copies, waits for them, and re-layouts, columns_of(): return lax.dynamic_slice_in_dim(weight, column * width, width, 1)  9.15 us
    pallas_call x2, Pallas kernels, attention(): pl.pallas_call(functools.partial(attention_kernel, stage=stage, docs=docs...  7.56 us
    pallas_call x4, Pallas kernels, projected(): pl.pallas_call(project_kernel, out_shape=jax.ShapeDtypeStruct((rows, widt...  3.62 us
    ppermute x5, waiting for transfers between devices, swapped(): return lax.ppermute(x, axis, [(0, 1), (1, 0)])  2.82 us
    pallas_call x1, Pallas kernels, planned(): pl.pallas_call(plan_kernel, out_shape=jax.ShapeDtypeStruct((listed(4, 0,...  2.62 us
  transfers between devices with their start and end apart: 17, of which 11 were waited for; matrix products, arithmetic and copies ran while one was open for 15% of the time, Pallas kernels for 17%

profile of v5, /device:TPU:1, one launch (start us, length us, event | category | flops | bytes accessed | tf_op | source)
XLA Modules:
  0.0 73.7 jit_solution(7293975422119353781)
XLA Ops:
  0.0 3.2 %collective-permute-start.3 = (bf16[640,5120]{1,0:T(8,128)(2,1)}, bf16[640,5120]{1,0:T(8,128)(2,1)}, u32[]{:S(2)}, u32[]{:S(2)}) collective-permute-start(bf16[640,5120]{1,0:T(8,128)(2,1)} %param.11), channel_id=1, source_target_pairs={{0,1},{1,0},{2,3},{3,2},{4,5},{5,4},{6,7},{7,6},{8,9},{9,8},{10,11... | collective-permute-start | bytes 19660808 | tf_op jit(solution)/shard_map/ppermute | solution.py:224
  3.2 1.0 %pad_select_fusion = bf16[512,128]{1,0:T(8,128)(2,1)S(1)} fusion(bf16[256,128]{1,0:T(8,128)(2,1)} %param.10, bf16[256,128]{1,0:T(8,128)(2,1)} %param.9, pred[512]{0:T(512)(128)(4,1)S(1)} %iota_compare_fusion), kind=kLoop, calls=%fused_computation.6 | loop fusion | flops 65536 | bytes 262656 | tf_op jit(solution)/shard_map/jit(_where)/select_n | solution.py:265
  4.3 7.0 %collective-permute-start = (bf16[512,128]{1,0:T(8,128)(2,1)S(1)}, bf16[512,128]{1,0:T(8,128)(2,1)S(1)}, u32[]{:S(2)}, u32[]{:S(2)}) collective-permute-start(bf16[512,128]{1,0:T(8,128)(2,1)S(1)} %pad_select_fusion), channel_id=1, source_target_pairs={{72,0},{76,4},{80,8},{84,12},{88,16},{92,20},{64,24},{68,28},{104,... | collective-permute-start | bytes 393224 | tf_op jit(solution)/shard_map/ppermute | solution.py:39
  11.3 3.0 %collective-permute-start.2 = (bf16[512,128]{1,0:T(8,128)(2,1)S(1)}, bf16[512,128]{1,0:T(8,128)(2,1)S(1)}, u32[]{:S(2)}, u32[]{:S(2)}) collective-permute-start(bf16[512,128]{1,0:T(8,128)(2,1)S(1)} %pad_select_fusion), channel_id=1, source_target_pairs={{16,0},{20,4},{24,8},{28,12},{0,16},{4,20},{8,24},{12,28},{48,32},... | collective-permute-start | bytes 393224 | tf_op jit(solution)/shard_map/ppermute | solution.py:39
  14.3 3.9 %constant_dynamic-slice_fusion.2 = bf16[640,2560]{1,0:T(8,128)(2,1)} fusion(bf16[640,5120]{1,0:T(8,128)(2,1)} %param.11, s32[]{:T(128)S(6)} %select_n.17), kind=kLoop, calls=%fused_computation.15 | loop fusion | bytes 6553604 | tf_op jit(solution)/shard_map/dynamic_slice | solution.py:234
  18.2 1.2 %collective-permute-start.14 = (bf16[640,2560]{1,0:T(8,128)(2,1)}, bf16[640,2560]{1,0:T(8,128)(2,1)}, u32[]{:S(2)}, u32[]{:S(2)}) collective-permute-start(bf16[640,2560]{1,0:T(8,128)(2,1)} %constant_dynamic-slice_fusion.2), channel_id=1, source_target_pairs={{2,0},{131,1},{128,2},{1,3},{130,128},{3,129},{0,130},{129,131},{6... | collective-permute-start | bytes 9830408 | tf_op jit(solution)/shard_map/ppermute | solution.py:230
  20.1 2.6 %plan.1 = s32[608]{0:T(1024)} custom-call(s32[64]{0:T(128)} %order.1, s32[8]{0:T(128)} %lengths.1, s32[64,64]{1,0:T(8,128)} %reveal.1, s32[1]{0:T(128)S(6)} %copy.13.step), custom_call_target="tpu_custom_call" | custom-call | tf_op jit(solution)/shard_map/plan/pallas_call | solution.py:195
  23.4 0.7 collective-permute-start.6
  24.1 1.2 %collective-permute-start.8 = (bf16[2048,128]{1,0:T(8,128)(2,1)S(1)}, bf16[2048,128]{1,0:T(8,128)(2,1)S(1)}, u32[]{:S(2)}, u32[]{:S(2)}) collective-permute-start(bf16[2048,128]{1,0:T(8,128)(2,1)S(1)} %pad_maximum_fusion.1), channel_id=1, source_target_pairs={{28,0},{0,4},{4,8},{8,12},{12,16},{16,20},{20,24},{24,28},{60,32},... | collective-permute-start | bytes 1572872 | tf_op jit(solution)/shard_map/ppermute | solution.py:39
  25.3 2.1 %collective-permute-start.4 = (bf16[2048,128]{1,0:T(8,128)(2,1)S(1)}, bf16[2048,128]{1,0:T(8,128)(2,1)S(1)}, u32[]{:S(2)}, u32[]{:S(2)}) collective-permute-start(bf16[2048,128]{1,0:T(8,128)(2,1)S(1)} %pad_maximum_fusion.1), channel_id=1, source_target_pairs={{32,0},{36,4},{40,8},{44,12},{48,16},{52,20},{56,24},{60,28},{64,3... | collective-permute-start | bytes 1572872 | tf_op jit(solution)/shard_map/ppermute | solution.py:39
  27.4 2.1 %constant_dynamic-slice_fusion.3 = (bf16[640,1280]{1,0:T(8,128)(2,1)S(1)}, bf16[640,1280]{1,0:T(8,128)(2,1)S(1)}) fusion(bf16[640,5120]{1,0:T(8,128)(2,1)} %collective-permute-done.3, s32[]{:T(128)S(6)} %select_n.16, bf16[640,5120]{1,0:T(8,128)(2,1)} %param.11), kind=kLoop, calls=%fused_computation.16 | loop fusion | bytes 6553604 | tf_op jit(solution)/shard_map/dynamic_slice | solution.py:234
  29.6 3.1 %collective-permute-done.6 = bf16[2048,128]{1,0:T(8,128)(2,1)S(1)} collective-permute-done((bf16[2048,128]{1,0:T(8,128)(2,1)S(1)}, bf16[2048,128]{1,0:T(8,128)(2,1)S(1)}, u32[]{:S(2)}, u32[]{:S(2)}) %collective-permute-start.6) | collective-permute-done | bytes 524320 | tf_op jit(solution)/shard_map/ppermute | solution.py:39
  32.7 4.3 %collective-permute-done.5 = bf16[2048,128]{1,0:T(8,128)(2,1)S(1)} collective-permute-done((bf16[2048,128]{1,0:T(8,128)(2,1)S(1)}, bf16[2048,128]{1,0:T(8,128)(2,1)S(1)}, u32[]{:S(2)}, u32[]{:S(2)}) %collective-permute-start.5) | collective-permute-done | bytes 524320 | tf_op jit(solution)/shard_map/ppermute | solution.py:39
  37.1 2.7 %collective-permute-done.8 = bf16[2048,128]{1,0:T(8,128)(2,1)S(1)} collective-permute-done((bf16[2048,128]{1,0:T(8,128)(2,1)S(1)}, bf16[2048,128]{1,0:T(8,128)(2,1)S(1)}, u32[]{:S(2)}, u32[]{:S(2)}) %collective-permute-start.8) | collective-permute-done | bytes 524320 | tf_op jit(solution)/shard_map/ppermute | solution.py:39
  40.4 1.2 %collective-permute-start.11 = (bf16[1536,128]{1,0:T(8,128)(2,1)S(1)}, bf16[1536,128]{1,0:T(8,128)(2,1)S(1)}, u32[]{:S(2)}, u32[]{:S(2)}) collective-permute-start(bf16[1536,128]{1,0:T(8,128)(2,1)S(1)} %get-tuple-element.42), channel_id=1, source_target_pairs={{96,0},{100,4},{104,8},{108,12},{112,16},{116,20},{120,24},{124,28... | collective-permute-start | bytes 1179656 | tf_op jit(solution)/shard_map/ppermute | solution.py:39
  41.6 2.5 %collective-permute-start.7 = (bf16[1536,128]{1,0:T(8,128)(2,1)S(1)}, bf16[1536,128]{1,0:T(8,128)(2,1)S(1)}, u32[]{:S(2)}, u32[]{:S(2)}) collective-permute-start(bf16[1536,128]{1,0:T(8,128)(2,1)S(1)} %get-tuple-element.41), channel_id=1, source_target_pairs={{4,0},{8,4},{12,8},{16,12},{20,16},{24,20},{28,24},{0,28},{36,32},... | collective-permute-start | bytes 1179656 | tf_op jit(solution)/shard_map/ppermute | solution.py:39
  44.0 0.7 collective-permute-start.9
  45.1 5.1 %attention_0.1 = (f32[2,1,640]{2,1,0:T(1,128)S(1)}, f32[2,8,640]{2,1,0:T(8,128)S(1)}, f32[2,128,640]{2,1,0:T(8,128)S(1)}) custom-call(s32[608]{0:T(1024)S(1)} %copy-done.2, bf16[256,640]{1,0:T(8,128)(2,1)S(1)} %copy-done.3, bf16[10240,128]{1,0:T(8,128)(2,1)S(1)} %constant_dynamic-update-slice_fusion.kv), custom_call_target="tpu_custom_call" | custom-call | flops 1000000000 | bytes 10000000 | tf_op jit(solution)/shard_map/attention_0/pallas_call | solution.py:207
  50.3 1.9 %collective-permute-done.9 = bf16[1536,128]{1,0:T(8,128)(2,1)S(1)} collective-permute-done((bf16[1536,128]{1,0:T(8,128)(2,1)S(1)}, bf16[1536,128]{1,0:T(8,128)(2,1)S(1)}, u32[]{:S(2)}, u32[]{:S(2)}) %collective-permute-start.9) | collective-permute-done | bytes 393248 | tf_op jit(solution)/shard_map/ppermute | solution.py:39
  52.3 2.5 %attention_1.1.heads = bf16[256,640]{1,0:T(8,128)(2,1)S(1)} custom-call(s32[608]{0:T(1024)S(1)} %copy-done.2, bf16[256,640]{1,0:T(8,128)(2,1)S(1)} %copy-done.3, bf16[6144,128]{1,0:T(8,128)(2,1)S(1)} %pad_maximum_fusion.kv, f32[2,1,640]{2,1,0:T(1,128)S(1)} %get-tuple-element.25.refs_0_, f32[2,8,640]{2,1,0:T(8,128)S(1)} %get-tuple-element.26.refs_1_, ...), custom_call_target="tpu_custom_call" | custom-call | flops 1000000000 | bytes 10000000 | tf_op jit(solution)/shard_map/attention_1/pallas_call | solution.py:207
  54.8 0.7 copy-done
  55.5 1.7 %collective-permute-done.14 = bf16[640,2560]{1,0:T(8,128)(2,1)} collective-permute-done((bf16[640,2560]{1,0:T(8,128)(2,1)}, bf16[640,2560]{1,0:T(8,128)(2,1)}, u32[]{:S(2)}, u32[]{:S(2)}) %collective-permute-start.14) | collective-permute-done | bytes 3276832 | tf_op jit(solution)/shard_map/ppermute | solution.py:230
  57.2 3.3 %collective-permute-start.15 = (bf16[640,2560]{1,0:T(8,128)(2,1)}, bf16[640,2560]{1,0:T(8,128)(2,1)}, u32[]{:S(2)}, u32[]{:S(2)}) collective-permute-start(bf16[640,2560]{1,0:T(8,128)(2,1)} %collective-permute-done.14), channel_id=1, source_target_pairs={{0,1},{1,0},{2,3},{3,2},{4,5},{5,4},{6,7},{7,6},{8,9},{9,8},{10,11... | collective-permute-start | bytes 9830408 | tf_op jit(solution)/shard_map/ppermute | solution.py:224
  60.6 1.2 %collective-permute-start.12 = (bf16[256,640]{1,0:T(8,128)(2,1)}, bf16[256,640]{1,0:T(8,128)(2,1)S(1)}, u32[]{:S(2)}, u32[]{:S(2)}) collective-permute-start(bf16[256,640]{1,0:T(8,128)(2,1)} %copy-done), channel_id=1, source_target_pairs={{0,2},{2,0},{1,3},{3,1},{4,6},{6,4},{5,7},{7,5},{8,10},{10,8},{9,1... | collective-permute-start | bytes 983048 | tf_op jit(solution)/shard_map/ppermute | solution.py:224
  61.8 1.0 %copy-done.1 = bf16[256,640]{1,0:T(8,128)(2,1)S(1)} copy-done((bf16[256,640]{1,0:T(8,128)(2,1)S(1)}, bf16[256,640]{1,0:T(8,128)(2,1)}, u32[]{:S(2)}) %copy-start.1) | copy-done | bytes 327704
  63.5 1.5 %constant_dynamic-slice_fusion.1.weight = bf16[640,1280]{1,0:T(8,128)(2,1)S(1)} fusion(bf16[640,2560]{1,0:T(8,128)(2,1)} %collective-permute-done.14, s32[]{:T(128)S(6)} %select_n.18), kind=kLoop, calls=%fused_computation.14 | loop fusion | bytes 3276804 | tf_op jit(solution)/shard_map/dynamic_slice | solution.py:234
  65.1 1.6 %collective-permute-done.13.heads = bf16[256,640]{1,0:T(8,128)(2,1)S(1)} collective-permute-done((bf16[256,640]{1,0:T(8,128)(2,1)}, bf16[256,640]{1,0:T(8,128)(2,1)S(1)}, u32[]{:S(2)}, u32[]{:S(2)}) %collective-permute-start.13) | collective-permute-done | bytes 327712 | tf_op jit(solution)/shard_map/ppermute | solution.py:224
  66.6 0.7 project.5.refs_0_
  67.3 1.5 %constant_dynamic-slice_fusion.weight = bf16[640,1280]{1,0:T(8,128)(2,1)S(1)} fusion(bf16[640,2560]{1,0:T(8,128)(2,1)} %collective-permute-done.15, s32[]{:T(128)S(6)} %select_n.18), kind=kLoop, calls=%fused_computation.13 | loop fusion | bytes 3276804 | tf_op jit(solution)/shard_map/dynamic_slice | solution.py:234
  68.9 0.7 collective-permute-done.12.heads
  69.6 1.4 %collective-permute-start.16 = (bf16[256,640]{1,0:T(8,128)(2,1)S(1)}, bf16[256,640]{1,0:T(8,128)(2,1)S(1)}, u32[]{:S(2)}, u32[]{:S(2)}) collective-permute-start(bf16[256,640]{1,0:T(8,128)(2,1)S(1)} %collective-permute-done.12.heads), channel_id=1, source_target_pairs={{0,1},{1,0},{2,3},{3,2},{4,5},{5,4},{6,7},{7,6},{8,9},{9,8},{10,11... | collective-permute-start | bytes 983048 | tf_op jit(solution)/shard_map/ppermute | solution.py:224
  72.2 1.5 %project.7 = bf16[256,1280]{1,0:T(8,128)(2,1)} custom-call(bf16[256,640]{1,0:T(8,128)(2,1)S(1)} %collective-permute-done.16.heads, bf16[640,1280]{1,0:T(8,128)(2,1)S(1)} %constant_dynamic-slice_fusion.weight, f32[256,1280]{1,0:T(8,128)S(1)} %project.6.refs_0_), custom_call_target="tpu_custom_call" | custom-call | flops 419430400 | bytes 1638400 | tf_op jit(solution)/shard_map/project/pallas_call | solution.py:248
  (35 shorter events, 3.8 us)
Async XLA Ops:
  0.0 23.4 %collective-permute-start.3 = (bf16[640,5120]{1,0:T(8,128)(2,1)}, bf16[640,5120]{1,0:T(8,128)(2,1)}, u32[]{:S(2)}, u32[]{:S(2)}) collective-permute-start(bf16[640,5120]{1,0:T(8,128)(2,1)} %param.11), channel_id=1, source_target_pairs={{0,1},{1,0},{2,3},{3,2},{4,5},{5,4},{6,7},{7,6},{8,9},{9,8},{10,11... | collective-permute-start | bytes 19660808 | tf_op jit(solution)/shard_map/ppermute | solution.py:224
  4.3 18.4 %collective-permute-start = (bf16[512,128]{1,0:T(8,128)(2,1)S(1)}, bf16[512,128]{1,0:T(8,128)(2,1)S(1)}, u32[]{:S(2)}, u32[]{:S(2)}) collective-permute-start(bf16[512,128]{1,0:T(8,128)(2,1)S(1)} %pad_select_fusion), channel_id=1, source_target_pairs={{72,0},{76,4},{80,8},{84,12},{88,16},{92,20},{64,24},{68,28},{104,... | collective-permute-start | bytes 393224 | tf_op jit(solution)/shard_map/ppermute | solution.py:39
  11.3 11.8 %collective-permute-start.1 = (bf16[512,128]{1,0:T(8,128)(2,1)S(1)}, bf16[512,128]{1,0:T(8,128)(2,1)S(1)}, u32[]{:S(2)}, u32[]{:S(2)}) collective-permute-start(bf16[512,128]{1,0:T(8,128)(2,1)S(1)} %pad_select_fusion), channel_id=1, source_target_pairs={{88,0},{92,4},{64,8},{68,12},{72,16},{76,20},{80,24},{84,28},{120,... | collective-permute-start | bytes 393224 | tf_op jit(solution)/shard_map/ppermute | solution.py:39
  11.3 12.1 %collective-permute-start.2 = (bf16[512,128]{1,0:T(8,128)(2,1)S(1)}, bf16[512,128]{1,0:T(8,128)(2,1)S(1)}, u32[]{:S(2)}, u32[]{:S(2)}) collective-permute-start(bf16[512,128]{1,0:T(8,128)(2,1)S(1)} %pad_select_fusion), channel_id=1, source_target_pairs={{16,0},{20,4},{24,8},{28,12},{0,16},{4,20},{8,24},{12,28},{48,32},... | collective-permute-start | bytes 393224 | tf_op jit(solution)/shard_map/ppermute | solution.py:39
  18.2 39.1 %collective-permute-start.14 = (bf16[640,2560]{1,0:T(8,128)(2,1)}, bf16[640,2560]{1,0:T(8,128)(2,1)}, u32[]{:S(2)}, u32[]{:S(2)}) collective-permute-start(bf16[640,2560]{1,0:T(8,128)(2,1)} %constant_dynamic-slice_fusion.2), channel_id=1, source_target_pairs={{2,0},{131,1},{128,2},{1,3},{130,128},{3,129},{0,130},{129,131},{6... | collective-permute-start | bytes 9830408 | tf_op jit(solution)/shard_map/ppermute | solution.py:230
  23.4 9.3 %collective-permute-start.6 = (bf16[2048,128]{1,0:T(8,128)(2,1)S(1)}, bf16[2048,128]{1,0:T(8,128)(2,1)S(1)}, u32[]{:S(2)}, u32[]{:S(2)}) collective-permute-start(bf16[2048,128]{1,0:T(8,128)(2,1)S(1)} %pad_maximum_fusion.1), channel_id=1, source_target_pairs={{4,0},{8,4},{12,8},{16,12},{20,16},{24,20},{28,24},{0,28},{36,32},... | collective-permute-start | bytes 1572872 | tf_op jit(solution)/shard_map/ppermute | solution.py:39
  24.1 15.7 %collective-permute-start.8 = (bf16[2048,128]{1,0:T(8,128)(2,1)S(1)}, bf16[2048,128]{1,0:T(8,128)(2,1)S(1)}, u32[]{:S(2)}, u32[]{:S(2)}) collective-permute-start(bf16[2048,128]{1,0:T(8,128)(2,1)S(1)} %pad_maximum_fusion.1), channel_id=1, source_target_pairs={{28,0},{0,4},{4,8},{8,12},{12,16},{16,20},{20,24},{24,28},{60,32},... | collective-permute-start | bytes 1572872 | tf_op jit(solution)/shard_map/ppermute | solution.py:39
  25.3 11.7 %collective-permute-start.4 = (bf16[2048,128]{1,0:T(8,128)(2,1)S(1)}, bf16[2048,128]{1,0:T(8,128)(2,1)S(1)}, u32[]{:S(2)}, u32[]{:S(2)}) collective-permute-start(bf16[2048,128]{1,0:T(8,128)(2,1)S(1)} %pad_maximum_fusion.1), channel_id=1, source_target_pairs={{32,0},{36,4},{40,8},{44,12},{48,16},{52,20},{56,24},{60,28},{64,3... | collective-permute-start | bytes 1572872 | tf_op jit(solution)/shard_map/ppermute | solution.py:39
  27.4 9.6 %collective-permute-start.5 = (bf16[2048,128]{1,0:T(8,128)(2,1)S(1)}, bf16[2048,128]{1,0:T(8,128)(2,1)S(1)}, u32[]{:S(2)}, u32[]{:S(2)}) collective-permute-start(bf16[2048,128]{1,0:T(8,128)(2,1)S(1)} %pad_maximum_fusion.1), channel_id=1, source_target_pairs={{96,0},{100,4},{104,8},{108,12},{112,16},{116,20},{120,24},{124,28... | collective-permute-start | bytes 1572872 | tf_op jit(solution)/shard_map/ppermute | solution.py:39
  40.0 5.1 %copy-start.2 = (s32[608]{0:T(1024)S(1)}, s32[608]{0:T(1024)}, u32[]{:S(2)}) copy-start(s32[608]{0:T(1024)} %plan.1) | copy-start | bytes 7300
  40.0 5.1 %copy-start.3 = (bf16[256,640]{1,0:T(8,128)(2,1)S(1)}, bf16[256,640]{1,0:T(8,128)(2,1)}, u32[]{:S(2)}) copy-start(bf16[256,640]{1,0:T(8,128)(2,1)} %q_ref.3) | copy-start | bytes 983044
  40.0 10.1 %collective-permute-start.10 = (bf16[1536,128]{1,0:T(8,128)(2,1)S(1)}, bf16[1536,128]{1,0:T(8,128)(2,1)S(1)}, u32[]{:S(2)}, u32[]{:S(2)}) collective-permute-start(bf16[1536,128]{1,0:T(8,128)(2,1)S(1)} %get-tuple-element.44), channel_id=1, source_target_pairs={{32,0},{36,4},{40,8},{44,12},{48,16},{52,20},{56,24},{60,28},{64,3... | collective-permute-start | bytes 1179656 | tf_op jit(solution)/shard_map/ppermute | solution.py:39
  40.4 9.8 %collective-permute-start.11 = (bf16[1536,128]{1,0:T(8,128)(2,1)S(1)}, bf16[1536,128]{1,0:T(8,128)(2,1)S(1)}, u32[]{:S(2)}, u32[]{:S(2)}) collective-permute-start(bf16[1536,128]{1,0:T(8,128)(2,1)S(1)} %get-tuple-element.42), channel_id=1, source_target_pairs={{96,0},{100,4},{104,8},{108,12},{112,16},{116,20},{120,24},{124,28... | collective-permute-start | bytes 1179656 | tf_op jit(solution)/shard_map/ppermute | solution.py:39
  41.6 8.8 %collective-permute-start.7 = (bf16[1536,128]{1,0:T(8,128)(2,1)S(1)}, bf16[1536,128]{1,0:T(8,128)(2,1)S(1)}, u32[]{:S(2)}, u32[]{:S(2)}) collective-permute-start(bf16[1536,128]{1,0:T(8,128)(2,1)S(1)} %get-tuple-element.41), channel_id=1, source_target_pairs={{4,0},{8,4},{12,8},{16,12},{20,16},{24,20},{28,24},{0,28},{36,32},... | collective-permute-start | bytes 1179656 | tf_op jit(solution)/shard_map/ppermute | solution.py:39
  44.0 8.1 %collective-permute-start.9 = (bf16[1536,128]{1,0:T(8,128)(2,1)S(1)}, bf16[1536,128]{1,0:T(8,128)(2,1)S(1)}, u32[]{:S(2)}, u32[]{:S(2)}) collective-permute-start(bf16[1536,128]{1,0:T(8,128)(2,1)S(1)} %get-tuple-element.43), channel_id=1, source_target_pairs={{28,0},{0,4},{4,8},{8,12},{12,16},{16,20},{20,24},{24,28},{60,32},... | collective-permute-start | bytes 1179656 | tf_op jit(solution)/shard_map/ppermute | solution.py:39
  54.8 0.7 copy-start
  57.2 10.1 %collective-permute-start.15 = (bf16[640,2560]{1,0:T(8,128)(2,1)}, bf16[640,2560]{1,0:T(8,128)(2,1)}, u32[]{:S(2)}, u32[]{:S(2)}) collective-permute-start(bf16[640,2560]{1,0:T(8,128)(2,1)} %collective-permute-done.14), channel_id=1, source_target_pairs={{0,1},{1,0},{2,3},{3,2},{4,5},{5,4},{6,7},{7,6},{8,9},{9,8},{10,11... | collective-permute-start | bytes 9830408 | tf_op jit(solution)/shard_map/ppermute | solution.py:224
  60.6 6.0 %collective-permute-start.13 = (bf16[256,640]{1,0:T(8,128)(2,1)}, bf16[256,640]{1,0:T(8,128)(2,1)S(1)}, u32[]{:S(2)}, u32[]{:S(2)}) collective-permute-start(bf16[256,640]{1,0:T(8,128)(2,1)} %copy-done), channel_id=1, source_target_pairs={{0,1},{1,0},{2,3},{3,2},{4,5},{5,4},{6,7},{7,6},{8,9},{9,8},{10,11... | collective-permute-start | bytes 983048 | tf_op jit(solution)/shard_map/ppermute | solution.py:224
  60.6 9.0 %collective-permute-start.12 = (bf16[256,640]{1,0:T(8,128)(2,1)}, bf16[256,640]{1,0:T(8,128)(2,1)S(1)}, u32[]{:S(2)}, u32[]{:S(2)}) collective-permute-start(bf16[256,640]{1,0:T(8,128)(2,1)} %copy-done), channel_id=1, source_target_pairs={{0,2},{2,0},{1,3},{3,1},{4,6},{6,4},{5,7},{7,5},{8,10},{10,8},{9,1... | collective-permute-start | bytes 983048 | tf_op jit(solution)/shard_map/ppermute | solution.py:224
  61.8 1.0 %copy-start.1 = (bf16[256,640]{1,0:T(8,128)(2,1)S(1)}, bf16[256,640]{1,0:T(8,128)(2,1)}, u32[]{:S(2)}) copy-start(bf16[256,640]{1,0:T(8,128)(2,1)} %copy-done) | copy-start | bytes 983044
  69.6 2.6 %collective-permute-start.16 = (bf16[256,640]{1,0:T(8,128)(2,1)S(1)}, bf16[256,640]{1,0:T(8,128)(2,1)S(1)}, u32[]{:S(2)}, u32[]{:S(2)}) collective-permute-start(bf16[256,640]{1,0:T(8,128)(2,1)S(1)} %collective-permute-done.12.heads), channel_id=1, source_target_pairs={{0,1},{1,0},{2,3},{3,2},{4,5},{5,4},{6,7},{7,6},{8,9},{9,8},{10,11... | collective-permute-start | bytes 983048 | tf_op jit(solution)/shard_map/ppermute | solution.py:224

commit v6 on v5

--- a/solution.py
+++ b/solution.py
@@ -280,12 +280,12 @@
     running = attention(0, plan, docs, queries, jnp.concatenate(near))
     heads = attention(1, plan, docs, queries, jnp.concatenate(last), running)
     beside, after = lax.optimization_barrier((beside, heads))
-    beside_1 = swapped(beside, "core")
+    beside_1 = swapped(columns_of(beside, 1 - core, width), "core")
     heads_beside = swapped(heads, "x")
     heads_1 = swapped(heads, "core")
     total = projected(heads, own_columns[0], jnp.float32)
     total = projected(heads_1, own_columns[1], jnp.float32, [total])
-    beside_columns = [columns_of(w, core, width) for w in (beside, beside_1)]
+    beside_columns = [columns_of(beside, core, width), beside_1]
     heads_beside, total, *beside_columns = lax.optimization_barrier((heads_beside, total, *beside_columns))
     heads_beside_1 = swapped(heads_beside, "core")
     total = projected(heads_beside, beside_columns[0], jnp.float32, [total])

time: 74.7 us -> 74.9 us (level)
  waiting for transfers between devices: 17.4 us -> 25 us
  local copies, waits for them, and re-layouts: 11.3 us -> 6.63 us
  Pallas kernels: 13.8 us -> 10.2 us
  other arithmetic: 1.29 us -> 2.26 us
    ppermute x5, waiting for transfers between devices: 2.82 us -> 6.87 us  [swapped(): return lax.ppermute(x, axis, [(0, 1), (1, 0)])]
    pallas_call x2, Pallas kernels: 7.56 us -> 3.99 us  [attention(): pl.pallas_call(functools.partial(attention_kernel, stage=stage, docs=docs...]
    ppermute x11, waiting for transfers between devices: 12.8 us -> 15.9 us  [moved(): return lax.ppermute(x, ('y', 'z'), route)]
    dynamic_slice x4 -> x3, local copies, waits for them, and re-layouts: 9.15 us -> 6.24 us  [columns_of(): return lax.dynamic_slice_in_dim(weight, column * width, width, 1)]
    unnamed x12 -> x8, local copies, waits for them, and re-layouts: 1.98 us -> 0.26 us
    concatenate x1, other arithmetic: 0.03 us -> 1 us  [first_round(): return jnp.concatenate([kv] + [moved(kv, *c) for c in CENTRES[1:]])]
  transfers between devices with their start and end apart: 17 -> 17, of which waited for: 11 -> 13; matrix products, arithmetic and copies ran while one was open for 15% -> 12% of each run, Pallas kernels for 17% -> 12%
where the time goes in v6:
time: 74.9 us; the launch traced here: 73.5 us
  starting transfers between devices  28.7 us (38%)
  waiting for transfers between devices  25 us (33%)
  Pallas kernels  10.2 us (14%)
  local copies, waits for them, and re-layouts  6.63 us (9%)
  other arithmetic  2.26 us (3%)
  between operations  0.85 us (1%)
    ppermute x11, starting transfers between devices, moved(): return lax.ppermute(x, ('y', 'z'), route)  18.8 us
    ppermute x11, waiting for transfers between devices, moved(): return lax.ppermute(x, ('y', 'z'), route)  15.9 us
    ppermute x5, starting transfers between devices, swapped(): return lax.ppermute(x, axis, [(0, 1), (1, 0)])  8.69 us
    ppermute x5, waiting for transfers between devices, swapped(): return lax.ppermute(x, axis, [(0, 1), (1, 0)])  6.87 us
    dynamic_slice x3, local copies, waits for them, and re-layouts, columns_of(): return lax.dynamic_slice_in_dim(weight, column * width, width, 1)  6.24 us
    pallas_call x2, Pallas kernels, attention(): pl.pallas_call(functools.partial(attention_kernel, stage=stage, docs=docs...  3.99 us
    pallas_call x4, Pallas kernels, projected(): pl.pallas_call(project_kernel, out_shape=jax.ShapeDtypeStruct((rows, widt...  3.55 us
    pallas_call x1, Pallas kernels, planned(): pl.pallas_call(plan_kernel, out_shape=jax.ShapeDtypeStruct((listed(4, 0,...  2.62 us
  transfers between devices with their start and end apart: 17, of which 13 were waited for; matrix products, arithmetic and copies ran while one was open for 12% of the time, Pallas kernels for 12%

profile of v6, /device:TPU:1, one launch (start us, length us, event | category | flops | bytes accessed | tf_op | source)
XLA Modules:
  0.0 73.5 jit_solution(16633867262434239657)
XLA Ops:
  0.0 3.2 %collective-permute-start.3 = (bf16[640,5120]{1,0:T(8,128)(2,1)}, bf16[640,5120]{1,0:T(8,128)(2,1)}, u32[]{:S(2)}, u32[]{:S(2)}) collective-permute-start(bf16[640,5120]{1,0:T(8,128)(2,1)} %param.11), channel_id=1, source_target_pairs={{0,1},{1,0},{2,3},{3,2},{4,5},{5,4},{6,7},{7,6},{8,9},{9,8},{10,11... | collective-permute-start | bytes 19660808 | tf_op jit(solution)/shard_map/ppermute | solution.py:224
  3.2 1.0 %pad_select_fusion = bf16[512,128]{1,0:T(8,128)(2,1)S(1)} fusion(bf16[256,128]{1,0:T(8,128)(2,1)} %param.10, bf16[256,128]{1,0:T(8,128)(2,1)} %param.9, pred[512]{0:T(512)(128)(4,1)S(1)} %iota_compare_fusion), kind=kLoop, calls=%fused_computation.6 | loop fusion | flops 65536 | bytes 262656 | tf_op jit(solution)/shard_map/jit(_where)/select_n | solution.py:265
  4.3 7.0 %collective-permute-start = (bf16[512,128]{1,0:T(8,128)(2,1)S(1)}, bf16[512,128]{1,0:T(8,128)(2,1)S(1)}, u32[]{:S(2)}, u32[]{:S(2)}) collective-permute-start(bf16[512,128]{1,0:T(8,128)(2,1)S(1)} %pad_select_fusion), channel_id=1, source_target_pairs={{72,0},{76,4},{80,8},{84,12},{88,16},{92,20},{64,24},{68,28},{104,... | collective-permute-start | bytes 393224 | tf_op jit(solution)/shard_map/ppermute | solution.py:39
  11.3 3.0 %collective-permute-start.2 = (bf16[512,128]{1,0:T(8,128)(2,1)S(1)}, bf16[512,128]{1,0:T(8,128)(2,1)}, u32[]{:S(2)}, u32[]{:S(2)}) collective-permute-start(bf16[512,128]{1,0:T(8,128)(2,1)S(1)} %pad_select_fusion), channel_id=1, source_target_pairs={{16,0},{20,4},{24,8},{28,12},{0,16},{4,20},{8,24},{12,28},{48,32},... | collective-permute-start | bytes 393224 | tf_op jit(solution)/shard_map/ppermute | solution.py:39
  14.3 3.9 %constant_dynamic-slice_fusion.2 = bf16[640,2560]{1,0:T(8,128)(2,1)} fusion(bf16[640,5120]{1,0:T(8,128)(2,1)} %param.11, s32[]{:T(128)S(6)} %select_n.19), kind=kLoop, calls=%fused_computation.15 | loop fusion | bytes 6553604 | tf_op jit(solution)/shard_map/dynamic_slice | solution.py:234
  18.2 1.2 %collective-permute-start.14 = (bf16[640,2560]{1,0:T(8,128)(2,1)}, bf16[640,2560]{1,0:T(8,128)(2,1)S(1)}, u32[]{:S(2)}, u32[]{:S(2)}) collective-permute-start(bf16[640,2560]{1,0:T(8,128)(2,1)} %constant_dynamic-slice_fusion.2), channel_id=1, source_target_pairs={{2,0},{131,1},{128,2},{1,3},{130,128},{3,129},{0,130},{129,131},{6... | collective-permute-start | bytes 9830408 | tf_op jit(solution)/shard_map/ppermute | solution.py:230
  20.0 2.6 %plan.1 = s32[608]{0:T(1024)} custom-call(s32[64]{0:T(128)} %order.1, s32[8]{0:T(128)} %lengths.1, s32[64,64]{1,0:T(8,128)} %reveal.1, s32[1]{0:T(128)S(6)} %copy.13.step), custom_call_target="tpu_custom_call" | custom-call | tf_op jit(solution)/shard_map/plan/pallas_call | solution.py:195
  23.5 1.0 %pad_maximum_fusion.1 = bf16[2048,128]{1,0:T(8,128)(2,1)S(1)} fusion(bf16[512,128]{1,0:T(8,128)(2,1)} %collective-permute-done.2, bf16[512,128]{1,0:T(8,128)(2,1)} %collective-permute-done.1, bf16[512,128]{1,0:T(8,128)(2,1)S(1)} %collective-permute-done, bf16[512,128]{1,0:T(8,128)(2,1)S(1)} %pad_select_fusion), kind=kLoop, calls=%fused_computation.1 | loop fusion | flops 2097152 | bytes 1048576 | tf_op jit(solution)/shard_map/concatenate | solution.py:43
  24.5 0.7 collective-permute-start.6
  25.2 1.2 %collective-permute-start.8 = (bf16[2048,128]{1,0:T(8,128)(2,1)S(1)}, bf16[2048,128]{1,0:T(8,128)(2,1)S(1)}, u32[]{:S(2)}, u32[]{:S(2)}) collective-permute-start(bf16[2048,128]{1,0:T(8,128)(2,1)S(1)} %pad_maximum_fusion.1), channel_id=1, source_target_pairs={{28,0},{0,4},{4,8},{8,12},{12,16},{16,20},{20,24},{24,28},{60,32},... | collective-permute-start | bytes 1572872 | tf_op jit(solution)/shard_map/ppermute | solution.py:39
  26.4 2.1 %collective-permute-start.4 = (bf16[2048,128]{1,0:T(8,128)(2,1)S(1)}, bf16[2048,128]{1,0:T(8,128)(2,1)S(1)}, u32[]{:S(2)}, u32[]{:S(2)}) collective-permute-start(bf16[2048,128]{1,0:T(8,128)(2,1)S(1)} %pad_maximum_fusion.1), channel_id=1, source_target_pairs={{32,0},{36,4},{40,8},{44,12},{48,16},{52,20},{56,24},{60,28},{64,3... | collective-permute-start | bytes 1572872 | tf_op jit(solution)/shard_map/ppermute | solution.py:39
  28.5 2.1 %constant_dynamic-slice_fusion.3 = (bf16[640,1280]{1,0:T(8,128)(2,1)S(1)}, bf16[640,1280]{1,0:T(8,128)(2,1)S(1)}) fusion(bf16[640,5120]{1,0:T(8,128)(2,1)} %collective-permute-done.3, s32[]{:T(128)S(6)} %select_n.18, bf16[640,5120]{1,0:T(8,128)(2,1)} %param.11), kind=kLoop, calls=%fused_computation.16 | loop fusion | bytes 6553604 | tf_op jit(solution)/shard_map/dynamic_slice | solution.py:234
  30.7 3.1 %collective-permute-done.6 = bf16[2048,128]{1,0:T(8,128)(2,1)S(1)} collective-permute-done((bf16[2048,128]{1,0:T(8,128)(2,1)S(1)}, bf16[2048,128]{1,0:T(8,128)(2,1)S(1)}, u32[]{:S(2)}, u32[]{:S(2)}) %collective-permute-start.6) | collective-permute-done | bytes 524320 | tf_op jit(solution)/shard_map/ppermute | solution.py:39
  33.8 4.3 %collective-permute-done.5 = bf16[2048,128]{1,0:T(8,128)(2,1)S(1)} collective-permute-done((bf16[2048,128]{1,0:T(8,128)(2,1)S(1)}, bf16[2048,128]{1,0:T(8,128)(2,1)S(1)}, u32[]{:S(2)}, u32[]{:S(2)}) %collective-permute-start.5) | collective-permute-done | bytes 524320 | tf_op jit(solution)/shard_map/ppermute | solution.py:39
  38.1 2.7 %collective-permute-done.8 = bf16[2048,128]{1,0:T(8,128)(2,1)S(1)} collective-permute-done((bf16[2048,128]{1,0:T(8,128)(2,1)S(1)}, bf16[2048,128]{1,0:T(8,128)(2,1)S(1)}, u32[]{:S(2)}, u32[]{:S(2)}) %collective-permute-start.8) | collective-permute-done | bytes 524320 | tf_op jit(solution)/shard_map/ppermute | solution.py:39
  41.6 1.0 %collective-permute-start.11 = (bf16[1536,128]{1,0:T(8,128)(2,1)S(1)}, bf16[1536,128]{1,0:T(8,128)(2,1)S(1)}, u32[]{:S(2)}, u32[]{:S(2)}) collective-permute-start(bf16[1536,128]{1,0:T(8,128)(2,1)S(1)} %get-tuple-element.44), channel_id=1, source_target_pairs={{96,0},{100,4},{104,8},{108,12},{112,16},{116,20},{120,24},{124,28... | collective-permute-start | bytes 1179656 | tf_op jit(solution)/shard_map/ppermute | solution.py:39
  42.6 2.6 %collective-permute-start.7 = (bf16[1536,128]{1,0:T(8,128)(2,1)S(1)}, bf16[1536,128]{1,0:T(8,128)(2,1)S(1)}, u32[]{:S(2)}, u32[]{:S(2)}) collective-permute-start(bf16[1536,128]{1,0:T(8,128)(2,1)S(1)} %get-tuple-element.43), channel_id=1, source_target_pairs={{4,0},{8,4},{12,8},{16,12},{20,16},{24,20},{28,24},{0,28},{36,32},... | collective-permute-start | bytes 1179656 | tf_op jit(solution)/shard_map/ppermute | solution.py:39
  46.2 2.2 %attention_0.1 = (f32[2,1,640]{2,1,0:T(1,128)S(1)}, f32[2,8,640]{2,1,0:T(8,128)S(1)}, f32[2,128,640]{2,1,0:T(8,128)S(1)}) custom-call(s32[608]{0:T(1024)S(1)} %copy-done, bf16[256,640]{1,0:T(8,128)(2,1)S(1)} %copy-done.1, bf16[10240,128]{1,0:T(8,128)(2,1)S(1)} %constant_dynamic-update-slice_fusion.kv), custom_call_target="tpu_custom_call" | custom-call | flops 1000000000 | bytes 10000000 | tf_op jit(solution)/shard_map/attention_0/pallas_call | solution.py:207
  48.6 1.6 %collective-permute-done.11 = bf16[1536,128]{1,0:T(8,128)(2,1)S(1)} collective-permute-done((bf16[1536,128]{1,0:T(8,128)(2,1)S(1)}, bf16[1536,128]{1,0:T(8,128)(2,1)S(1)}, u32[]{:S(2)}, u32[]{:S(2)}) %collective-permute-start.11) | collective-permute-done | bytes 393248 | tf_op jit(solution)/shard_map/ppermute | solution.py:39
  50.2 1.1 %collective-permute-done.7 = bf16[1536,128]{1,0:T(8,128)(2,1)S(1)} collective-permute-done((bf16[1536,128]{1,0:T(8,128)(2,1)S(1)}, bf16[1536,128]{1,0:T(8,128)(2,1)S(1)}, u32[]{:S(2)}, u32[]{:S(2)}) %collective-permute-start.7) | collective-permute-done | bytes 393248 | tf_op jit(solution)/shard_map/ppermute | solution.py:39
  51.3 2.1 %collective-permute-done.9 = bf16[1536,128]{1,0:T(8,128)(2,1)S(1)} collective-permute-done((bf16[1536,128]{1,0:T(8,128)(2,1)S(1)}, bf16[1536,128]{1,0:T(8,128)(2,1)S(1)}, u32[]{:S(2)}, u32[]{:S(2)}) %collective-permute-start.9) | collective-permute-done | bytes 393248 | tf_op jit(solution)/shard_map/ppermute | solution.py:39
  53.5 1.7 %attention_1.1.heads = bf16[256,640]{1,0:T(8,128)(2,1)S(1)} custom-call(s32[608]{0:T(1024)S(1)} %copy-done, bf16[256,640]{1,0:T(8,128)(2,1)S(1)} %copy-done.1, bf16[6144,128]{1,0:T(8,128)(2,1)S(1)} %pad_maximum_fusion.kv, f32[2,1,640]{2,1,0:T(1,128)S(1)} %get-tuple-element.25.refs_0_, f32[2,8,640]{2,1,0:T(8,128)S(1)} %get-tuple-element.26.refs_1_, ...), custom_call_target="tpu_custom_call" | custom-call | flops 1000000000 | bytes 10000000 | tf_op jit(solution)/shard_map/attention_1/pallas_call | solution.py:207
  55.2 2.2 %collective-permute-done.14 = bf16[640,2560]{1,0:T(8,128)(2,1)S(1)} collective-permute-done((bf16[640,2560]{1,0:T(8,128)(2,1)}, bf16[640,2560]{1,0:T(8,128)(2,1)S(1)}, u32[]{:S(2)}, u32[]{:S(2)}) %collective-permute-start.14) | collective-permute-done | bytes 3276832 | tf_op jit(solution)/shard_map/ppermute | solution.py:230
  57.6 2.9 %collective-permute-start.15 = (bf16[640,1280]{1,0:T(8,128)(2,1)S(1)}, bf16[640,1280]{1,0:T(8,128)(2,1)S(1)}, u32[]{:S(2)}, u32[]{:S(2)}) collective-permute-start(bf16[640,1280]{1,0:T(8,128)(2,1)S(1)} %get-tuple-element.35), channel_id=1, source_target_pairs={{0,1},{1,0},{2,3},{3,2},{4,5},{5,4},{6,7},{7,6},{8,9},{9,8},{10,11... | collective-permute-start | bytes 4915208 | tf_op jit(solution)/shard_map/ppermute | solution.py:224
  60.6 1.2 %collective-permute-start.12 = (bf16[256,640]{1,0:T(8,128)(2,1)S(1)}, bf16[256,640]{1,0:T(8,128)(2,1)S(1)}, u32[]{:S(2)}, u32[]{:S(2)}) collective-permute-start(bf16[256,640]{1,0:T(8,128)(2,1)S(1)} %attention_1.1.heads), channel_id=1, source_target_pairs={{0,2},{2,0},{1,3},{3,1},{4,6},{6,4},{5,7},{7,5},{8,10},{10,8},{9,1... | collective-permute-start | bytes 983048 | tf_op jit(solution)/shard_map/ppermute | solution.py:224
  61.8 0.7 project.4.refs_0_
  62.5 1.6 %collective-permute-done.13.heads = bf16[256,640]{1,0:T(8,128)(2,1)S(1)} collective-permute-done((bf16[256,640]{1,0:T(8,128)(2,1)S(1)}, bf16[256,640]{1,0:T(8,128)(2,1)S(1)}, u32[]{:S(2)}, u32[]{:S(2)}) %collective-permute-start.13) | collective-permute-done | bytes 327712 | tf_op jit(solution)/shard_map/ppermute | solution.py:224
  64.1 0.7 project.5.refs_0_
  64.8 4.7 %collective-permute-done.12.heads = bf16[256,640]{1,0:T(8,128)(2,1)S(1)} collective-permute-done((bf16[256,640]{1,0:T(8,128)(2,1)S(1)}, bf16[256,640]{1,0:T(8,128)(2,1)S(1)}, u32[]{:S(2)}, u32[]{:S(2)}) %collective-permute-start.12) | collective-permute-done | bytes 327712 | tf_op jit(solution)/shard_map/ppermute | solution.py:224
  69.5 1.2 %collective-permute-start.16 = (bf16[256,640]{1,0:T(8,128)(2,1)S(1)}, bf16[256,640]{1,0:T(8,128)(2,1)S(1)}, u32[]{:S(2)}, u32[]{:S(2)}) collective-permute-start(bf16[256,640]{1,0:T(8,128)(2,1)S(1)} %collective-permute-done.12.heads), channel_id=1, source_target_pairs={{0,1},{1,0},{2,3},{3,2},{4,5},{5,4},{6,7},{7,6},{8,9},{9,8},{10,11... | collective-permute-start | bytes 983048 | tf_op jit(solution)/shard_map/ppermute | solution.py:224
  70.7 0.7 project.6.refs_0_
  72.0 1.5 %project.7 = bf16[256,1280]{1,0:T(8,128)(2,1)} custom-call(bf16[256,640]{1,0:T(8,128)(2,1)S(1)} %collective-permute-done.16.heads, bf16[640,1280]{1,0:T(8,128)(2,1)S(1)} %collective-permute-done.15.weight, f32[256,1280]{1,0:T(8,128)S(1)} %project.6.refs_0_), custom_call_target="tpu_custom_call" | custom-call | flops 419430400 | bytes 1638400 | tf_op jit(solution)/shard_map/project/pallas_call | solution.py:248
  (30 shorter events, 3.6 us)
Async XLA Ops:
  0.0 24.5 %collective-permute-start.3 = (bf16[640,5120]{1,0:T(8,128)(2,1)}, bf16[640,5120]{1,0:T(8,128)(2,1)}, u32[]{:S(2)}, u32[]{:S(2)}) collective-permute-start(bf16[640,5120]{1,0:T(8,128)(2,1)} %param.11), channel_id=1, source_target_pairs={{0,1},{1,0},{2,3},{3,2},{4,5},{5,4},{6,7},{7,6},{8,9},{9,8},{10,11... | collective-permute-start | bytes 19660808 | tf_op jit(solution)/shard_map/ppermute | solution.py:224
  4.3 18.4 %collective-permute-start = (bf16[512,128]{1,0:T(8,128)(2,1)S(1)}, bf16[512,128]{1,0:T(8,128)(2,1)S(1)}, u32[]{:S(2)}, u32[]{:S(2)}) collective-permute-start(bf16[512,128]{1,0:T(8,128)(2,1)S(1)} %pad_select_fusion), channel_id=1, source_target_pairs={{72,0},{76,4},{80,8},{84,12},{88,16},{92,20},{64,24},{68,28},{104,... | collective-permute-start | bytes 393224 | tf_op jit(solution)/shard_map/ppermute | solution.py:39
  11.3 11.9 %collective-permute-start.1 = (bf16[512,128]{1,0:T(8,128)(2,1)S(1)}, bf16[512,128]{1,0:T(8,128)(2,1)}, u32[]{:S(2)}, u32[]{:S(2)}) collective-permute-start(bf16[512,128]{1,0:T(8,128)(2,1)S(1)} %pad_select_fusion), channel_id=1, source_target_pairs={{88,0},{92,4},{64,8},{68,12},{72,16},{76,20},{80,24},{84,28},{120,... | collective-permute-start | bytes 393224 | tf_op jit(solution)/shard_map/ppermute | solution.py:39
  11.3 12.2 %collective-permute-start.2 = (bf16[512,128]{1,0:T(8,128)(2,1)S(1)}, bf16[512,128]{1,0:T(8,128)(2,1)}, u32[]{:S(2)}, u32[]{:S(2)}) collective-permute-start(bf16[512,128]{1,0:T(8,128)(2,1)S(1)} %pad_select_fusion), channel_id=1, source_target_pairs={{16,0},{20,4},{24,8},{28,12},{0,16},{4,20},{8,24},{12,28},{48,32},... | collective-permute-start | bytes 393224 | tf_op jit(solution)/shard_map/ppermute | solution.py:39
  18.2 39.2 %collective-permute-start.14 = (bf16[640,2560]{1,0:T(8,128)(2,1)}, bf16[640,2560]{1,0:T(8,128)(2,1)S(1)}, u32[]{:S(2)}, u32[]{:S(2)}) collective-permute-start(bf16[640,2560]{1,0:T(8,128)(2,1)} %constant_dynamic-slice_fusion.2), channel_id=1, source_target_pairs={{2,0},{131,1},{128,2},{1,3},{130,128},{3,129},{0,130},{129,131},{6... | collective-permute-start | bytes 9830408 | tf_op jit(solution)/shard_map/ppermute | solution.py:230
  24.5 9.3 %collective-permute-start.6 = (bf16[2048,128]{1,0:T(8,128)(2,1)S(1)}, bf16[2048,128]{1,0:T(8,128)(2,1)S(1)}, u32[]{:S(2)}, u32[]{:S(2)}) collective-permute-start(bf16[2048,128]{1,0:T(8,128)(2,1)S(1)} %pad_maximum_fusion.1), channel_id=1, source_target_pairs={{4,0},{8,4},{12,8},{16,12},{20,16},{24,20},{28,24},{0,28},{36,32},... | collective-permute-start | bytes 1572872 | tf_op jit(solution)/shard_map/ppermute | solution.py:39
  25.2 15.7 %collective-permute-start.8 = (bf16[2048,128]{1,0:T(8,128)(2,1)S(1)}, bf16[2048,128]{1,0:T(8,128)(2,1)S(1)}, u32[]{:S(2)}, u32[]{:S(2)}) collective-permute-start(bf16[2048,128]{1,0:T(8,128)(2,1)S(1)} %pad_maximum_fusion.1), channel_id=1, source_target_pairs={{28,0},{0,4},{4,8},{8,12},{12,16},{16,20},{20,24},{24,28},{60,32},... | collective-permute-start | bytes 1572872 | tf_op jit(solution)/shard_map/ppermute | solution.py:39
  26.4 11.7 %collective-permute-start.4 = (bf16[2048,128]{1,0:T(8,128)(2,1)S(1)}, bf16[2048,128]{1,0:T(8,128)(2,1)S(1)}, u32[]{:S(2)}, u32[]{:S(2)}) collective-permute-start(bf16[2048,128]{1,0:T(8,128)(2,1)S(1)} %pad_maximum_fusion.1), channel_id=1, source_target_pairs={{32,0},{36,4},{40,8},{44,12},{48,16},{52,20},{56,24},{60,28},{64,3... | collective-permute-start | bytes 1572872 | tf_op jit(solution)/shard_map/ppermute | solution.py:39
  28.5 9.6 %collective-permute-start.5 = (bf16[2048,128]{1,0:T(8,128)(2,1)S(1)}, bf16[2048,128]{1,0:T(8,128)(2,1)S(1)}, u32[]{:S(2)}, u32[]{:S(2)}) collective-permute-start(bf16[2048,128]{1,0:T(8,128)(2,1)S(1)} %pad_maximum_fusion.1), channel_id=1, source_target_pairs={{96,0},{100,4},{104,8},{108,12},{112,16},{116,20},{120,24},{124,28... | collective-permute-start | bytes 1572872 | tf_op jit(solution)/shard_map/ppermute | solution.py:39
  41.1 5.1 %copy-start = (s32[608]{0:T(1024)S(1)}, s32[608]{0:T(1024)}, u32[]{:S(2)}) copy-start(s32[608]{0:T(1024)} %plan.1) | copy-start | bytes 7300
  41.1 5.1 %copy-start.1 = (bf16[256,640]{1,0:T(8,128)(2,1)S(1)}, bf16[256,640]{1,0:T(8,128)(2,1)}, u32[]{:S(2)}) copy-start(bf16[256,640]{1,0:T(8,128)(2,1)} %q_ref.3) | copy-start | bytes 983044
  41.1 7.5 %collective-permute-start.10 = (bf16[1536,128]{1,0:T(8,128)(2,1)S(1)}, bf16[1536,128]{1,0:T(8,128)(2,1)S(1)}, u32[]{:S(2)}, u32[]{:S(2)}) collective-permute-start(bf16[1536,128]{1,0:T(8,128)(2,1)S(1)} %get-tuple-element.46), channel_id=1, source_target_pairs={{32,0},{36,4},{40,8},{44,12},{48,16},{52,20},{56,24},{60,28},{64,3... | collective-permute-start | bytes 1179656 | tf_op jit(solution)/shard_map/ppermute | solution.py:39
  41.6 8.6 %collective-permute-start.11 = (bf16[1536,128]{1,0:T(8,128)(2,1)S(1)}, bf16[1536,128]{1,0:T(8,128)(2,1)S(1)}, u32[]{:S(2)}, u32[]{:S(2)}) collective-permute-start(bf16[1536,128]{1,0:T(8,128)(2,1)S(1)} %get-tuple-element.44), channel_id=1, source_target_pairs={{96,0},{100,4},{104,8},{108,12},{112,16},{116,20},{120,24},{124,28... | collective-permute-start | bytes 1179656 | tf_op jit(solution)/shard_map/ppermute | solution.py:39
  42.6 8.7 %collective-permute-start.7 = (bf16[1536,128]{1,0:T(8,128)(2,1)S(1)}, bf16[1536,128]{1,0:T(8,128)(2,1)S(1)}, u32[]{:S(2)}, u32[]{:S(2)}) collective-permute-start(bf16[1536,128]{1,0:T(8,128)(2,1)S(1)} %get-tuple-element.43), channel_id=1, source_target_pairs={{4,0},{8,4},{12,8},{16,12},{20,16},{24,20},{28,24},{0,28},{36,32},... | collective-permute-start | bytes 1179656 | tf_op jit(solution)/shard_map/ppermute | solution.py:39
  45.3 8.1 %collective-permute-start.9 = (bf16[1536,128]{1,0:T(8,128)(2,1)S(1)}, bf16[1536,128]{1,0:T(8,128)(2,1)S(1)}, u32[]{:S(2)}, u32[]{:S(2)}) collective-permute-start(bf16[1536,128]{1,0:T(8,128)(2,1)S(1)} %get-tuple-element.45), channel_id=1, source_target_pairs={{28,0},{0,4},{4,8},{8,12},{12,16},{16,20},{20,24},{24,28},{60,32},... | collective-permute-start | bytes 1179656 | tf_op jit(solution)/shard_map/ppermute | solution.py:39
  57.6 11.9 %collective-permute-start.15 = (bf16[640,1280]{1,0:T(8,128)(2,1)S(1)}, bf16[640,1280]{1,0:T(8,128)(2,1)S(1)}, u32[]{:S(2)}, u32[]{:S(2)}) collective-permute-start(bf16[640,1280]{1,0:T(8,128)(2,1)S(1)} %get-tuple-element.35), channel_id=1, source_target_pairs={{0,1},{1,0},{2,3},{3,2},{4,5},{5,4},{6,7},{7,6},{8,9},{9,8},{10,11... | collective-permute-start | bytes 4915208 | tf_op jit(solution)/shard_map/ppermute | solution.py:224
  60.5 3.6 %collective-permute-start.13 = (bf16[256,640]{1,0:T(8,128)(2,1)S(1)}, bf16[256,640]{1,0:T(8,128)(2,1)S(1)}, u32[]{:S(2)}, u32[]{:S(2)}) collective-permute-start(bf16[256,640]{1,0:T(8,128)(2,1)S(1)} %attention_1.1.heads), channel_id=1, source_target_pairs={{0,1},{1,0},{2,3},{3,2},{4,5},{5,4},{6,7},{7,6},{8,9},{9,8},{10,11... | collective-permute-start | bytes 983048 | tf_op jit(solution)/shard_map/ppermute | solution.py:224
  60.6 8.9 %collective-permute-start.12 = (bf16[256,640]{1,0:T(8,128)(2,1)S(1)}, bf16[256,640]{1,0:T(8,128)(2,1)S(1)}, u32[]{:S(2)}, u32[]{:S(2)}) collective-permute-start(bf16[256,640]{1,0:T(8,128)(2,1)S(1)} %attention_1.1.heads), channel_id=1, source_target_pairs={{0,2},{2,0},{1,3},{3,1},{4,6},{6,4},{5,7},{7,5},{8,10},{10,8},{9,1... | collective-permute-start | bytes 983048 | tf_op jit(solution)/shard_map/ppermute | solution.py:224
  69.5 2.5 %collective-permute-start.16 = (bf16[256,640]{1,0:T(8,128)(2,1)S(1)}, bf16[256,640]{1,0:T(8,128)(2,1)S(1)}, u32[]{:S(2)}, u32[]{:S(2)}) collective-permute-start(bf16[256,640]{1,0:T(8,128)(2,1)S(1)} %collective-permute-done.12.heads), channel_id=1, source_target_pairs={{0,1},{1,0},{2,3},{3,2},{4,5},{5,4},{6,7},{7,6},{8,9},{9,8},{10,11... | collective-permute-start | bytes 983048 | tf_op jit(solution)/shard_map/ppermute | solution.py:224
